TPU v7x, 32 devices: a whole 2x2x4 slice. The times are simulated.
32 devices in a mesh: dp: 4 (over z), expert: 8 (over y, x, core).
Axes of the slice: x: 2, y: 2, z: 4, core: 2. Of those that a mesh axis runs over, the one named last changes fastest.
Arguments:
- tokens: bfloat16 [2, 2048, 2048], P(None, ('dp', 'expert')), may hold values from -6 to 6
- lengths: int32 [2, 32, 4], P(None, ('dp', 'expert')), may hold values from 1 to 32, 64 in all within a row
- expert_ids: int32 [2, 2048, 8], P(None, ('dp', 'expert')), may hold values from 0 to 15, all different within a row; in each aligned block of 64 rows (0 to 63, 64 to 127, ..., all dimensions but the last counted through in order) at most 40 rows name the same one
- gates: float32 [2, 2048, 8], P(None, ('dp', 'expert')), may hold values from 0.05 to 0.2
- attn_gain: bfloat16 [2048], P(('dp', 'expert')), may hold values from 0.5 to 1.5
- w_qkv: bfloat16 [2048, 6144], P(('dp', 'expert')), may hold values from -0.125 to 0.125
- q_gain: bfloat16 [2048], P(('dp', 'expert')), may hold values from 0.5 to 1.5
- k_gain: bfloat16 [2048], P(('dp', 'expert')), may hold values from 0.5 to 1.5
- w_out: bfloat16 [2048, 2048], P(('dp', 'expert')), may hold values from -0.5 to 0.5
- ffn_gain: bfloat16 [2048], P(('dp', 'expert')), may hold values from 0.5 to 1.5
- expert_in: bfloat16 [16, 2048, 2048], P('expert', 'dp'), may hold values from -0.125 to 0.125
- expert_out: bfloat16 [16, 1024, 2048], P('expert', 'dp'), may hold values from -0.75 to 0.75
- out_grad: bfloat16 [2, 2048, 2048], P(None, ('dp', 'expert')), may hold values from -6 to 6
Outputs:
- out: bfloat16 [2, 2048, 2048], P(None, ('dp', 'expert'))
- grad_tokens: float32 [2, 2048, 2048], P(None, ('dp', 'expert'))
- grad_gates: float32 [2, 2048, 8], P(None, ('dp', 'expert'))
- grad_attn_gain: float32 [2048], P(('dp', 'expert'))
- grad_w_qkv: float32 [2048, 6144], P(('dp', 'expert'))
- grad_q_gain: float32 [2048], P(('dp', 'expert'))
- grad_k_gain: float32 [2048], P(('dp', 'expert'))
- grad_w_out: float32 [2048, 2048], P(('dp', 'expert'))
- grad_ffn_gain: float32 [2048], P(('dp', 'expert'))
- grad_expert_in: float32 [16, 2048, 2048], P('expert', 'dp')
- grad_expert_out: float32 [16, 1024, 2048], P('expert', 'dp')
Inputs may be any that keep to these rules, and one draw needn't show every extreme that they name: `expert_ids`: each row names 8 different experts; in each aligned block of 64 rows (one pack) no expert is named by more than 40 rows, and in some block one expert is named by exactly 40 rows. Each pack's 4 lengths sum to 64, and the longest is exactly 32.
All inputs are finite; a program needn't handle non-finite values.
Results may differ from a plain program's by a relative error of at most 0.014.
Values may be sent and summed in bfloat16 or wider, within the bound.
A program may use at most 320 MiB of HBM per device.

v0:
```python
import jax
import jax.numpy as jnp
from jax import lax
from jax.sharding import PartitionSpec as P

HEAD = 128


epsilon = 1e-05
base_theta = 10000.0
masked_score = -1e30


def normalize(values):
    factor = lax.rsqrt(jnp.mean(values * values, axis=-1, keepdims=True) + epsilon)
    return (values * factor, factor)


def rms_back(upstream, normal, factor, gain):
    weighted = upstream * gain
    inner = jnp.mean(weighted * normal, axis=-1, keepdims=True)
    return (factor * (weighted - normal * inner), jnp.sum(upstream * normal, axis=0))


def rotate(field, position, turning):
    length = field.shape[0]
    heads = field.reshape(length, -1, HEAD)
    half = HEAD // 2
    ladder = jnp.arange(half, dtype=jnp.float32) * (2.0 / HEAD)
    frequency = jnp.exp(-jnp.log(base_theta) * ladder)
    angle = position.astype(jnp.float32)[:, None] * frequency[None, :]
    cosine = jnp.cos(angle)[:, None, :]
    sine = turning * jnp.sin(angle)[:, None, :]
    first = heads[..., :half]
    second = heads[..., half:]
    turned = jnp.concatenate(
        [first * cosine - second * sine, second * cosine + first * sine], axis=-1
    )
    return turned.reshape(length, -1)


def layout(doc_lengths, length):
    ends = jnp.cumsum(doc_lengths)
    starts = ends - doc_lengths
    places = jnp.arange(length, dtype=jnp.int32)
    document = jnp.sum((places[:, None] >= ends[None, :]).astype(jnp.int32), axis=1)
    member = (places[:, None] >= starts[None, :]) & (places[:, None] < ends[None, :])
    first_place = jnp.sum(jnp.where(member, starts[None, :], 0), axis=1)
    return (document, places - first_place)


def allowed_pairs(document):
    places = jnp.arange(document.shape[0], dtype=jnp.int32)
    return (document[:, None] == document[None, :]) & (places[:, None] >= places[None, :])


def attention_scores(query_rows, key_rows, document):
    raw = jnp.einsum(
        "qhd,khd->hqk", query_rows, key_rows, preferred_element_type=jnp.float32
    ) * HEAD ** (-0.5)
    return jnp.where(allowed_pairs(document)[None], raw, masked_score)


def route_local(expert_rows, experts, capacity):
    flat_ids = expert_rows.reshape(-1)
    count = flat_ids.shape[0]
    onehot = (flat_ids[:, None] == jnp.arange(experts, dtype=jnp.int32)[None, :]).astype(jnp.int32)
    before = jnp.cumsum(onehot, axis=0) - onehot
    ranks = jnp.sum(before * onehot, axis=1)
    slot_index = flat_ids * capacity + ranks
    filler = jnp.full((experts * capacity,), count, jnp.int32)
    return (slot_index, filler.at[slot_index].set(jnp.arange(count, dtype=jnp.int32)))


def contract_rows(left, right):
    return lax.dot_general(
        left, right, (((0,), (0,)), ((), ())), preferred_element_type=jnp.float32
    )


def contract_last(left, right):
    return lax.dot_general(
        left, right, (((1,), (1,)), ((), ())), preferred_element_type=jnp.float32
    )


def local(
    tokens,
    lengths,
    expert_ids,
    gates,
    attn_gain,
    w_qkv,
    q_gain,
    k_gain,
    w_out,
    ffn_gain,
    expert_in,
    expert_out,
    out_grad,
):
    single = jnp.float32
    narrow = jnp.bfloat16
    micro_count, seq_len, model_width = tokens.shape
    top_count = expert_ids.shape[2]
    owners = lax.axis_size("expert")
    local_experts = expert_in.shape[0]
    experts = owners * local_experts
    capacity = 5 * seq_len * top_count // (4 * experts)
    shape_rows = (owners, local_experts * capacity, model_width)
    fetched = (
        lax.all_gather(attn_gain, ("dp", "expert"), axis=0, tiled=True),
        lax.all_gather(w_qkv, ("dp", "expert"), axis=0, tiled=True),
        lax.all_gather(q_gain, ("dp", "expert"), axis=0, tiled=True),
        lax.all_gather(k_gain, ("dp", "expert"), axis=0, tiled=True),
        lax.all_gather(w_out, ("dp", "expert"), axis=0, tiled=True),
        lax.all_gather(ffn_gain, ("dp", "expert"), axis=0, tiled=True),
    )
    gain_attn = fetched[0].astype(single)
    weight_qkv = fetched[1]
    gain_query = fetched[2].astype(single)
    gain_key = fetched[3].astype(single)
    weight_out = fetched[4]
    gain_ffn = fetched[5].astype(single)
    whole_in, whole_out = (
        lax.all_gather(expert_in, "dp", axis=1, tiled=True),
        lax.all_gather(expert_out, "dp", axis=1, tiled=True),
    )
    saved = []
    results = []
    for micro_step in range(micro_count):
        inputs = tokens[micro_step].astype(single)
        normal_in, factor_in = normalize(inputs)
        normed_in = (normal_in * gain_attn).astype(narrow)
        projected = jnp.dot(normed_in, weight_qkv, preferred_element_type=single)
        normal_q, factor_q = normalize(projected[:, :model_width])
        normal_k, factor_k = normalize(projected[:, model_width : 2 * model_width])
        document, position = layout(lengths[micro_step, 0], seq_len)
        query_rows = (
            rotate(normal_q * gain_query, position, 1.0).astype(narrow).reshape(seq_len, -1, HEAD)
        )
        key_rows = (
            rotate(normal_k * gain_key, position, 1.0).astype(narrow).reshape(seq_len, -1, HEAD)
        )
        value_rows = projected[:, 2 * model_width :].astype(narrow).reshape(seq_len, -1, HEAD)
        scores = attention_scores(query_rows, key_rows, document)
        highest = jnp.max(scores, axis=-1, keepdims=True)
        unnormed = jnp.exp(scores - highest)
        totals = jnp.sum(unnormed, axis=-1, keepdims=True)
        attn_probs = (unnormed / totals).astype(narrow)
        logsum = highest + jnp.log(totals)
        attended = (
            jnp.einsum("hqk,khd->qhd", attn_probs, value_rows, preferred_element_type=single)
            .reshape(seq_len, model_width)
            .astype(narrow)
        )
        middle = inputs + jnp.dot(attended, weight_out, preferred_element_type=single)
        normal_mid, factor_mid = normalize(middle)
        routed_in = (normal_mid * gain_ffn).astype(narrow)
        slot_index, route_of_slot = route_local(expert_ids[micro_step], experts, capacity)
        weight_in, weight_down = (whole_in, whole_out)
        padded = jnp.concatenate([routed_in, jnp.zeros((1, model_width), narrow)], axis=0)
        outgoing = padded[route_of_slot // top_count].reshape(shape_rows)
        arrived = lax.all_to_all(
            outgoing, "expert", split_axis=0, concat_axis=0, tiled=True
        ).reshape(owners, local_experts, capacity, model_width)
        gate_up = jnp.einsum("necd,edf->necf", arrived, weight_in, preferred_element_type=single)
        hidden_units = gate_up.shape[-1] // 2
        hidden = (jax.nn.silu(gate_up[..., :hidden_units]) * gate_up[..., hidden_units:]).astype(
            narrow
        )
        produced = jnp.einsum(
            "necf,efd->necd", hidden, weight_down, preferred_element_type=single
        ).astype(narrow)
        returned = lax.all_to_all(
            produced.reshape(shape_rows), "expert", split_axis=0, concat_axis=0, tiled=True
        ).reshape(experts * capacity, model_width)
        picked = returned[slot_index].reshape(seq_len, top_count, model_width)
        mixture = jnp.sum(gates[micro_step][..., None] * picked.astype(single), axis=1)
        results.append((middle + mixture).astype(narrow))
        saved.append(
            (
                normal_in,
                factor_in,
                normed_in,
                normal_q,
                factor_q,
                normal_k,
                factor_k,
                document,
                position,
                query_rows,
                key_rows,
                value_rows,
                attn_probs,
                logsum,
                attended,
                normal_mid,
                factor_mid,
                slot_index,
                route_of_slot,
                arrived,
                gate_up,
                hidden,
                picked,
            )
        )
    grad_gain_attn = jnp.zeros((model_width,), single)
    grad_gain_query = jnp.zeros((model_width,), single)
    grad_gain_key = jnp.zeros((model_width,), single)
    grad_gain_ffn = jnp.zeros((model_width,), single)
    grad_qkv_total = jnp.zeros(weight_qkv.shape, single)
    grad_out_total = jnp.zeros(weight_out.shape, single)
    grad_in_whole = jnp.zeros(whole_in.shape, single)
    grad_down_whole = jnp.zeros(whole_out.shape, single)
    token_grads = []
    gate_grads = []
    for micro_step in range(micro_count):
        (
            normal_in,
            factor_in,
            normed_in,
            normal_q,
            factor_q,
            normal_k,
            factor_k,
            document,
            position,
            query_rows,
            key_rows,
            value_rows,
            attn_probs,
            logsum,
            attended,
            normal_mid,
            factor_mid,
            slot_index,
            route_of_slot,
            arrived,
            gate_up,
            hidden,
            picked,
        ) = saved[micro_step]
        upstream = out_grad[micro_step].astype(single)
        gate_grads.append(jnp.sum(upstream[:, None, :] * picked.astype(single), axis=2))
        scaled = (
            (gates[micro_step][..., None] * upstream[:, None, :])
            .astype(narrow)
            .reshape(-1, model_width)
        )
        scaled = jnp.concatenate([scaled, jnp.zeros((1, model_width), narrow)], axis=0)
        sent_grads = lax.all_to_all(
            scaled[route_of_slot].reshape(shape_rows),
            "expert",
            split_axis=0,
            concat_axis=0,
            tiled=True,
        ).reshape(owners, local_experts, capacity, model_width)
        weight_in, weight_down = (whole_in, whole_out)
        grad_hidden = jnp.einsum(
            "necd,efd->necf", sent_grads, weight_down, preferred_element_type=single
        )
        hidden_units = gate_up.shape[-1] // 2
        gate_part = gate_up[..., :hidden_units]
        up_part = gate_up[..., hidden_units:]
        sigmoid = jax.nn.sigmoid(gate_part)
        activated = gate_part * sigmoid
        grad_gate = grad_hidden * up_part * sigmoid * (1.0 + gate_part * (1.0 - sigmoid))
        grad_up = grad_hidden * activated
        grad_gate_up = jnp.concatenate([grad_gate, grad_up], axis=-1).astype(narrow)
        part_down = jnp.einsum("necf,necd->efd", hidden, sent_grads, preferred_element_type=single)
        part_in = jnp.einsum("necd,necf->edf", arrived, grad_gate_up, preferred_element_type=single)
        grad_rows = jnp.einsum(
            "necf,edf->necd", grad_gate_up, weight_in, preferred_element_type=single
        ).astype(narrow)
        grad_in_whole = grad_in_whole + part_in
        grad_down_whole = grad_down_whole + part_down
        came_back = lax.all_to_all(
            grad_rows.reshape(shape_rows), "expert", split_axis=0, concat_axis=0, tiled=True
        ).reshape(experts * capacity, model_width)
        grad_routed = jnp.sum(
            came_back[slot_index].reshape(seq_len, top_count, model_width).astype(single), axis=1
        )
        grad_mid, gain_piece = rms_back(grad_routed, normal_mid, factor_mid, gain_ffn)
        grad_gain_ffn = grad_gain_ffn + gain_piece
        grad_middle = upstream + grad_mid
        grad_branch = grad_middle.astype(narrow)
        grad_out_total = grad_out_total + contract_rows(attended, grad_branch)
        grad_attended = (
            contract_last(grad_branch, weight_out).astype(narrow).reshape(seq_len, -1, HEAD)
        )
        scores = attention_scores(query_rows, key_rows, document)
        probs_full = jnp.exp(scores - logsum)
        grad_probs = jnp.einsum(
            "qhd,khd->hqk", grad_attended, value_rows, preferred_element_type=single
        )
        inner = jnp.sum(grad_probs * probs_full, axis=-1, keepdims=True)
        grad_scores = (probs_full * (grad_probs - inner)).astype(narrow)
        grad_query = jnp.einsum(
            "hqk,khd->qhd", grad_scores, key_rows, preferred_element_type=single
        ) * HEAD ** (-0.5)
        grad_key = jnp.einsum(
            "hqk,qhd->khd", grad_scores, query_rows, preferred_element_type=single
        ) * HEAD ** (-0.5)
        grad_value = jnp.einsum(
            "hqk,qhd->khd", attn_probs, grad_attended, preferred_element_type=single
        )
        grad_q_raw, query_piece = rms_back(
            rotate(grad_query.reshape(seq_len, model_width), position, -1.0),
            normal_q,
            factor_q,
            gain_query,
        )
        grad_k_raw, key_piece = rms_back(
            rotate(grad_key.reshape(seq_len, model_width), position, -1.0),
            normal_k,
            factor_k,
            gain_key,
        )
        grad_gain_query = grad_gain_query + query_piece
        grad_gain_key = grad_gain_key + key_piece
        grad_qkv = jnp.concatenate(
            [grad_q_raw, grad_k_raw, grad_value.reshape(seq_len, model_width)], axis=1
        ).astype(narrow)
        grad_qkv_total = grad_qkv_total + contract_rows(normed_in, grad_qkv)
        grad_normed = contract_last(grad_qkv, weight_qkv)
        grad_input, attn_piece = rms_back(grad_normed, normal_in, factor_in, gain_attn)
        grad_gain_attn = grad_gain_attn + attn_piece
        token_grads.append(grad_middle + grad_input)
    sums = (
        lax.psum_scatter(grad_gain_attn, ("dp", "expert"), scatter_dimension=0, tiled=True),
        lax.psum_scatter(grad_qkv_total, ("dp", "expert"), scatter_dimension=0, tiled=True),
        lax.psum_scatter(grad_gain_query, ("dp", "expert"), scatter_dimension=0, tiled=True),
        lax.psum_scatter(grad_gain_key, ("dp", "expert"), scatter_dimension=0, tiled=True),
        lax.psum_scatter(grad_out_total, ("dp", "expert"), scatter_dimension=0, tiled=True),
        lax.psum_scatter(grad_gain_ffn, ("dp", "expert"), scatter_dimension=0, tiled=True),
    )
    grad_in_share, grad_down_share = (
        lax.psum_scatter(
            grad_in_whole.astype(jnp.bfloat16), "dp", scatter_dimension=1, tiled=True
        ).astype(jnp.float32),
        lax.psum_scatter(
            grad_down_whole.astype(jnp.bfloat16), "dp", scatter_dimension=1, tiled=True
        ).astype(jnp.float32),
    )
    return (
        jnp.stack(results),
        jnp.stack(token_grads),
        jnp.stack(gate_grads),
        sums[0],
        sums[1],
        sums[2],
        sums[3],
        sums[4],
        sums[5],
        grad_in_share,
        grad_down_share,
    )


def solution(mesh):
    return jax.shard_map(
        local,
        mesh=mesh,
        in_specs=(
            P(None, ("dp", "expert"), None),
            P(None, ("dp", "expert"), None),
            P(None, ("dp", "expert"), None),
            P(None, ("dp", "expert"), None),
            P(("dp", "expert")),
            P(("dp", "expert"), None),
            P(("dp", "expert")),
            P(("dp", "expert")),
            P(("dp", "expert"), None),
            P(("dp", "expert")),
            P("expert", "dp", None),
            P("expert", "dp", None),
            P(None, ("dp", "expert"), None),
        ),
        out_specs=(
            P(None, ("dp", "expert"), None),
            P(None, ("dp", "expert"), None),
            P(None, ("dp", "expert"), None),
            P(("dp", "expert")),
            P(("dp", "expert"), None),
            P(("dp", "expert")),
            P(("dp", "expert")),
            P(("dp", "expert"), None),
            P(("dp", "expert")),
            P("expert", "dp", None),
            P("expert", "dp", None),
        ),
        check_vma=False,
    )
```

profile of v0, /device:TPU:0, one launch (start us, length us, event | category | flops | bytes accessed | tf_op | source)
XLA Modules:
  0.0 1912.1 jit_solution(4744712112241388438)
XLA Ops:
  11.6 43.7 %all-reduce.13 = (bf16[2048]{0:T(1024)(128)(2,1)S(1)}, bf16[2048]{0:T(1024)(128)(2,1)S(1)}, bf16[2048]{0:T(1024)(128)(2,1)S(1)}, bf16[2048]{0:T(1024)(128)(2,1)S(1)}) all-reduce(bf16[2048]{0:T(1024)(128)(2,1)S(1)} %dynamic-update-slice, bf16[2048]{0:T(1024)(128)(2,1)S(1)} %dynamic-update-slice.2, ...), channel_id=1, replica_groups=mesh['dp'=4,'expert'=8] {'dp','expert'}, use_global_device_ids=true, to_apply=%add.4 | all-reduce | flops 8192 | bytes 32768
  61.3 108.4 %all-gather.5.cloned.1.call-done = bf16[2048,6144]{1,0:T(8,128)(2,1)} async-done(((bf16[64,6144]{1,0:T(8,128)(2,1)}), bf16[2048,6144]{1,0:T(8,128)(2,1)}) %all-gather.5.cloned.1.call-update) | async-done | bytes 25165840 | tf_op jit(solution)/shard_map/all_gather | solution.py:113
  169.7 10.5 fusion.155
  180.5 11.0 fusion.158
  197.1 51.0 %all-gather.7.cloned.1.call-done = bf16[2048,2048]{1,0:T(8,128)(2,1)} async-done(((bf16[64,2048]{1,0:T(8,128)(2,1)}), bf16[2048,2048]{1,0:T(8,128)(2,1)}) %all-gather.7.cloned.1.call-update) | async-done | bytes 8388624 | tf_op jit(solution)/shard_map/all_gather | solution.py:116
  274.7 20.6 %all-to-all-done = bf16[8,80,2048]{2,1,0:T(8,128)(2,1)} async-done(((bf16[8,80,2048]{2,1,0:T(8,128)(2,1)}), bf16[8,80,2048]{2,1,0:T(8,128)(2,1)}, u32[]{:S(2)}, u32[]{:S(2)}) %all-to-all-start) | async-done | bytes 2621472 | tf_op jit(solution)/shard_map/all_to_all | solution.py:164
  299.1 236.1 %all-gather.9.cloned.1.call-done = bf16[2,2048,2048]{2,1,0:T(8,128)(2,1)} async-done(((bf16[2,512,2048]{2,1,0:T(8,128)(2,1)}), bf16[2,2048,2048]{2,1,0:T(8,128)(2,1)}) %all-gather.9.cloned.1.call-update) | async-done | bytes 16777232 | tf_op jit(solution)/shard_map/all_gather | solution.py:126
  535.1 13.5 fusion.24
  548.7 135.7 %all-gather.11.cloned.1.call-done = bf16[2,1024,2048]{2,1,0:T(8,128)(2,1)} async-done(((bf16[2,256,2048]{2,1,0:T(8,128)(2,1)}), bf16[2,1024,2048]{2,1,0:T(8,128)(2,1)}) %all-gather.11.cloned.1.call-update) | async-done | bytes 8388624 | tf_op jit(solution)/shard_map/all_gather | solution.py:127
  684.4 11.8 fusion.60
  696.3 10.1 fusion.45
  724.2 20.1 %all-to-all-done.5 = bf16[8,80,2048]{2,1,0:T(8,128)(2,1)S(1)} async-done(((bf16[8,80,2048]{2,1,0:T(8,128)(2,1)}), bf16[8,80,2048]{2,1,0:T(8,128)(2,1)S(1)}, u32[]{:S(2)}, u32[]{:S(2)}) %all-to-all-start.5) | async-done | bytes 2621472 | tf_op jit(solution)/shard_map/all_to_all | solution.py:278
  765.9 26.5 %all-to-all-done.2 = bf16[8,80,2048]{2,1,0:T(8,128)(2,1)} async-done(((bf16[8,80,2048]{2,1,0:T(8,128)(2,1)}), bf16[8,80,2048]{2,1,0:T(8,128)(2,1)}, u32[]{:S(2)}, u32[]{:S(2)}) %all-to-all-start.2) | async-done | bytes 2621472 | tf_op jit(solution)/shard_map/all_to_all | solution.py:164
  797.2 9.5 fusion.71
  806.8 13.5 fusion.27
  820.2 9.0 all-to-all-done.6
  829.3 10.9 fusion.56
  840.2 11.5 fusion.1
  853.4 18.0 fusion.63
  871.4 20.2 %fusion = bf16[2,2048,2048]{2,1,0:T(8,128)(2,1)} fusion(f32[2,2048,2048,1]{2,1,0,3:T(8,128)} %fusion.63, bf16[8,2,40,2048]{3,2,1,0:T(8,128)(2,1)} %bitcast.33, bf16[8,2,40,1024]{3,2,0,1:T(8,128)(2,1)S(1)} %copy-done.106, bf16[8,2,40,1024]{3,2,0,1:T(8,128)(2,1)S(1)} %copy-done.105), kind=kOutput, calls=%fused_computation.11 | convolution fusion | flops 5390729216 | bytes 55574528 | tf_op jit(solution)/shard_map/necd,necf->edf/dot_general | solution.py:272
  905.0 10.3 fusion.42
  917.0 20.2 %all-to-all-done.1 = bf16[8,80,2048]{2,1,0:T(8,128)(2,1)S(1)} async-done(((bf16[8,80,2048]{2,1,0:T(8,128)(2,1)}), bf16[8,80,2048]{2,1,0:T(8,128)(2,1)S(1)}, u32[]{:S(2)}, u32[]{:S(2)}) %all-to-all-start.1) | async-done | bytes 2621472 | tf_op jit(solution)/shard_map/all_to_all | solution.py:175
  950.6 23.8 %all-to-all-done.7 = bf16[8,80,2048]{2,1,0:T(8,128)(2,1)} async-done(((bf16[8,80,2048]{2,1,0:T(8,128)(2,1)}), bf16[8,80,2048]{2,1,0:T(8,128)(2,1)}, u32[]{:S(2)}, u32[]{:S(2)}) %all-to-all-start.7) | async-done | bytes 2621472 | tf_op jit(solution)/shard_map/all_to_all | solution.py:278
  992.0 19.0 all-to-all-done.3
  1054.6 20.6 %fusion.117 = f32[2048,6144]{1,0:T(8,128)} fusion(bf16[64,2048]{1,0:T(8,128)(2,1)S(1)} %bitcast.410, bf16[64,2048]{1,0:T(8,128)(2,1)S(1)} %get-tuple-element.122, bf16[64,2048]{1,0:T(8,128)(2,1)S(1)} %get-tuple-element.123, f32[2048]{0:T(1024)S(1)} %copy-done.48, f32[64]{0:T(128)S(1)} %copy-done.73, bf16[2,64,2048]{2,1,0:T(8,128)(2,1)S(1)} %copy-done.5), kind=kOutput, calls=%fused_computation.223 | convolution fusion | flops 1613496320 | bytes 51388928 | tf_op jit(solution)/shard_map/dot_general | solution.py:76
  1075.3 32.2 %convolution_add_fusion = f32[2048,6144]{1,0:T(8,128)} fusion(f32[2048,6144]{1,0:T(8,128)} %fusion.117, bf16[64,2048]{1,0:T(8,128)(2,1)S(1)} %bitcast.412, bf16[64,2048]{1,0:T(8,128)(2,1)S(1)} %get-tuple-element.75, bf16[64,2048]{1,0:T(8,128)(2,1)S(1)} %get-tuple-element.74, f32[64]{0:T(128)S(1)} %copy-done.71, f32[2048]{0:T(1024)S(1)} %copy-done.48, ...), kind=kOutput, calls=%fused_computation.12 | convolution fusion | flops 1626079232 | bytes 101720576 | tf_op jit(solution)/shard_map/dot_general | solution.py:76
  1107.6 12.6 fusion.116
  1120.2 12.9 fusion.100
  1133.2 41.0 %all-reduce.12 = (f32[2048]{0:T(1024)S(1)}, f32[2048]{0:T(1024)S(1)}, f32[2048]{0:T(1024)S(1)}, f32[2048]{0:T(1024)S(1)}) all-reduce(f32[2048]{0:T(1024)S(1)} %add.287, f32[2048]{0:T(1024)S(1)} %add.289, f32[2048]{0:T(1024)S(1)} %add.290, f32[2048]{0:T(1024)S(1)} %add.292), channel_id=2, replica_groups=mesh['dp'=4,'expert'=8] {'dp','expert'}, use_global_device_ids=true, to_apply=%region_44.45.clone | all-reduce | flops 8192 | bytes 65536
  1184.6 92.5 %reduce-scatter.9.cloned.1.call-done = bf16[2,512,2048]{2,1,0:T(8,128)(2,1)} async-done(((bf16[2,2048,2048]{2,1,0:T(8,128)(2,1)}), bf16[2,512,2048]{2,1,0:T(8,128)(2,1)}) %reduce-scatter.9.cloned.1.call-update) | async-done | bytes 4194320 | tf_op jit(solution)/shard_map/reduce_scatter | solution.py:339
  1283.7 180.0 %reduce-scatter.7.cloned.1.call-done = f32[64,2048]{1,0:T(8,128)} async-done(((f32[2048,2048]{1,0:T(8,128)}), f32[64,2048]{1,0:T(8,128)}) %reduce-scatter.7.cloned.1.call-update) | async-done | bytes 524304 | tf_op jit(solution)/shard_map/reduce_scatter | solution.py:335
  1463.7 441.3 %reduce-scatter.5.cloned.1.call-done = f32[64,6144]{1,0:T(8,128)} async-done(((f32[2048,6144]{1,0:T(8,128)}), f32[64,6144]{1,0:T(8,128)}) %reduce-scatter.5.cloned.1.call-update) | async-done | bytes 1572880 | tf_op jit(solution)/shard_map/reduce_scatter | solution.py:332
  (408 shorter events, 197.8 us)
Async XLA Ops:
  7.2 162.5 %all-gather.5.cloned.1.call-start = ((), (), s32[]{:S(2)}) async-start(), calls=%async_computation.12 | async-start | bytes 25952256 | tf_op jit(solution)/shard_map/all_gather | solution.py:113
  7.9 240.3 %all-gather.7.cloned.1.call-start = ((), (), s32[]{:S(2)}) async-start(), calls=%async_computation.13 | async-start | bytes 8650752 | tf_op jit(solution)/shard_map/all_gather | solution.py:116
  8.7 46.6 %copy-start.95 = (s32[2,1,4]{2,1,0:T(1,128)S(1)}, s32[2,1,4]{2,1,0:T(1,128)}, u32[]{:S(2)}) copy-start(s32[2,1,4]{2,1,0:T(1,128)} %param.14) | copy-start | bytes 100
  8.7 526.4 %all-gather.9.cloned.1.call-start = ((), (), s32[]{:S(2)}) async-start(), calls=%async_computation.14 | async-start | bytes 20971520 | tf_op jit(solution)/shard_map/all_gather | solution.py:126
  9.5 675.0 %all-gather.11.cloned.1.call-start = ((), (), s32[]{:S(2)}) async-start(), calls=%async_computation.15 | async-start | bytes 10485760 | tf_op jit(solution)/shard_map/all_gather | solution.py:127
  10.6 169.7 %copy-start.70 = (f32[64]{0:T(128)}, f32[64]{0:T(128)S(1)}, u32[]{:S(2)}) copy-start(f32[64]{0:T(128)S(1)} %add_rsqrt_fusion.3) | copy-start | bytes 772
  55.3 125.2 %copy-start.47 = (f32[2048]{0:T(1024)}, f32[2048]{0:T(1024)S(1)}, u32[]{:S(2)}) copy-start(f32[2048]{0:T(1024)S(1)} %convert_element_type.244) | copy-start | bytes 24580
  55.3 136.4 %copy-start.55 = (f32[2048]{0:T(1024)}, f32[2048]{0:T(1024)S(1)}, u32[]{:S(2)}) copy-start(f32[2048]{0:T(1024)S(1)} %convert_element_type.247) | copy-start | bytes 24580
  55.3 136.4 %copy-start.57 = (f32[2048]{0:T(1024)}, f32[2048]{0:T(1024)S(1)}, u32[]{:S(2)}) copy-start(f32[2048]{0:T(1024)S(1)} %convert_element_type.249) | copy-start | bytes 24580
  55.4 125.1 %copy-start.72 = (f32[64]{0:T(128)}, f32[64]{0:T(128)S(1)}, u32[]{:S(2)}) copy-start(f32[64]{0:T(128)S(1)} %add_rsqrt_fusion.7) | copy-start | bytes 772
  56.0 694.8 %copy-start.53 = (f32[2048]{0:T(1024)}, f32[2048]{0:T(1024)S(1)}, u32[]{:S(2)}) copy-start(f32[2048]{0:T(1024)S(1)} %convert_element_type.254) | copy-start | bytes 24580
  61.3 132.3 %copy-start.49 = (f32[64,64]{1,0:T(8,128)}, f32[64,64]{1,0:T(8,128)S(1)}, u32[]{:S(2)}) copy-start(f32[64,64]{1,0:T(8,128)S(1)} %get-tuple-element.143) | copy-start | bytes 49156
  61.3 653.6 %copy-start.51 = (f32[64,64]{1,0:T(8,128)}, f32[64,64]{1,0:T(8,128)S(1)}, u32[]{:S(2)}) copy-start(f32[64,64]{1,0:T(8,128)S(1)} %get-tuple-element.152) | copy-start | bytes 49156
  195.4 57.8 %copy-start.61 = (f32[16,64]{1,0:T(8,128)}, f32[16,64]{1,0:T(8,128)S(1)}, u32[]{:S(2)}) copy-start(f32[16,64]{1,0:T(8,128)S(1)} %get-tuple-element.154) | copy-start | bytes 12292
  197.1 56.1 %copy-start.43 = (bf16[16,8,8,128]{3,2,1,0:T(8,128)(2,1)}, bf16[16,8,8,128]{3,2,1,0:T(8,128)(2,1)S(1)}, u32[]{:S(2)}) copy-start(bf16[16,8,8,128]{3,2,1,0:T(8,128)(2,1)S(1)} %fusion.80) | copy-start | bytes 786436
  253.3 497.5 %copy-start.93 = (f32[64]{0:T(128)}, f32[64]{0:T(128)S(1)}, u32[]{:S(2)}) copy-start(f32[64]{0:T(128)S(1)} %add_rsqrt_fusion.4) | copy-start | bytes 772
  258.3 37.1 %all-to-all-start = ((bf16[8,80,2048]{2,1,0:T(8,128)(2,1)}), bf16[8,80,2048]{2,1,0:T(8,128)(2,1)}, u32[]{:S(2)}, u32[]{:S(2)}) async-start(bf16[8,80,2048]{2,1,0:T(8,128)(2,1)} %bitcast.10), calls=%async_computation | async-start | bytes 5242880 | tf_op jit(solution)/shard_map/all_to_all | solution.py:164
  295.3 253.3 %all-to-all-start.4 = ((bf16[8,80,2048]{2,1,0:T(8,128)(2,1)}), bf16[8,80,2048]{2,1,0:T(8,128)(2,1)S(1)}, u32[]{:S(2)}, u32[]{:S(2)}) async-start(bf16[8,80,2048]{2,1,0:T(8,128)(2,1)} %bitcast.398), calls=%async_computation.4 | async-start | bytes 5242880 | tf_op jit(solution)/shard_map/all_to_all | solution.py:252
  548.7 147.6 %copy-start.24 = (bf16[8,80,2048]{2,1,0:T(8,128)(2,1)}, bf16[8,80,2048]{2,1,0:T(8,128)(2,1)S(1)}, u32[]{:S(2)}) copy-start(bf16[8,80,2048]{2,1,0:T(8,128)(2,1)S(1)} %all-to-all-done.4) | copy-start | bytes 7864324
  708.0 36.3 %all-to-all-start.5 = ((bf16[8,80,2048]{2,1,0:T(8,128)(2,1)}), bf16[8,80,2048]{2,1,0:T(8,128)(2,1)S(1)}, u32[]{:S(2)}, u32[]{:S(2)}) async-start(bf16[8,80,2048]{2,1,0:T(8,128)(2,1)} %bitcast.400), calls=%async_computation.5 | async-start | bytes 5242880 | tf_op jit(solution)/shard_map/all_to_all | solution.py:278
  712.1 32.2 %copy-start.74 = (s32[1024]{0:T(1024)}, s32[1024]{0:T(1024)S(1)}, u32[]{:S(2)}) copy-start(s32[1024]{0:T(1024)S(1)} %pad_clamp_fusion.4) | copy-start | bytes 12292
  724.2 26.5 %copy-start.91 = (f32[64]{0:T(128)}, f32[64]{0:T(128)S(1)}, u32[]{:S(2)}) copy-start(f32[64]{0:T(128)S(1)} %add_rsqrt_fusion) | copy-start | bytes 772
  755.7 36.7 %all-to-all-start.2 = ((bf16[8,80,2048]{2,1,0:T(8,128)(2,1)}), bf16[8,80,2048]{2,1,0:T(8,128)(2,1)}, u32[]{:S(2)}, u32[]{:S(2)}) async-start(bf16[8,80,2048]{2,1,0:T(8,128)(2,1)} %bitcast.32), calls=%async_computation.2 | async-start | bytes 5242880 | tf_op jit(solution)/shard_map/all_to_all | solution.py:164
  792.3 36.9 %all-to-all-start.6 = ((bf16[8,80,2048]{2,1,0:T(8,128)(2,1)}), bf16[8,80,2048]{2,1,0:T(8,128)(2,1)}, u32[]{:S(2)}, u32[]{:S(2)}) async-start(bf16[8,80,2048]{2,1,0:T(8,128)(2,1)} %bitcast.399), calls=%async_computation.6 | async-start | bytes 5242880 | tf_op jit(solution)/shard_map/all_to_all | solution.py:252
  797.0 383.5 %reduce-scatter.11.cloned.1.call-start = ((), (), s32[]{:S(2)}) async-start(), calls=%async_computation.19 | async-start | bytes 10485760 | tf_op jit(solution)/shard_map/reduce_scatter | solution.py:342
  851.7 425.3 %reduce-scatter.9.cloned.1.call-start = ((), (), s32[]{:S(2)}) async-start(), calls=%async_computation.18 | async-start | bytes 20971520 | tf_op jit(solution)/shard_map/reduce_scatter | solution.py:339
  901.4 35.8 %all-to-all-start.1 = ((bf16[8,80,2048]{2,1,0:T(8,128)(2,1)}), bf16[8,80,2048]{2,1,0:T(8,128)(2,1)S(1)}, u32[]{:S(2)}, u32[]{:S(2)}) async-start(bf16[8,80,2048]{2,1,0:T(8,128)(2,1)} %bitcast.403), calls=%async_computation.1 | async-start | bytes 5242880 | tf_op jit(solution)/shard_map/all_to_all | solution.py:175
  937.2 37.1 %all-to-all-start.7 = ((bf16[8,80,2048]{2,1,0:T(8,128)(2,1)}), bf16[8,80,2048]{2,1,0:T(8,128)(2,1)}, u32[]{:S(2)}, u32[]{:S(2)}) async-start(bf16[8,80,2048]{2,1,0:T(8,128)(2,1)} %bitcast.402), calls=%async_computation.7 | async-start | bytes 5242880 | tf_op jit(solution)/shard_map/all_to_all | solution.py:278
  974.3 36.7 %all-to-all-start.3 = ((bf16[8,80,2048]{2,1,0:T(8,128)(2,1)}), bf16[8,80,2048]{2,1,0:T(8,128)(2,1)}, u32[]{:S(2)}, u32[]{:S(2)}) async-start(bf16[8,80,2048]{2,1,0:T(8,128)(2,1)} %bitcast.401), calls=%async_computation.3 | async-start | bytes 5242880 | tf_op jit(solution)/shard_map/all_to_all | solution.py:175
  978.7 484.9 %reduce-scatter.7.cloned.1.call-start = ((), (), s32[]{:S(2)}) async-start(), calls=%async_computation.17 | async-start | bytes 17301504 | tf_op jit(solution)/shard_map/reduce_scatter | solution.py:335
  1033.7 871.2 %reduce-scatter.5.cloned.1.call-start = ((), (), s32[]{:S(2)}) async-start(), calls=%async_computation.16 | async-start | bytes 51904512 | tf_op jit(solution)/shard_map/reduce_scatter | solution.py:332
  1041.0 34.3 %copy-start.26 = (bf16[16,8,8,128]{3,2,0,1:T(8,128)(2,1)}, bf16[16,8,8,128]{3,2,0,1:T(8,128)(2,1)S(1)}, u32[]{:S(2)}) copy-start(bf16[16,8,8,128]{3,2,0,1:T(8,128)(2,1)S(1)} %copy.411) | copy-start | bytes 786436
  (92 other events, 310.9 us)
Sparse Core Ops, SparseCore 0:
  10.9 158.7 all-gather.4
  172.6 75.5 all-gather.6
  249.7 285.3 all-gather.8
  536.6 147.8 all-gather.10
  851.8 140.8 reduce-scatter.10
  995.0 282.0 reduce-scatter.8
  1280.0 183.5 reduce-scatter.6
  1471.8 433.1 reduce-scatter.4
where the time goes:
time: 1920 us; the launch traced here: 1910 us
  waiting for transfers between devices  1390 us (72%)
  matrix products  281 us (15%)
  blocking collectives  84.7 us (4%)
  local copies, waits for them, and re-layouts  68.7 us (4%)
  other arithmetic  39.1 us (2%)
  starting transfers between devices  35.3 us (2%)
    reduce_scatter x1, waiting for transfers between devices, local(): lax.psum_scatter(grad_qkv_total, ('dp', 'expert'), scatter_dimension=0, t...  441 us
    all_gather x1, waiting for transfers between devices, local(): lax.all_gather(expert_in, 'dp', axis=1, tiled=True)  236 us
    reduce_scatter x1, waiting for transfers between devices, local(): lax.psum_scatter(grad_out_total, ('dp', 'expert'), scatter_dimension=0, t...  180 us
    all_gather x1, waiting for transfers between devices, local(): lax.all_gather(expert_out, 'dp', axis=1, tiled=True)  136 us
    all_gather x1, waiting for transfers between devices, local(): lax.all_gather(w_qkv, ('dp', 'expert'), axis=0, tiled=True)  108 us
    reduce_scatter x1, waiting for transfers between devices, local(): lax.psum_scatter(grad_in_whole.astype(jnp.bfloat16), 'dp', scatter_dimens...  92.5 us
    unnamed x2, blocking collectives  84.7 us
    dot_general x4, matrix products, contract_rows(): lax.dot_general(left, right, (((0,), (0,)), ((), ())), preferred_element_...  63.4 us
  transfers between devices with their start and end apart: 16, of which 14 were waited for; matrix products, arithmetic and copies ran while one was open for 17% of the time, Pallas kernels for 0%

commit v1 on v0

v1 whole, which is shorter than its diff:
```python
import jax
import jax.numpy as jnp
from jax import lax
from jax.sharding import PartitionSpec as P

HEAD = 128
epsilon = 1e-05
base_theta = 10000.0
masked_score = -1e30
single = jnp.float32
narrow = jnp.bfloat16


def normalize(values):
    factor = lax.rsqrt(jnp.mean(values * values, axis=-1, keepdims=True) + epsilon)
    return (values * factor, factor)


def rms_back(upstream, normal, factor, gain):
    weighted = upstream * gain
    inner = jnp.mean(weighted * normal, axis=-1, keepdims=True)
    return (factor * (weighted - normal * inner), jnp.sum(upstream * normal, axis=0))


def angles(position):
    half = HEAD // 2
    ladder = jnp.arange(half, dtype=single) * (2.0 / HEAD)
    frequency = jnp.exp(-jnp.log(base_theta) * ladder)
    angle = position.astype(single)[:, None] * frequency[None, :]
    return (jnp.cos(angle)[:, None, :], jnp.sin(angle)[:, None, :])


def rotate(field, cosine, sine):
    length = field.shape[0]
    heads = field.reshape(length, -1, HEAD)
    half = HEAD // 2
    first = heads[..., :half]
    second = heads[..., half:]
    turned = jnp.concatenate(
        [first * cosine - second * sine, second * cosine + first * sine], axis=-1
    )
    return turned.reshape(length, -1)


def layout(doc_lengths, length):
    packs, count = doc_lengths.shape
    upto = jnp.arange(count)[None, :] <= jnp.arange(count)[:, None]
    ends = jnp.sum(jnp.where(upto[None], doc_lengths[:, None, :], 0), axis=2)
    starts = ends - doc_lengths
    places = jnp.arange(length, dtype=jnp.int32)[None, :, None]
    document = jnp.sum((places >= ends[:, None, :]).astype(jnp.int32), axis=2)
    member = (places >= starts[:, None, :]) & (places < ends[:, None, :])
    first_place = jnp.sum(jnp.where(member, starts[:, None, :], 0), axis=2)
    document = document + (count + 1) * jnp.arange(packs, dtype=jnp.int32)[:, None]
    return (document.reshape(-1), (places[..., 0] - first_place).reshape(-1))


def contract_rows(left, right, kind=single):
    return lax.dot_general(left, right, (((0,), (0,)), ((), ())), preferred_element_type=kind)


def contract_last(left, right, kind=single):
    return lax.dot_general(left, right, (((1,), (1,)), ((), ())), preferred_element_type=kind)


def core_groups():
    return [[2 * chip + core for chip in range(lax.axis_size("expert") // 2)] for core in range(2)]


def chip_groups():
    return [[2 * chip, 2 * chip + 1] for chip in range(lax.axis_size("expert") // 2)]


def gather_alike(block):
    column = lax.all_gather(block, "dp", axis=0)
    return lax.all_gather(column, "expert", axis=1, axis_index_groups=core_groups())


def scatter_alike(blocks):
    column = lax.psum_scatter(
        blocks, "expert", scatter_dimension=1, axis_index_groups=core_groups()
    )
    return lax.psum_scatter(column, "dp", scatter_dimension=0)


def fetch_weights(expert_in, expert_out):
    depth = lax.axis_size("dp")
    held, rows, columns = expert_in.shape
    part = columns // (2 * depth)
    cut = expert_in.reshape(held, rows, 2, depth, part)
    turned = lax.all_to_all(cut, "dp", split_axis=3, concat_axis=1, tiled=True)
    both = lax.all_gather(turned[:, :, :, 0], "expert", axis=0, axis_index_groups=chip_groups())
    weight_in = both.transpose(2, 3, 0, 1, 4).reshape(depth * rows, 4 * held * part)
    weight_down = lax.all_gather(
        expert_out, "expert", axis=0, axis_index_groups=chip_groups()
    ).reshape(-1, expert_out.shape[2])
    return (weight_in, weight_down)


def return_weights(grad_in, grad_down, held):
    depth = lax.axis_size("dp")
    rows, columns = grad_in.shape
    part = columns // (4 * held)
    cut = grad_in.reshape(rows, 2, 2, held, part)
    own = lax.psum_scatter(cut, "expert", scatter_dimension=2, axis_index_groups=chip_groups())
    own = own.reshape(depth, rows // depth, 2, held, part)
    turned = lax.all_to_all(own, "dp", split_axis=0, concat_axis=0)
    share_in = turned.transpose(3, 1, 2, 0, 4).reshape(held, rows // depth, 2 * depth * part)
    down = grad_down.reshape(2, held, part, grad_down.shape[1])
    share_down = lax.psum_scatter(
        down, "expert", scatter_dimension=0, axis_index_groups=chip_groups()
    )
    return (share_in, share_down)


def expert_round(mid_rows, up_rows, gate, weight_in, weight_down):
    count = gate.shape[1]
    part = weight_down.shape[0] // count
    wide = jnp.broadcast_to(gate[:, :, None], gate.shape + (part,)).reshape(gate.shape[0], -1)
    gate_up = jnp.dot(mid_rows, weight_in, preferred_element_type=single)
    hidden_units = gate_up.shape[1] // 2
    gate_part = gate_up[:, :hidden_units]
    up_part = gate_up[:, hidden_units:]
    sigmoid = jax.nn.sigmoid(gate_part)
    activated = gate_part * sigmoid
    hidden = activated * up_part
    back = contract_last(up_rows, weight_down)
    scaled = (wide * hidden).astype(narrow)
    piece_out = jnp.dot(scaled, weight_down, preferred_element_type=narrow)
    piece_gates = jnp.sum((hidden * back).reshape(-1, count, part), axis=2)
    grad_hidden = wide * back
    grad_gate = grad_hidden * up_part * sigmoid * (1.0 + gate_part * (1.0 - sigmoid))
    grad_up = grad_hidden * activated
    grad_gate_up = jnp.concatenate([grad_gate, grad_up], axis=1).astype(narrow)
    piece_mid = contract_last(grad_gate_up, weight_in, narrow)
    return (piece_out, piece_mid, piece_gates, grad_gate_up, scaled)


def expert_rounds(mid_rows, up_rows, gate, weight_in, weight_down):
    total = mid_rows.shape[0]
    rounds = max(1, total // 2048)

    def one(sums, pieces):
        mid, up, weights = pieces
        piece_out, piece_mid, piece_gates, grad_gate_up, scaled = expert_round(
            mid, up, weights, weight_in, weight_down
        )
        grads = (contract_rows(mid, grad_gate_up), contract_rows(scaled, up))
        return (jax.tree.map(jnp.add, sums, grads), (piece_out, piece_mid, piece_gates))

    if rounds == 1:
        piece_out, piece_mid, piece_gates, grad_gate_up, scaled = expert_round(
            mid_rows, up_rows, gate, weight_in, weight_down
        )
        grads = (contract_rows(mid_rows, grad_gate_up, narrow), contract_rows(scaled, up_rows, narrow))
        return (piece_out, piece_mid, piece_gates) + grads
    start = (jnp.zeros(weight_in.shape, single), jnp.zeros(weight_down.shape, single))
    cut = jax.tree.map(lambda a: a.reshape(rounds, total // rounds, -1), (mid_rows, up_rows, gate))
    sums, made = lax.scan(one, start, cut)
    made = jax.tree.map(lambda a: a.reshape(total, -1), made)
    return made + (sums[0].astype(narrow), sums[1].astype(narrow))


def local(
    tokens,
    lengths,
    expert_ids,
    gates,
    attn_gain,
    w_qkv,
    q_gain,
    k_gain,
    w_out,
    ffn_gain,
    expert_in,
    expert_out,
    out_grad,
):
    micro_count, seq_len, model_width = tokens.shape
    rows = micro_count * seq_len
    depth = lax.axis_size("dp")
    owners = lax.axis_size("expert")
    held = expert_in.shape[0]
    experts = owners * held
    chip_experts = 2 * held
    everyone = ("dp", "expert")
    gain_rows = jnp.stack([attn_gain, q_gain, k_gain, ffn_gain]).astype(single)
    gains = lax.all_gather(gain_rows, everyone, axis=1, tiled=True)
    gain_attn, gain_query, gain_key, gain_ffn = gains[0], gains[1], gains[2], gains[3]
    weight_qkv = lax.all_gather(w_qkv, everyone, axis=0, tiled=True)
    weight_out = lax.all_gather(w_out, everyone, axis=0, tiled=True)
    weight_in, weight_down = fetch_weights(expert_in, expert_out)

    inputs = tokens.reshape(rows, model_width).astype(single)
    upstream = out_grad.reshape(rows, model_width)
    ids = expert_ids.reshape(rows, -1)
    gate_rows = gates.reshape(rows, -1)
    onehot = (ids[:, :, None] == jnp.arange(experts, dtype=jnp.int32)).astype(single)
    dense = jnp.sum(onehot * gate_rows[:, :, None], axis=1)

    normal_in, factor_in = normalize(inputs)
    normed_in = (normal_in * gain_attn).astype(narrow)
    projected = jnp.dot(normed_in, weight_qkv, preferred_element_type=single)
    normal_q, factor_q = normalize(projected[:, :model_width])
    normal_k, factor_k = normalize(projected[:, model_width : 2 * model_width])
    document, position = layout(lengths[:, 0], seq_len)
    cosine, sine = angles(position)
    query_rows = rotate(normal_q * gain_query, cosine, sine).astype(narrow).reshape(rows, -1, HEAD)
    key_rows = rotate(normal_k * gain_key, cosine, sine).astype(narrow).reshape(rows, -1, HEAD)
    value_rows = projected[:, 2 * model_width :].astype(narrow).reshape(rows, -1, HEAD)
    places = jnp.arange(rows, dtype=jnp.int32)
    allowed = (document[:, None] == document[None, :]) & (places[:, None] >= places[None, :])
    raw = jnp.einsum("qhd,khd->hqk", query_rows, key_rows, preferred_element_type=single)
    scores = jnp.where(allowed[None], raw * HEAD ** (-0.5), masked_score)
    highest = jnp.max(scores, axis=-1, keepdims=True)
    unnormed = jnp.exp(scores - highest)
    probs = unnormed / jnp.sum(unnormed, axis=-1, keepdims=True)
    attn_probs = probs.astype(narrow)
    attended = (
        jnp.einsum("hqk,khd->qhd", attn_probs, value_rows, preferred_element_type=single)
        .reshape(rows, model_width)
        .astype(narrow)
    )
    middle = inputs + jnp.dot(attended, weight_out, preferred_element_type=single)
    normal_mid, factor_mid = normalize(middle)
    routed_in = (normal_mid * gain_ffn).astype(narrow)

    chip = lax.axis_index("expert") // 2
    up_rows = gather_alike(upstream).reshape(-1, model_width)
    mid_rows = gather_alike(routed_in).reshape(-1, model_width)
    every_gate = gather_alike(dense.T)
    mine = lax.dynamic_slice_in_dim(every_gate, chip * chip_experts, chip_experts, axis=2)
    gate = mine.transpose(0, 1, 3, 2).reshape(-1, chip_experts)
    piece_out, piece_mid, piece_gates, grad_in_part, grad_down_part = expert_rounds(
        mid_rows, up_rows, gate, weight_in, weight_down
    )

    chips = owners // 2
    mixture = scatter_alike(piece_out.reshape(depth, chips, rows, model_width)).astype(single)
    grad_routed = scatter_alike(piece_mid.reshape(depth, chips, rows, model_width)).astype(single)
    by_gate = piece_gates.reshape(depth, chips, rows, chip_experts).transpose(0, 1, 3, 2)
    spread = jnp.zeros((depth, chips, experts, rows), single)
    spread = lax.dynamic_update_slice_in_dim(spread, by_gate, chip * chip_experts, axis=2)
    gate_table = scatter_alike(spread).T
    grad_gates = jnp.sum(onehot * gate_table[:, None, :], axis=2)
    results = (middle + mixture).astype(narrow)

    grad_mid, piece_ffn = rms_back(grad_routed, normal_mid, factor_mid, gain_ffn)
    grad_middle = upstream.astype(single) + grad_mid
    grad_branch = grad_middle.astype(narrow)
    grad_out_part = contract_rows(attended, grad_branch, narrow)
    grad_attended = contract_last(grad_branch, weight_out).astype(narrow).reshape(rows, -1, HEAD)
    grad_probs = jnp.einsum("qhd,khd->hqk", grad_attended, value_rows, preferred_element_type=single)
    inner = jnp.sum(grad_probs * probs, axis=-1, keepdims=True)
    grad_scores = (probs * (grad_probs - inner)).astype(narrow)
    grad_query = jnp.einsum(
        "hqk,khd->qhd", grad_scores, key_rows, preferred_element_type=single
    ) * HEAD ** (-0.5)
    grad_key = jnp.einsum(
        "hqk,qhd->khd", grad_scores, query_rows, preferred_element_type=single
    ) * HEAD ** (-0.5)
    grad_value = jnp.einsum("hqk,qhd->khd", attn_probs, grad_attended, preferred_element_type=single)
    grad_q_raw, piece_query = rms_back(
        rotate(grad_query.reshape(rows, model_width), cosine, -sine), normal_q, factor_q, gain_query
    )
    grad_k_raw, piece_key = rms_back(
        rotate(grad_key.reshape(rows, model_width), cosine, -sine), normal_k, factor_k, gain_key
    )
    grad_qkv = jnp.concatenate(
        [grad_q_raw, grad_k_raw, grad_value.reshape(rows, model_width)], axis=1
    ).astype(narrow)
    grad_qkv_part = contract_rows(normed_in, grad_qkv, narrow)
    grad_normed = contract_last(grad_qkv, weight_qkv)
    grad_input, piece_attn = rms_back(grad_normed, normal_in, factor_in, gain_attn)
    grad_tokens = grad_middle + grad_input

    pieces = jnp.stack([piece_attn, piece_query, piece_key, piece_ffn])
    gain_sums = lax.psum_scatter(pieces, everyone, scatter_dimension=1, tiled=True)
    grad_qkv_share = lax.psum_scatter(grad_qkv_part, everyone, scatter_dimension=0, tiled=True)
    grad_out_share = lax.psum_scatter(grad_out_part, everyone, scatter_dimension=0, tiled=True)
    share_in, share_down = return_weights(grad_in_part, grad_down_part, held)
    shape = (micro_count, seq_len, model_width)
    return (
        results.reshape(shape),
        grad_tokens.reshape(shape),
        grad_gates.reshape(expert_ids.shape),
        gain_sums[0],
        grad_qkv_share.astype(single),
        gain_sums[1],
        gain_sums[2],
        grad_out_share.astype(single),
        gain_sums[3],
        share_in.astype(single),
        share_down.astype(single),
    )


def solution(mesh):
    by_rows = P(None, ("dp", "expert"), None)
    flat = P(("dp", "expert"))
    split = P(("dp", "expert"), None)
    held = P("expert", "dp", None)
    return jax.shard_map(
        local,
        mesh=mesh,
        in_specs=(
            by_rows, by_rows, by_rows, by_rows, flat, split, flat, flat, split, flat, held, held, by_rows,
        ),
        out_specs=(by_rows, by_rows, by_rows, flat, split, flat, flat, split, flat, held, held),
        check_vma=False,
    )
```

time: 1920 us -> 1690 us (0.88)
  waiting for transfers between devices: 1390 us -> 1080 us
  matrix products: 281 us -> 194 us
  blocking collectives: 84.7 us -> 166 us
  local copies, waits for them, and re-layouts: 68.7 us -> 143 us
  other arithmetic: 39.1 us -> 63.1 us
  starting transfers between devices: 35.3 us -> 12.6 us
    reduce_scatter x4 -> x6, waiting for transfers between devices: 714 us -> 438 us  [the longest x1 246 us: local(): lax.psum_scatter(grad_qkv_part, everyone, scatter_dimension=0, tiled=True)]
    unnamed x8 -> x24, waiting for transfers between devices: 2.65 us -> 187 us
    all_gather x0 -> x3, blocking collectives: none -> 166 us  [the longest x1 144 us: local(): gains = lax.all_gather(gain_rows, everyone, axis=1, tiled=True)]
    all_gather x4 -> x8, waiting for transfers between devices: 531 us -> 366 us  [the longest x2 141 us: gather_alike(): lax.all_gather(column, 'expert', axis=1, axis_index_groups=core_groups())]
    dot_general x14 -> x2, matrix products: 144 us -> 38.4 us  [the longest x1 24.4 us: expert_round(): gate_up = jnp.dot(mid_rows, weight_in, preferred_element_type=single)]
    unnamed x2 -> x0, blocking collectives: 84.7 us -> none
    reshape x2 -> x7, local copies, waits for them, and re-layouts: 0.09 us -> 55.3 us  [the longest x2 28.9 us: fetch_weights(): both.transpose(2, 3, 0, 1, 4).reshape(depth * rows, 4 * held * part)]
    all_to_all x8 -> x2, waiting for transfers between devices: 139 us -> 91 us  [the longest x1 91 us: return_weights(): turned = lax.all_to_all(own, 'dp', split_axis=0, concat_axis=0)]
  transfers between devices with their start and end apart: 16 -> 21, of which waited for: 14 -> 16; matrix products, arithmetic and copies ran while one was open for 17% -> 18% of each run, Pallas kernels for 0% -> 0%
where the time goes in v1:
time: 1690 us; the launch traced here: 1680 us
  waiting for transfers between devices  1080 us (64%)
  matrix products  194 us (11%)
  blocking collectives  166 us (10%)
  local copies, waits for them, and re-layouts  143 us (8%)
  other arithmetic  63.1 us (4%)
    reduce_scatter x1, waiting for transfers between devices, local(): lax.psum_scatter(grad_qkv_part, everyone, scatter_dimension=0, tiled=True)  246 us
    unnamed x24, waiting for transfers between devices  187 us
    reduce_scatter x1, waiting for transfers between devices, local(): lax.psum_scatter(grad_out_part, everyone, scatter_dimension=0, tiled=True)  162 us
    all_gather x1, blocking collectives, local(): gains = lax.all_gather(gain_rows, everyone, axis=1, tiled=True)  144 us
    all_gather x2, waiting for transfers between devices, gather_alike(): lax.all_gather(column, 'expert', axis=1, axis_index_groups=core_groups())  141 us
    all_to_all x1, waiting for transfers between devices, return_weights(): turned = lax.all_to_all(own, 'dp', split_axis=0, concat_axis=0)  91 us
    all_gather x2, waiting for transfers between devices, gather_alike(): column = lax.all_gather(block, 'dp', axis=0)  84.4 us
    dot_general x4, matrix products, contract_last(): lax.dot_general(left, right, (((1,), (1,)), ((), ())), preferred_element_...  68.9 us
  transfers between devices with their start and end apart: 21, of which 16 were waited for; matrix products, arithmetic and copies ran while one was open for 18% of the time, Pallas kernels for 0%

profile of v1, /device:TPU:0, one launch (start us, length us, event | category | flops | bytes accessed | tf_op | source)
XLA Modules:
  0.0 1676.0 jit_solution(3775767803881344464)
XLA Ops:
  14.9 11.4 copy.253
  32.7 144.4 %all-gather.6 = f32[32,64,4]{1,2,0:T(4,128)S(1)} all-gather(f32[1,64,4]{1,2,0:T(4,128)S(1)} %convert_bitcast_fusion), channel_id=1, replica_groups=mesh['dp'=4,'expert'=8] {'dp','expert'}, dimensions={0}, use_global_device_ids=true | all-gather | bytes 33792 | tf_op jit(solution)/shard_map/all_gather | solution.py:188
  180.1 63.3 %all-gather.16.cloned.1.call-done = bf16[2048,6144]{1,0:T(8,128)(2,1)} async-done(((bf16[64,6144]{1,0:T(8,128)(2,1)}), bf16[2048,6144]{1,0:T(8,128)(2,1)}) %all-gather.16.cloned.1.call-update) | async-done | bytes 25165840 | tf_op jit(solution)/shard_map/all_gather | solution.py:190
  243.4 10.1 fusion.53
  265.1 56.8 %all-gather.18.cloned.1.call-done = bf16[2048,2048]{1,0:T(8,128)(2,1)} async-done(((bf16[64,2048]{1,0:T(8,128)(2,1)}), bf16[2048,2048]{1,0:T(8,128)(2,1)}) %all-gather.18.cloned.1.call-update) | async-done | bytes 8388624 | tf_op jit(solution)/shard_map/all_gather | solution.py:191
  334.4 39.0 %all-gather.24.cloned.1.call-done = bf16[512,2048]{1,0:T(8,128)(2,1)} async-done(((bf16[128,2048]{1,0:T(8,128)(2,1)}), bf16[512,2048]{1,0:T(8,128)(2,1)}) %all-gather.24.cloned.1.call-update) | async-done | bytes 2097168 | tf_op jit(solution)/shard_map/all_gather | solution.py:75
  374.3 45.3 %all-gather.22.cloned.1.call-done = bf16[4,128,2048]{2,1,0:T(8,128)(2,1)} async-done(((bf16[1,128,2048]{2,1,0:T(8,128)(2,1)}), bf16[4,128,2048]{2,1,0:T(8,128)(2,1)}) %all-gather.22.cloned.1.call-update) | async-done | bytes 2097168 | tf_op jit(solution)/shard_map/all_gather | solution.py:75
  419.9 20.3 %all-gather.20.cloned.1.call-done = bf16[2,2,2048,2,256]{4,2,3,1,0:T(8,128)(2,1)} async-done(((bf16[1,2,2048,2,256]{4,2,3,1,0:T(8,128)(2,1)}), bf16[2,2,2048,2,256]{4,2,3,1,0:T(8,128)(2,1)}) %all-gather.20.cloned.1.call-update) | async-done | bytes 8388624 | tf_op jit(solution)/shard_map/all_gather | solution.py:92
  440.1 16.4 copy.255
  456.5 14.5 reshape.354
  471.0 59.7 %all-gather.26.cloned.1.call-done = bf16[4,512,2048]{2,1,0:T(8,128)(2,1)} async-done(((bf16[4,128,2048]{2,1,0:T(8,128)(2,1)}), bf16[4,512,2048]{2,1,0:T(8,128)(2,1)}) %all-gather.26.cloned.1.call-update) | async-done | bytes 8388624 | tf_op jit(solution)/shard_map/all_gather | solution.py:76
  530.7 24.4 %fusion.54 = f32[2048,2048]{1,0:T(8,128)} fusion(bf16[2048,2048]{1,0:T(8,128)(2,1)} %bitcast.269, bf16[2048,2048]{1,0:T(8,128)(2,1)} %reshape.354), kind=kOutput, calls=%fused_computation.141 | convolution fusion | flops 17179869184 | bytes 33554432 | tf_op jit(solution)/shard_map/dot_general | solution.py:120
  555.0 81.5 %all-gather.30.cloned.1.call-done = bf16[4,512,2048]{2,1,0:T(8,128)(2,1)} async-done(((bf16[4,128,2048]{2,1,0:T(8,128)(2,1)}), bf16[4,512,2048]{2,1,0:T(8,128)(2,1)}) %all-gather.30.cloned.1.call-update) | async-done | bytes 8388624 | tf_op jit(solution)/shard_map/all_gather | solution.py:76
  636.6 21.6 %fusion.6 = (f32[2048,1024]{1,0:T(8,128)}, f32[2048,1024]{1,0:T(8,128)}) fusion(f32[2048,2048]{1,0:T(8,128)} %fusion.54, bf16[2048,2048]{1,0:T(8,128)(2,1)} %bitcast.271, bf16[1024,2048]{1,0:T(8,128)(2,1)} %bitcast.273), kind=kOutput, calls=%fused_computation.13 | convolution fusion | flops 8602517504 | bytes 46137344 | tf_op jit(solution)/shard_map/dot_general | solution.py:63
  658.1 10.6 reshape.363
  676.3 23.9 %reduce-scatter.40.cloned.1.call-done = f32[4,1,16,128]{3,2,0,1:T(8,128)} async-done(((f32[4,4,16,128]{3,2,0,1:T(8,128)}), f32[4,1,16,128]{3,2,0,1:T(8,128)}) %reduce-scatter.40.cloned.1.call-update) | async-done | bytes 32784
  700.5 14.5 reshape.384
  722.7 13.1 all-gather
  749.2 15.0 multiply_convert_fusion.1
  766.1 23.2 %fusion.1 = bf16[4,4,128,2048]{3,2,0,1:T(8,128)(2,1)} fusion(bf16[2048,2048,1,1]{1,0,2,3:T(8,128)(2,1)} %reshape.384, bf16[4,4,128,1024]{3,2,1,0:T(8,128)(2,1)} %bitcast.215, bf16[4,4,128,1024]{3,2,1,0:T(8,128)(2,1)S(1)} %bitcast.214), kind=kOutput, calls=%fused_computation.3 | convolution fusion | flops 17196646400 | bytes 25165824 | tf_op jit(solution)/shard_map/dot_general | solution.py:63
  789.4 14.1 fusion.4
  803.5 69.7 %reduce-scatter.38.cloned.1.call-done = bf16[4,1,128,2048]{3,2,0,1:T(8,128)(2,1)} async-done(((bf16[4,4,128,2048]{3,2,0,1:T(8,128)(2,1)}), bf16[4,1,128,2048]{3,2,0,1:T(8,128)(2,1)}) %reduce-scatter.38.cloned.1.call-update) | async-done | bytes 2097168
  873.3 89.6 %reduce-scatter.36.cloned.1.call-done = bf16[4,1,128,2048]{3,2,0,1:T(8,128)(2,1)} async-done(((bf16[4,4,128,2048]{3,2,0,1:T(8,128)(2,1)}), bf16[4,1,128,2048]{3,2,0,1:T(8,128)(2,1)}) %reduce-scatter.36.cloned.1.call-update) | async-done | bytes 2097168
  971.2 12.3 copy.295
  983.5 23.8 %fusion.55 = bf16[2048,2,2,2,256]{4,0,3,2,1:T(8,128)(2,1)} fusion(bf16[2048,2048,1,1,1]{1,0,4,3,2:T(8,128)(2,1)} %bitcast.270, bf16[2,2,2,256,2048]{4,3,2,1,0:T(8,128)(2,1)} %bitcast.219), kind=kOutput, calls=%fused_computation.142 | convolution fusion | flops 17179869184 | bytes 25165824 | tf_op jit(solution)/shard_map/dot_general | solution.py:59
  1013.9 14.4 fusion.56
  1030.0 24.5 %reduce-scatter.22.cloned.1.call-done = bf16[1,128,2048]{2,1,0:T(8,128)(2,1)} async-done(((bf16[4,128,2048]{2,1,0:T(8,128)(2,1)}), bf16[1,128,2048]{2,1,0:T(8,128)(2,1)}) %reduce-scatter.22.cloned.1.call-update) | async-done | bytes 524304 | tf_op jit(solution)/shard_map/reduce_scatter | solution.py:83
  1082.9 16.9 %multiply_reduce_fusion = (f32[2048]{0:T(1024)S(1)}, f32[128]{0:T(128)S(1)}, f32[128,2048]{1,0:T(8,128)}) fusion(bf16[2,64,2048]{2,1,0:T(8,128)(2,1)} %param.13, f32[128]{0:T(128)S(1)} %copy-done.44, f32[2048]{0:T(1024)S(1)} %bitcast.250, bf16[2048,6144]{1,0:T(8,128)(2,1)} %all-gather.16.cloned.1.call-done, bf16[128,2048]{1,0:T(8,128)(2,1)} %copy.294, ...), kind=kOutput, calls=%fused_computation.48 | convolution fusion | flops 3227777024 | bytes 28328960 | tf_op jit(solution)/shard_map/dot_general | solution.py:63
  1109.5 11.9 fusion.21
  1137.8 91.0 %all-to-all-done.1 = bf16[4,512,2,2,256]{4,1,3,2,0:T(8,128)(2,1)} async-done(((bf16[4,512,2,2,256]{4,1,3,2,0:T(8,128)(2,1)}), bf16[4,512,2,2,256]{4,1,3,2,0:T(8,128)(2,1)}, u32[]{:S(2)}, u32[]{:S(2)}) %all-to-all-start.1) | async-done | bytes 4194336 | tf_op jit(solution)/shard_map/all_to_all | solution.py:107
  1257.4 161.5 %reduce-scatter.30.cloned.1.call-done = bf16[64,2048]{1,0:T(8,128)(2,1)} async-done(((bf16[2048,2048]{1,0:T(8,128)(2,1)}), bf16[64,2048]{1,0:T(8,128)(2,1)}) %reduce-scatter.30.cloned.1.call-update) | async-done | bytes 262160 | tf_op jit(solution)/shard_map/reduce_scatter | solution.py:280
  1420.7 246.0 %reduce-scatter.28.cloned.1.call-done = bf16[64,6144]{1,0:T(8,128)(2,1)} async-done(((bf16[2048,6144]{1,0:T(8,128)(2,1)}), bf16[64,6144]{1,0:T(8,128)(2,1)}) %reduce-scatter.28.cloned.1.call-update) | async-done | bytes 786448 | tf_op jit(solution)/shard_map/reduce_scatter | solution.py:279
  (234 shorter events, 176.3 us)
Async XLA Ops:
  7.2 236.3 %all-gather.16.cloned.1.call-start = ((), (), s32[]{:S(2)}) async-start(), calls=%async_computation.12 | async-start | bytes 25952256 | tf_op jit(solution)/shard_map/all_gather | solution.py:190
  7.9 314.0 %all-gather.18.cloned.1.call-start = ((), (), s32[]{:S(2)}) async-start(), calls=%async_computation.13 | async-start | bytes 8650752 | tf_op jit(solution)/shard_map/all_gather | solution.py:191
  14.9 162.3 %copy-start.7 = (bf16[2,64,2048]{2,1,0:T(8,128)(2,1)S(1)}, bf16[2,64,2048]{2,1,0:T(8,128)(2,1)}, u32[]{:S(2)}) copy-start(bf16[2,64,2048]{2,1,0:T(8,128)(2,1)} %param.13) | copy-start | bytes 1572868
  14.9 162.6 %copy-start.42 = (s32[2,1,4]{2,1,0:T(1,128)S(1)}, s32[2,1,4]{2,1,0:T(1,128)}, u32[]{:S(2)}) copy-start(s32[2,1,4]{2,1,0:T(1,128)} %param.14) | copy-start | bytes 100
  26.3 303.1 %all-to-all-start = ((bf16[2,512,2,4,256]{4,2,1,0,3:T(2,128)(2,1)}), bf16[2,512,2,4,256]{4,2,1,0,3:T(2,128)(2,1)}, u32[]{:S(2)}, u32[]{:S(2)}) async-start(bf16[2,512,2,4,256]{4,2,1,0,3:T(2,128)(2,1)} %copy.253), calls=%async_computation | async-start | bytes 8388608 | tf_op jit(solution)/shard_map/all_to_all | solution.py:91
  32.6 340.8 %all-gather.24.cloned.1.call-start = ((), (), s32[]{:S(2)}) async-start(), calls=%async_computation.22 | async-start | bytes 2621440 | tf_op jit(solution)/shard_map/all_gather | solution.py:75
  178.1 83.6 %copy-start.31 = (pred[128,128]{0,1:T(8,128)(4,1)}, pred[128,128]{0,1:T(8,128)(4,1)S(1)}, u32[]{:S(2)}) copy-start(pred[128,128]{0,1:T(8,128)(4,1)S(1)} %fusion.34) | copy-start | bytes 49156
  179.0 76.6 %copy-start.18 = (f32[128,64]{1,0:T(8,128)}, f32[128,64]{1,0:T(8,128)S(1)}, u32[]{:S(2)}) copy-start(f32[128,64]{1,0:T(8,128)S(1)} %get-tuple-element.128) | copy-start | bytes 98308
  179.1 74.7 %copy-start.24 = (f32[1,2048]{1,0:T(1,128)}, f32[1,2048]{1,0:T(1,128)S(1)}, u32[]{:S(2)}) copy-start(f32[1,2048]{1,0:T(1,128)S(1)} %get-tuple-element.123) | copy-start | bytes 24580
  179.1 74.7 %copy-start.26 = (f32[1,2048]{1,0:T(1,128)}, f32[1,2048]{1,0:T(1,128)S(1)}, u32[]{:S(2)}) copy-start(f32[1,2048]{1,0:T(1,128)S(1)} %get-tuple-element.124) | copy-start | bytes 24580
  179.1 147.8 %copy-start.22 = (f32[1,2048]{1,0:T(1,128)}, f32[1,2048]{1,0:T(1,128)S(1)}, u32[]{:S(2)}) copy-start(f32[1,2048]{1,0:T(1,128)S(1)} %get-tuple-element.122) | copy-start | bytes 24580
  261.7 65.1 %copy-start.32 = (f32[16,128]{1,0:T(8,128)}, f32[16,128]{1,0:T(8,128)S(1)}, u32[]{:S(2)}) copy-start(f32[16,128]{1,0:T(8,128)S(1)} %get-tuple-element.129) | copy-start | bytes 24580
  328.8 90.8 %all-gather.22.cloned.1.call-start = ((), (), s32[]{:S(2)}) async-start(), calls=%async_computation.16 | async-start | bytes 2621440 | tf_op jit(solution)/shard_map/all_gather | solution.py:75
  329.4 110.8 %all-gather.20.cloned.1.call-start = ((), (), s32[]{:S(2)}) async-start(), calls=%async_computation.14 | async-start | bytes 12582912 | tf_op jit(solution)/shard_map/all_gather | solution.py:92
  334.3 196.3 %all-gather.26.cloned.1.call-start = ((), (), s32[]{:S(2)}) async-start(), calls=%async_computation.23 | async-start | bytes 10485760 | tf_op jit(solution)/shard_map/all_gather | solution.py:76
  373.5 181.6 %all-gather.28.cloned.1.call-start = ((), (), s32[]{:S(2)}) async-start(), calls=%async_computation.24 | async-start | bytes 6291456 | tf_op jit(solution)/shard_map/all_gather | solution.py:94
  374.2 262.3 %all-gather.30.cloned.1.call-start = ((), (), s32[]{:S(2)}) async-start(), calls=%async_computation.25 | async-start | bytes 10485760 | tf_op jit(solution)/shard_map/all_gather | solution.py:76
  419.6 280.7 %reduce-scatter.40.cloned.1.call-start = ((), (), s32[]{:S(2)}) async-start(), calls=%async_computation.30 | async-start | bytes 163840
  668.7 31.7 %copy-start.39 = (f32[2,64,8]{1,2,0:T(8,128)S(1)}, f32[2,64,8]{1,2,0:T(8,128)}, u32[]{:S(2)}) copy-start(f32[2,64,8]{1,2,0:T(8,128)} %param.16) | copy-start | bytes 12292
  676.3 45.1 %reduce-scatter.26.cloned.1.call-start = ((), (), s32[]{:S(2)}) async-start(), calls=%async_computation.18 | async-start | bytes 40960 | tf_op jit(solution)/shard_map/reduce_scatter | solution.py:83
  700.3 172.9 %reduce-scatter.38.cloned.1.call-start = ((), (), s32[]{:S(2)}) async-start(), calls=%async_computation.29 | async-start | bytes 10485760
  789.4 173.5 %reduce-scatter.36.cloned.1.call-start = ((), (), s32[]{:S(2)}) async-start(), calls=%async_computation.28 | async-start | bytes 10485760
  803.5 225.0 %reduce-scatter.24.cloned.1.call-start = ((), (), s32[]{:S(2)}) async-start(), calls=%async_computation.17 | async-start | bytes 2621440 | tf_op jit(solution)/shard_map/reduce_scatter | solution.py:83
  873.2 181.3 %reduce-scatter.22.cloned.1.call-start = ((), (), s32[]{:S(2)}) async-start(), calls=%async_computation.15 | async-start | bytes 2621440 | tf_op jit(solution)/shard_map/reduce_scatter | solution.py:83
  962.9 159.8 %all-reduce.6.cloned.1.call-start = ((), (), s32[]{:S(2)}) async-start(), calls=%async_computation.27 | async-start | bytes 16777216
  1007.4 126.3 %reduce-scatter.32.cloned.1.call-start = ((), (), s32[]{:S(2)}) async-start(), calls=%async_computation.21 | async-start | bytes 6291456 | tf_op jit(solution)/shard_map/reduce_scatter | solution.py:110
  1013.9 40.6 %copy-start.16 = (bf16[2,64,2048]{2,1,0:T(8,128)(2,1)S(1)}, bf16[2,64,2048]{2,1,0:T(8,128)(2,1)}, u32[]{:S(2)}) copy-start(bf16[2,64,2048]{2,1,0:T(8,128)(2,1)} %param.25) | copy-start | bytes 1572868
  1028.2 39.0 %copy-start.33 = (f32[16,128]{1,0:T(8,128)S(1)}, f32[16,128]{1,0:T(8,128)}, u32[]{:S(2)}) copy-start(f32[16,128]{1,0:T(8,128)} %copy-done.32) | copy-start | bytes 24580
  1028.3 225.7 %reduce-scatter.34.cloned.1.call-start = ((), (), s32[]{:S(2)}) async-start(), calls=%async_computation.26 | async-start | bytes 1081344
  1101.3 317.6 %reduce-scatter.30.cloned.1.call-start = ((), (), s32[]{:S(2)}) async-start(), calls=%async_computation.20 | async-start | bytes 8650752 | tf_op jit(solution)/shard_map/reduce_scatter | solution.py:280
  1108.3 558.4 %reduce-scatter.28.cloned.1.call-start = ((), (), s32[]{:S(2)}) async-start(), calls=%async_computation.19 | async-start | bytes 25952256 | tf_op jit(solution)/shard_map/reduce_scatter | solution.py:279
  1128.1 100.7 %all-to-all-start.1 = ((bf16[4,512,2,2,256]{4,1,3,2,0:T(8,128)(2,1)}), bf16[4,512,2,2,256]{4,1,3,2,0:T(8,128)(2,1)}, u32[]{:S(2)}, u32[]{:S(2)}) async-start(bf16[4,512,2,2,256]{4,1,3,2,0:T(8,128)(2,1)} %copy.274), calls=%async_computation.6 | async-start | bytes 8388608 | tf_op jit(solution)/shard_map/all_to_all | solution.py:107
  (39 other events, 316.5 us)
Sparse Core Ops, SparseCore 0:
  10.9 232.5 all-gather.15
  246.3 75.5 all-gather.17
  328.9 44.4 all-gather.23
  374.9 44.6 all-gather.21
  421.5 18.5 all-gather.19
  441.8 88.7 all-gather.25
  532.2 13.6 all-gather.27
  547.7 88.7 all-gather.29
  676.4 23.8 reduce-scatter.39
  702.4 18.9 reduce-scatter.25
  789.5 83.6 reduce-scatter.37
  876.4 86.3 reduce-scatter.35
  965.1 43.8 reduce-scatter.23
  1011.3 43.1 reduce-scatter.21
  1057.4 38.1 all-reduce.5
  1097.8 13.2 reduce-scatter.31
  1113.3 140.7 reduce-scatter.33
  1256.2 162.6 reduce-scatter.29
  1425.3 241.3 reduce-scatter.27

commit v2 on v1

--- a/solution.py
+++ b/solution.py
@@ -1,6 +1,8 @@
 import jax
 import jax.numpy as jnp
 from jax import lax
+from jax.experimental import pallas as pl
+from jax.experimental.pallas import tpu as pltpu
 from jax.sharding import PartitionSpec as P
 
 HEAD = 128
@@ -159,6 +161,907 @@
     sums, made = lax.scan(one, start, cut)
     made = jax.tree.map(lambda a: a.reshape(total, -1), made)
     return made + (sums[0].astype(narrow), sums[1].astype(narrow))
+
+
+MESH = pl.DeviceIdType.MESH
+HBM = pl.BlockSpec(memory_space=pl.ANY)
+DEPTH = 4
+RING = 4
+
+
+def ring_turn(number):
+    high = lax.div(number, 2)
+    return number + high * (1 - 2 * lax.rem(number, 2))
+
+
+class Here:
+    def __init__(self):
+        number = lax.axis_index("expert")
+        self.z = lax.axis_index("dp")
+        self.core = lax.rem(number, 2)
+        self.chip = lax.div(number, 2)
+        self.q = ring_turn(self.chip)
+
+    def chip_at(self, turn):
+        return ring_turn(lax.rem(self.q + turn + RING, RING))
+
+    def beside(self, turn):
+        return (self.z, 2 * self.chip_at(turn) + self.core)
+
+    def above(self, steps):
+        return (lax.rem(self.z + steps + DEPTH, DEPTH), 2 * self.chip + self.core)
+
+    def sibling(self):
+        return (self.z, 2 * self.chip + 1 - self.core)
+
+    def meet(self):
+        barrier = pltpu.get_barrier_semaphore()
+        others = [self.beside(1), self.beside(-1), self.sibling()]
+        others += [self.above(steps) for steps in range(1, DEPTH)]
+        for other in others:
+            pl.semaphore_signal(barrier, inc=1, device_id=other, device_id_type=MESH)
+        pl.semaphore_wait(barrier, len(others))
+
+
+def remote(source, target, sent, arrived, device):
+    return pltpu.make_async_remote_copy(
+        src_ref=source,
+        dst_ref=target,
+        send_sem=sent,
+        recv_sem=arrived,
+        device_id=device,
+        device_id_type=MESH,
+    )
+
+
+GATHER_SEMS = [
+    pltpu.SemaphoreType.DMA((2, 2, DEPTH - 1)),
+    pltpu.SemaphoreType.DMA((2, DEPTH, 2, 2)),
+    pltpu.SemaphoreType.DMA((2, DEPTH)),
+    pltpu.SemaphoreType.DMA((1,)),
+]
+
+
+class Gather:
+    def __init__(self, here, source, whole, halves, shared, sems):
+        self.here, self.source, self.whole, self.halves, self.shared = here, source, whole, halves, shared
+        self.line, self.ring, self.pair, self.own = sems
+
+    def block(self, z, turn):
+        chip = self.here.chip_at(turn)
+        return self.whole.at[z, chip, self.here.core] if self.shared else self.whole.at[z, chip]
+
+    def keep(self):
+        return pltpu.make_async_copy(self.source, self.block(self.here.z, 0), self.own.at[0])
+
+    def along(self, step, way, first):
+        z = self.here.z - step + 1 if way == 0 else self.here.z + step - 1
+        block = self.block(z, 0)
+        return remote(
+            self.source if first else block,
+            block,
+            self.line.at[0, way, step - 1],
+            self.line.at[1, way, step - 1],
+            self.here.above(1 if way == 0 else -1),
+        )
+
+    def round(self, z, way, first=False):
+        turn = 1 if way == 0 else -1
+        block = self.block(z, 0)
+        return remote(
+            self.source if first else block,
+            block,
+            self.ring.at[0, z, way, 0],
+            self.ring.at[1, z, way, 0],
+            self.here.beside(turn),
+        )
+
+    def heard(self, z, way):
+        block = self.block(z, -1 if way == 0 else 1)
+        return remote(
+            block, block, self.ring.at[0, z, way, 0], self.ring.at[1, z, way, 0], self.here.beside(1)
+        )
+
+    def onward(self, z, way, mine):
+        if self.halves[way] is None:
+            return None
+        turn = (-1 if mine else -2) if way == 0 else (1 if mine else 2)
+        block = self.block(z, turn).at[pl.ds(*self.halves[way])]
+        return remote(
+            block,
+            block,
+            self.ring.at[0, z, way, 1],
+            self.ring.at[1, z, way, 1],
+            self.here.beside(1 if way == 0 else -1),
+        )
+
+    def swap(self, z, mine):
+        core = self.here.core if mine else 1 - self.here.core
+        part = self.whole.at[z, :, core]
+        return remote(part, part, self.pair.at[0, z], self.pair.at[1, z], self.here.sibling())
+
+
+def start(copy):
+    if copy is not None:
+        copy.start()
+
+
+def run_gather(here, items, between=()):
+    places = [(0, 0)] + [(step, way) for step in range(1, DEPTH) for way in (0, 1)]
+
+    def when(step, way, body):
+        z = here.z - step if way == 0 else here.z + step
+        if step == 0:
+            body(z)
+        else:
+            pl.when(z >= 0 if way == 0 else z < DEPTH)(lambda: body(z))
+
+    def depart(step, way, item):
+        ahead = here.z + 1 < DEPTH if way == 0 else here.z >= 1
+        pl.when(ahead)(lambda: item.along(step + 1, way, step == 0).start())
+
+    for item in items:
+        item.keep().start()
+        for way in (0, 1):
+            depart(0, way, item)
+        for way in (0, 1):
+            item.round(here.z, way, True).start()
+
+    def second(z):
+        for item in items:
+            for way in (0, 1):
+                item.heard(z, way).wait_recv()
+                start(item.onward(z, way, True))
+
+    def third(z):
+        for item in items:
+            for way in (0, 1):
+                copy = item.onward(z, way, False)
+                if copy is not None:
+                    copy.wait_recv()
+            if item.shared:
+                item.swap(z, True).start()
+
+    for step in range(1, DEPTH):
+        for way in (0, 1):
+
+            def first(z, step=step, way=way):
+                for item in items:
+                    block = item.block(z, 0)
+                    remote(
+                        block, block, item.line.at[0, way, step - 1], item.line.at[1, way, step - 1], here.above(1)
+                    ).wait_recv()
+                    if step + 1 < DEPTH:
+                        depart(step, way, item)
+                    for side in (0, 1):
+                        item.round(z, side).start()
+
+            when(step, way, first)
+        if step == 1:
+            for item in items:
+                item.keep().wait()
+        if step <= len(between):
+            between[step - 1]()
+        for before, way in places:
+            if before == step - 1:
+                when(before, way, second)
+        for before, way in places:
+            if before == step - 2:
+                when(before, way, third)
+    for before, way in places:
+        if before == DEPTH - 1:
+            when(before, way, second)
+    for late in (DEPTH - 2, DEPTH - 1):
+        for before, way in places:
+            if before == late:
+                when(before, way, third)
+
+    def settle(z):
+        for item in items:
+            for way in (0, 1):
+                item.round(z, way).wait_send()
+                copy = item.onward(z, way, True)
+                if copy is not None:
+                    copy.wait_send()
+            if item.shared:
+                item.swap(z, True).wait_send()
+                item.swap(z, False).wait_recv()
+
+    for step, way in places:
+        when(step, way, settle)
+    for item in items:
+        for step in range(DEPTH - 1):
+            for way in (0, 1):
+
+                def sent(z, step=step, way=way, item=item):
+                    ahead = here.z + 1 < DEPTH if way == 0 else here.z >= 1
+                    pl.when(ahead)(lambda: item.along(step + 1, way, step == 0).wait_send())
+
+                when(step, way, sent)
+
+
+class Recut:
+    def __init__(self, here, source_in, source_out, whole_in, whole_out, sems):
+        self.here, self.source_in, self.source_out = here, source_in, source_out
+        self.whole_in, self.whole_out = whole_in, whole_out
+        self.cut, self.pair, self.down, self.own = sems
+        self.held, self.rows, columns = source_in.shape
+        self.hidden = columns // 2
+        self.part = self.hidden // DEPTH
+
+    def pieces(self, steps, arriving):
+        here, copies = self.here, []
+        mine = lax.rem(here.z + DEPTH - steps, DEPTH) if arriving else here.z
+        away = lax.rem(here.z + steps, DEPTH)
+        for side in range(2):
+            for expert in range(self.held):
+                columns = side * self.held * 2 * self.part + (here.core * self.held + expert) * self.part
+                target = self.whole_in.at[
+                    pl.ds(pl.multiple_of(mine * self.rows, 16), self.rows),
+                    pl.ds(pl.multiple_of(columns, 128), self.part),
+                ]
+                source = self.source_in.at[
+                    expert, :, pl.ds(pl.multiple_of(side * self.hidden + away * self.part, 128), self.part)
+                ]
+                spot = (steps, side * self.held + expert)
+                if steps == 0:
+                    copies.append(pltpu.make_async_copy(source, target, self.own.at[spot[1]]))
+                else:
+                    copies.append(
+                        remote(
+                            target if arriving else source,
+                            target,
+                            self.cut.at[(0,) + spot],
+                            self.cut.at[(1,) + spot],
+                            here.above(steps),
+                        )
+                    )
+        return copies
+
+    def across(self, steps, mine):
+        here, copies = self.here, []
+        core = here.core if mine else 1 - here.core
+        row = lax.rem(here.z + DEPTH - steps, DEPTH)
+        width = self.held * self.part
+        for side in range(2):
+            spot = self.whole_in.at[
+                pl.ds(pl.multiple_of(row * self.rows, 16), self.rows),
+                pl.ds(pl.multiple_of(side * 2 * width + core * width, 128), width),
+            ]
+            copies.append(
+                remote(spot, spot, self.pair.at[0, steps, side], self.pair.at[1, steps, side], here.sibling())
+            )
+        return copies
+
+    def lower(self, mine):
+        here = self.here
+        core = here.core if mine else 1 - here.core
+        spot = self.whole_out.at[pl.ds(core * self.held, self.held)]
+        return remote(
+            self.source_out if mine else spot, spot, self.down.at[0], self.down.at[1], here.sibling()
+        )
+
+    def lower_own(self):
+        return pltpu.make_async_copy(
+            self.source_out, self.whole_out.at[pl.ds(self.here.core * self.held, self.held)], self.own.at[4]
+        )
+
+    def begin(self):
+        for copy in self.pieces(0, False):
+            copy.start()
+        self.lower_own().start()
+        self.lower(True).start()
+        for steps in range(1, DEPTH):
+            for copy in self.pieces(steps, False):
+                copy.start()
+
+    def relay(self):
+        for steps in range(DEPTH):
+            for copy in self.pieces(steps, True):
+                copy.wait() if steps == 0 else copy.wait_recv()
+            for copy in self.across(steps, True):
+                copy.start()
+
+    def end(self):
+        self.lower_own().wait()
+        self.lower(True).wait_send()
+        self.lower(False).wait_recv()
+        for steps in range(DEPTH):
+            if steps:
+                for copy in self.pieces(steps, False):
+                    copy.wait_send()
+            for copy in self.across(steps, True):
+                copy.wait_send()
+            for copy in self.across(steps, False):
+                copy.wait_recv()
+
+
+RECUT_SEMS = [
+    pltpu.SemaphoreType.DMA((2, DEPTH, 4)),
+    pltpu.SemaphoreType.DMA((2, DEPTH, 2)),
+    pltpu.SemaphoreType.DMA((2,)),
+    pltpu.SemaphoreType.DMA((5,)),
+]
+
+
+def halves_of(rows, split=True):
+    return ((0, rows // 2), (rows // 2, rows - rows // 2)) if split else ((0, rows), None)
+
+
+def first_gather_kernel(wq, wo, up, small, ein, eout, wq_all, wo_all, up_all, small_all, win, wout, *sems):
+    here = Here()
+    here.meet()
+    items = []
+    for number, (source, whole, halves, shared) in enumerate(
+        (
+            (small, small_all, halves_of(small.shape[0], False), True),
+            (wq, wq_all, halves_of(wq.shape[0]), True),
+            (wo, wo_all, halves_of(wo.shape[0]), True),
+            (up, up_all, halves_of(up.shape[0]), False),
+        )
+    ):
+        items.append(Gather(here, source, whole, halves, shared, sems[4 * number : 4 * number + 4]))
+    recut = Recut(here, ein, eout, win, wout, sems[16:20])
+    run_gather(here, items, (recut.begin,))
+    recut.relay()
+    recut.end()
+
+
+def first_gather(wq, wo, up, small, ein, eout):
+    def whole(array, shared):
+        lead = (DEPTH, RING, 2) if shared else (DEPTH, RING)
+        return jax.ShapeDtypeStruct(lead + array.shape, array.dtype)
+
+    held, rows, columns = ein.shape
+    return pl.pallas_call(
+        first_gather_kernel,
+        out_shape=(
+            whole(wq, True),
+            whole(wo, True),
+            whole(up, False),
+            whole(small, True),
+            jax.ShapeDtypeStruct((DEPTH * rows, columns), ein.dtype),
+            jax.ShapeDtypeStruct((2 * held,) + eout.shape[1:], eout.dtype),
+        ),
+        in_specs=[HBM] * 6,
+        out_specs=(HBM,) * 6,
+        scratch_shapes=GATHER_SEMS * 4 + RECUT_SEMS,
+        compiler_params=pltpu.CompilerParams(collective_id=1, has_side_effects=True),
+        name="bring",
+    )(wq, wo, up, small, ein, eout)
+
+
+def row_gather_kernel(rows, whole, *sems):
+    here = Here()
+    here.meet()
+    run_gather(here, [Gather(here, rows, whole, halves_of(rows.shape[0]), False, sems)])
+
+
+def row_gather(rows):
+    return pl.pallas_call(
+        row_gather_kernel,
+        out_shape=jax.ShapeDtypeStruct((DEPTH, RING) + rows.shape, rows.dtype),
+        in_specs=[HBM],
+        out_specs=HBM,
+        scratch_shapes=GATHER_SEMS,
+        compiler_params=pltpu.CompilerParams(collective_id=2, has_side_effects=True),
+        name="spread",
+    )(rows)
+
+
+def add_up(target, terms, rows, columns):
+    high = 16 if rows % 16 == 0 else 8
+    wide = min(columns, 1024)
+    across = columns // wide
+
+    def piece(number, carry):
+        row = pl.multiple_of(lax.div(number, across) * high, high)
+        column = pl.multiple_of(lax.rem(number, across) * wide, 128)
+        spot = (pl.ds(row, high), pl.ds(column, wide))
+        total = terms[0][spot].astype(single)
+        for term in terms[1:]:
+            total = total + term[spot].astype(single)
+        target[spot] = total.astype(target.dtype)
+        return carry
+
+    lax.fori_loop(0, (rows // high) * across, piece, 0)
+
+
+SUM_SEMS = [
+    pltpu.SemaphoreType.DMA((2, DEPTH, 2)),
+    pltpu.SemaphoreType.DMA((2, DEPTH, 2)),
+    pltpu.SemaphoreType.DMA((2, 2, DEPTH)),
+    pltpu.SemaphoreType.DMA((DEPTH, RING, 2)),
+]
+
+
+def sum_scratch(rows, columns, kind, halves, paired):
+    high = max(size for _, size in filter(None, halves))
+    kept = RING if paired else RING - 1
+    made = [
+        pltpu.VMEM((DEPTH, kept, rows, columns), kind),
+        pltpu.VMEM((DEPTH, 2, high, columns), kind),
+        pltpu.VMEM((DEPTH, 2, rows, columns), kind),
+        pltpu.VMEM((2, DEPTH, rows, columns), kind),
+    ] + SUM_SEMS
+    if paired:
+        made += [pltpu.VMEM((DEPTH, RING, rows, columns), kind), pltpu.SemaphoreType.DMA((2, DEPTH, 2))]
+    return made
+
+
+class Sum:
+    def __init__(self, here, sources, target, halves, paired, scratch):
+        self.here, self.sources, self.target, self.halves, self.paired = here, sources, target, halves, paired
+        self.mine, self.half, self.full, self.column = scratch[:4]
+        self.half_sem, self.full_sem, self.line_sem, self.load_sem = scratch[4:8]
+        if paired:
+            self.other, self.pair_sem = scratch[8:10]
+        self.rows, self.columns = self.mine.shape[2:]
+
+    def kept(self, z, turn):
+        return self.mine.at[z, turn if self.paired else {0: 0, 1: 1, 3: 2}[turn]]
+
+    def raw(self, part, z, turn):
+        chip = self.here.chip_at(turn)
+        return part.at[z, chip, self.here.core] if self.paired else part.at[z, chip]
+
+    def spots(self):
+        at, made = 0, []
+        for part in self.sources:
+            made.append((part, pl.ds(at, part.shape[-1])))
+            at += part.shape[-1]
+        return made
+
+    def loads(self, z, turn):
+        return [
+            pltpu.make_async_copy(
+                self.raw(part, z, turn), self.kept(z, turn).at[:, spot], self.load_sem.at[z, turn, number]
+            )
+            for number, (part, spot) in enumerate(self.spots())
+        ]
+
+    def swaps(self, z, mine):
+        return [
+            remote(
+                part.at[z, :, 1 - self.here.core] if mine else self.other.at[z, :, :, spot],
+                self.other.at[z, :, :, spot],
+                self.pair_sem.at[0, z, number],
+                self.pair_sem.at[1, z, number],
+                self.here.sibling(),
+            )
+            for number, (part, spot) in enumerate(self.spots())
+        ]
+
+    def toss(self, z, way):
+        if self.halves[way] is None:
+            return None
+        rows = pl.ds(*self.halves[way])
+        source = (self.kept(z, 2) if self.paired else self.raw(self.sources[0], z, 2)).at[rows]
+        return remote(
+            source,
+            self.half.at[z, way, pl.ds(0, self.halves[way][1])],
+            self.half_sem.at[0, z, way],
+            self.half_sem.at[1, z, way],
+            self.here.beside(1 if way == 0 else -1),
+        )
+
+    def pass_on(self, z, way):
+        return remote(
+            self.kept(z, 1 if way == 0 else 3),
+            self.full.at[z, way],
+            self.full_sem.at[0, z, way],
+            self.full_sem.at[1, z, way],
+            self.here.beside(1 if way == 0 else -1),
+        )
+
+    def climb(self, z, way, up):
+        return remote(
+            self.kept(z, 0),
+            self.column.at[way, z],
+            self.line_sem.at[0, way, z],
+            self.line_sem.at[1, way, z],
+            self.here.above(2 * up - 1),
+        )
+
+    def begin(self, z):
+        if self.paired:
+            for copy in self.swaps(z, True):
+                copy.start()
+        for turn in (2, 1, 3, 0):
+            if turn != 2 or self.paired:
+                for copy in self.loads(z, turn):
+                    copy.start()
+        if not self.paired:
+            for way in (0, 1):
+                start(self.toss(z, way))
+
+    def merge(self, z):
+        if not self.paired:
+            return
+        for copy in self.swaps(z, False):
+            copy.wait_recv()
+        for turn in (2, 1, 3, 0):
+            for copy in self.loads(z, turn):
+                copy.wait()
+            kept = self.kept(z, turn)
+            add_up(kept, [kept, self.other.at[z, self.here.chip_at(turn)]], self.rows, self.columns)
+            if turn == 2:
+                for way in (0, 1):
+                    start(self.toss(z, way))
+
+    def second(self, z):
+        for way, turn in ((0, 1), (1, 3)):
+            if not self.paired:
+                for copy in self.loads(z, turn):
+                    copy.wait()
+            copy = self.toss(z, way)
+            if copy is not None:
+                copy.wait_recv()
+                begin, size = self.halves[way]
+                rows = self.kept(z, turn).at[pl.ds(begin, size)]
+                add_up(rows, [rows, self.half.at[z, way, pl.ds(0, size)]], size, self.columns)
+            self.pass_on(z, way).start()
+
+    def third(self, z, last):
+        here = self.here
+        if not self.paired:
+            for copy in self.loads(z, 0):
+                copy.wait()
+        for way in (0, 1):
+            self.pass_on(z, way).wait_recv()
+        kept = self.kept(z, 0)
+        terms = [kept, self.full.at[z, 0], self.full.at[z, 1]]
+        if last:
+            below, above = self.column.at[0, z], self.column.at[1, z]
+
+            @pl.when(here.z == 0)
+            def _():
+                self.climb(z, 1, 0).wait_recv()
+                add_up(self.target, terms + [above], self.rows, self.columns)
+
+            @pl.when(here.z == DEPTH - 1)
+            def _():
+                self.climb(z, 0, 0).wait_recv()
+                add_up(self.target, terms + [below], self.rows, self.columns)
+
+            @pl.when((here.z > 0) & (here.z < DEPTH - 1))
+            def _():
+                for way in (0, 1):
+                    self.climb(z, way, 0).wait_recv()
+                add_up(self.target, terms + [below, above], self.rows, self.columns)
+
+            return
+        up = (z > here.z).astype(jnp.int32)
+        way = 1 - up
+        follows = up * here.z + way * (DEPTH - 1 - here.z)
+
+        @pl.when(follows > 0)
+        def _():
+            self.climb(z, way, up).wait_recv()
+            add_up(kept, terms + [self.column.at[way, z]], self.rows, self.columns)
+
+        @pl.when(follows == 0)
+        def _():
+            add_up(kept, terms, self.rows, self.columns)
+
+        self.climb(z, way, up).start()
+
+    def end(self, z, last):
+        if self.paired:
+            for copy in self.swaps(z, True):
+                copy.wait_send()
+        for way in (0, 1):
+            copy = self.toss(z, way)
+            if copy is not None:
+                copy.wait_send()
+            self.pass_on(z, way).wait_send()
+        if not last:
+            up = (z > self.here.z).astype(jnp.int32)
+            self.climb(z, 1 - up, up).wait_send()
+
+
+def far_first(here, number):
+    high = lax.div(here.z, 2)
+    inner = lax.rem(lax.div(here.z + 1, 2), 2)
+    low = (DEPTH - 1 - number) + inner * (0, -2, 1, 1)[number]
+    return low + high * (DEPTH - 1 - 2 * low)
+
+
+def run_sum(here, items, before=None, between=None):
+    order = [far_first(here, number) for number in range(DEPTH)]
+    for z in order:
+        for item in items:
+            item.begin(z)
+    if before is not None:
+        before()
+    for item in items:
+        item.merge(order[0])
+    for number, z in enumerate(order):
+        for item in items:
+            item.second(z)
+        if number + 1 < DEPTH:
+            for item in items:
+                item.merge(order[number + 1])
+        if number == 0 and between is not None:
+            between()
+        if number:
+            for item in items:
+                item.third(order[number - 1], False)
+    for item in items:
+        item.third(order[-1], True)
+    for number, z in enumerate(order):
+        for item in items:
+            item.end(z, number == DEPTH - 1)
+
+
+class Share:
+    def __init__(self, here, source, target, sems, held):
+        self.here, self.source, self.target, self.sems, self.held = here, source, target, sems, held
+        self.rows = target.shape[1]
+        self.part = source.shape[1] // held
+
+    def pieces(self, steps, arriving):
+        here = self.here
+        origin = lax.rem(here.z + DEPTH - steps, DEPTH) if arriving else here.z
+        away = lax.rem(here.z + steps, DEPTH)
+        copies = []
+        for expert in range(self.held):
+            target = self.target.at[expert, :, pl.ds(pl.multiple_of(origin * self.part, 128), self.part)]
+            source = self.source.at[
+                pl.ds(pl.multiple_of(away * self.rows, 16), self.rows), pl.ds(expert * self.part, self.part)
+            ]
+            if steps == 0:
+                copies.append(pltpu.make_async_copy(source, target, self.sems.at[0, 0, expert]))
+            else:
+                copies.append(
+                    remote(
+                        target if arriving else source,
+                        target,
+                        self.sems.at[0, steps, expert],
+                        self.sems.at[1, steps, expert],
+                        here.above(steps),
+                    )
+                )
+        return copies
+
+    def begin(self):
+        for steps in range(DEPTH):
+            for copy in self.pieces(steps, False):
+                copy.start()
+
+    def end(self):
+        for steps in range(DEPTH):
+            for copy in self.pieces(steps, False):
+                copy.wait() if steps == 0 else copy.wait_send()
+            if steps:
+                for copy in self.pieces(steps, True):
+                    copy.wait_recv()
+
+
+def row_sum_kernel(
+    out, mid, gate, gin, gdown, out_sum, mid_sum, gate_sum, gate_half, up_half, down_sum, *scratch
+):
+    here = Here()
+    here.meet()
+    rows, slots = out.shape[2], gate.shape[2]
+    items = [
+        Sum(here, [mid], mid_sum, halves_of(rows), False, scratch[0:8]),
+        Sum(here, [out], out_sum, halves_of(rows), False, scratch[8:16]),
+        Sum(here, [gate], gate_sum, halves_of(slots, False), False, scratch[16:24]),
+    ]
+    other_in, other_down, own_in, own_down, sems, loads, share_sems = scratch[24:31]
+    width = own_in.shape[2]
+    tall = own_down.shape[0]
+    swaps, kept = [], []
+    for side in range(2):
+        for core, into in ((1 - here.core, swaps), (here.core, kept)):
+            source = gin.at[:, pl.ds(pl.multiple_of(side * 2 * width + core * width, 128), width)]
+            into.append((source, side))
+    copies = [
+        remote(source, other_in.at[side], sems.at[0, side], sems.at[1, side], here.sibling())
+        for source, side in swaps
+    ]
+    copies.append(
+        remote(
+            gdown.at[pl.ds(pl.multiple_of((1 - here.core) * tall, 16), tall)],
+            other_down,
+            sems.at[0, 2],
+            sems.at[1, 2],
+            here.sibling(),
+        )
+    )
+    fetched = [pltpu.make_async_copy(source, own_in.at[side], loads.at[side]) for source, side in kept]
+    fetched.append(
+        pltpu.make_async_copy(
+            gdown.at[pl.ds(pl.multiple_of(here.core * tall, 16), tall)], own_down, loads.at[2]
+        )
+    )
+    held = 2
+    share = Share(here, own_in.at[0], gate_half, share_sems, held)
+
+    def before():
+        for copy in copies + fetched:
+            copy.start()
+
+    def between():
+        for side in range(2):
+            copies[side].wait_recv()
+            fetched[side].wait()
+            target = own_in.at[0] if side == 0 else up_half
+            add_up(target, [own_in.at[side], other_in.at[side]], own_in.shape[1], width)
+            if side == 0:
+                share.begin()
+        copies[2].wait_recv()
+        fetched[2].wait()
+        add_up(down_sum, [own_down, other_down], tall, own_down.shape[1])
+
+    run_sum(here, items, before, between)
+    share.end()
+    for copy in copies:
+        copy.wait_send()
+
+
+def row_sum(out, mid, gate, gin, gdown, held):
+    rows, columns = out.shape[2:]
+    slots = gate.shape[2]
+    deep, wide = gin.shape
+    width = wide // 4
+    tall = gdown.shape[0] // 2
+    vmem = pl.BlockSpec(memory_space=pltpu.VMEM)
+    return pl.pallas_call(
+        row_sum_kernel,
+        out_shape=(
+            jax.ShapeDtypeStruct((rows, columns), single),
+            jax.ShapeDtypeStruct((rows, columns), single),
+            jax.ShapeDtypeStruct(gate.shape[2:], single),
+            jax.ShapeDtypeStruct((held, deep // DEPTH, wide // 2), narrow),
+            jax.ShapeDtypeStruct((deep, width), narrow),
+            jax.ShapeDtypeStruct((tall, columns), single),
+        ),
+        in_specs=[HBM] * 5,
+        out_specs=(vmem, vmem, vmem, HBM, vmem, vmem),
+        scratch_shapes=sum_scratch(rows, columns, narrow, halves_of(rows), False) * 2
+        + sum_scratch(slots, gate.shape[3], single, halves_of(slots, False), False)
+        + [
+            pltpu.VMEM((2, deep, width), narrow),
+            pltpu.VMEM((tall, columns), narrow),
+            pltpu.VMEM((2, deep, width), narrow),
+            pltpu.VMEM((tall, columns), narrow),
+            pltpu.SemaphoreType.DMA((2, 3)),
+            pltpu.SemaphoreType.DMA((3,)),
+            pltpu.SemaphoreType.DMA((2, DEPTH, 2)),
+        ],
+        compiler_params=pltpu.CompilerParams(
+            collective_id=3, has_side_effects=True, vmem_limit_bytes=62 * 2**20
+        ),
+        name="collect",
+    )(out, mid, gate, gin, gdown)
+
+
+def last_sum_kernel(gq, go, small, up_half, q_sum, small_sum, up_share, *scratch):
+    here = Here()
+    here.meet()
+    rows = gq.shape[3]
+    items = [
+        Sum(here, [gq, go], q_sum, halves_of(rows), True, scratch[0:10]),
+        Sum(here, [small], small_sum, halves_of(small.shape[3], False), True, scratch[10:20]),
+    ]
+    share = Share(here, up_half, up_share, scratch[20], 2)
+    run_sum(here, items, share.begin)
+    share.end()
+
+
+def last_sum(gq, go, small, up_half, held):
+    rows = gq.shape[3]
+    columns = gq.shape[4] + go.shape[4]
+    vmem = pl.BlockSpec(memory_space=pltpu.VMEM)
+    deep, width = up_half.shape
+    return pl.pallas_call(
+        last_sum_kernel,
+        out_shape=(
+            jax.ShapeDtypeStruct((rows, columns), single),
+            jax.ShapeDtypeStruct(small.shape[3:], single),
+            jax.ShapeDtypeStruct((held, deep // DEPTH, DEPTH * width // held), narrow),
+        ),
+        in_specs=[HBM] * 4,
+        out_specs=(vmem, vmem, HBM),
+        scratch_shapes=sum_scratch(rows, columns, narrow, halves_of(rows), True)
+        + sum_scratch(small.shape[3], small.shape[4], single, halves_of(small.shape[3], False), True)
+        + [pltpu.SemaphoreType.DMA((2, DEPTH, 2))],
+        compiler_params=pltpu.CompilerParams(
+            collective_id=4, has_side_effects=True, vmem_limit_bytes=62 * 2**20
+        ),
+        name="deliver",
+    )(gq, go, small, up_half)
+
+
+def by_kernels():
+    return lax.axis_size("dp") == DEPTH and lax.axis_size("expert") == 2 * RING
+
+
+def bring_all(w_qkv, w_out, upstream, dense, gain_rows, expert_in, expert_out):
+    width = upstream.shape[1]
+    share = gain_rows.shape[1]
+    if by_kernels():
+        experts, rows = dense.shape[1], dense.shape[0]
+        small = jnp.concatenate([dense.T, jnp.pad(gain_rows, ((0, 4), (0, rows - share)))], axis=0)
+        wq, wo, up, all_small, weight_in, weight_down = first_gather(
+            w_qkv, w_out, upstream, small, expert_in, expert_out
+        )
+        gains = all_small[:, :, :, experts : experts + 4, :share].transpose(3, 0, 1, 2, 4).reshape(4, -1)
+        core = lax.rem(lax.axis_index("expert"), 2)
+        every_gate = lax.dynamic_index_in_dim(all_small, core, axis=2, keepdims=False)[:, :, :experts]
+        return (
+            wq.reshape(-1, w_qkv.shape[1]),
+            wo.reshape(-1, w_out.shape[1]),
+            up.reshape(-1, width),
+            every_gate,
+            gains,
+            weight_in,
+            weight_down.reshape(-1, width),
+        )
+    everyone = ("dp", "expert")
+    weight_in, weight_down = fetch_weights(expert_in, expert_out)
+    return (
+        lax.all_gather(w_qkv, everyone, axis=0, tiled=True),
+        lax.all_gather(w_out, everyone, axis=0, tiled=True),
+        gather_alike(upstream).reshape(-1, width),
+        gather_alike(dense.T),
+        lax.all_gather(gain_rows, everyone, axis=1, tiled=True),
+        weight_in,
+        weight_down,
+    )
+
+
+def spread_rows(block):
+    every = row_gather(block) if by_kernels() else gather_alike(block)
+    return every.reshape(-1, block.shape[1])
+
+
+def collect_all(out, mid, gate, grad_in, grad_down, held):
+    if by_kernels():
+        return row_sum(out, mid, gate, grad_in, grad_down, held)
+    return (
+        scatter_alike(out).astype(single),
+        scatter_alike(mid).astype(single),
+        scatter_alike(gate),
+        grad_in,
+        grad_down,
+    )
+
+
+def deliver_all(pieces, grad_qkv, grad_out, half_way, held):
+    owners = lax.axis_size("dp") * lax.axis_size("expert")
+    share = pieces.shape[1] // owners
+    if by_kernels():
+        gate_half, up_half, down = half_way
+        lead = (DEPTH, RING, 2)
+        small = pieces.reshape(4, owners, share).transpose(1, 0, 2)
+        small = jnp.pad(small, ((0, 0), (0, 4), (0, 128 - share))).reshape(lead + (8, 128))
+        shares, gains, up_share = last_sum(
+            grad_qkv.reshape(lead + (-1,) + grad_qkv.shape[1:]),
+            grad_out.reshape(lead + (-1,) + grad_out.shape[1:]),
+            small,
+            up_half,
+            held,
+        )
+        wide = grad_qkv.shape[1]
+        return (
+            gains[:4, :share],
+            shares[:, :wide],
+            shares[:, wide:],
+            jnp.concatenate([gate_half, up_share], axis=2).astype(single),
+            down.reshape(held, -1, down.shape[1]),
+        )
+    everyone = ("dp", "expert")
+    share_in, share_down = return_weights(*half_way, held)
+    return (
+        lax.psum_scatter(pieces, everyone, scatter_dimension=1, tiled=True),
+        lax.psum_scatter(grad_qkv, everyone, scatter_dimension=0, tiled=True).astype(single),
+        lax.psum_scatter(grad_out, everyone, scatter_dimension=0, tiled=True).astype(single),
+        share_in.astype(single),
+        share_down.astype(single),
+    )
 
 
 def local(
@@ -183,20 +1086,17 @@
     held = expert_in.shape[0]
     experts = owners * held
     chip_experts = 2 * held
-    everyone = ("dp", "expert")
-    gain_rows = jnp.stack([attn_gain, q_gain, k_gain, ffn_gain]).astype(single)
-    gains = lax.all_gather(gain_rows, everyone, axis=1, tiled=True)
-    gain_attn, gain_query, gain_key, gain_ffn = gains[0], gains[1], gains[2], gains[3]
-    weight_qkv = lax.all_gather(w_qkv, everyone, axis=0, tiled=True)
-    weight_out = lax.all_gather(w_out, everyone, axis=0, tiled=True)
-    weight_in, weight_down = fetch_weights(expert_in, expert_out)
-
     inputs = tokens.reshape(rows, model_width).astype(single)
     upstream = out_grad.reshape(rows, model_width)
     ids = expert_ids.reshape(rows, -1)
     gate_rows = gates.reshape(rows, -1)
     onehot = (ids[:, :, None] == jnp.arange(experts, dtype=jnp.int32)).astype(single)
     dense = jnp.sum(onehot * gate_rows[:, :, None], axis=1)
+    gain_rows = jnp.stack([attn_gain, q_gain, k_gain, ffn_gain]).astype(single)
+    weight_qkv, weight_out, up_rows, every_gate, gains, weight_in, weight_down = bring_all(
+        w_qkv, w_out, upstream, dense, gain_rows, expert_in, expert_out
+    )
+    gain_attn, gain_query, gain_key, gain_ffn = gains[0], gains[1], gains[2], gains[3]
 
     normal_in, factor_in = normalize(inputs)
     normed_in = (normal_in * gain_attn).astype(narrow)
@@ -226,9 +1126,7 @@
     routed_in = (normal_mid * gain_ffn).astype(narrow)
 
     chip = lax.axis_index("expert") // 2
-    up_rows = gather_alike(upstream).reshape(-1, model_width)
-    mid_rows = gather_alike(routed_in).reshape(-1, model_width)
-    every_gate = gather_alike(dense.T)
+    mid_rows = spread_rows(routed_in)
     mine = lax.dynamic_slice_in_dim(every_gate, chip * chip_experts, chip_experts, axis=2)
     gate = mine.transpose(0, 1, 3, 2).reshape(-1, chip_experts)
     piece_out, piece_mid, piece_gates, grad_in_part, grad_down_part = expert_rounds(
@@ -236,12 +1134,18 @@
     )
 
     chips = owners // 2
-    mixture = scatter_alike(piece_out.reshape(depth, chips, rows, model_width)).astype(single)
-    grad_routed = scatter_alike(piece_mid.reshape(depth, chips, rows, model_width)).astype(single)
     by_gate = piece_gates.reshape(depth, chips, rows, chip_experts).transpose(0, 1, 3, 2)
     spread = jnp.zeros((depth, chips, experts, rows), single)
     spread = lax.dynamic_update_slice_in_dim(spread, by_gate, chip * chip_experts, axis=2)
-    gate_table = scatter_alike(spread).T
+    mixture, grad_routed, gate_table, *half_way = collect_all(
+        piece_out.reshape(depth, chips, rows, model_width),
+        piece_mid.reshape(depth, chips, rows, model_width),
+        spread,
+        grad_in_part,
+        grad_down_part,
+        held,
+    )
+    gate_table = gate_table.T
     grad_gates = jnp.sum(onehot * gate_table[:, None, :], axis=2)
     results = (middle + mixture).astype(narrow)
 
@@ -275,23 +1179,22 @@
     grad_tokens = grad_middle + grad_input
 
     pieces = jnp.stack([piece_attn, piece_query, piece_key, piece_ffn])
-    gain_sums = lax.psum_scatter(pieces, everyone, scatter_dimension=1, tiled=True)
-    grad_qkv_share = lax.psum_scatter(grad_qkv_part, everyone, scatter_dimension=0, tiled=True)
-    grad_out_share = lax.psum_scatter(grad_out_part, everyone, scatter_dimension=0, tiled=True)
-    share_in, share_down = return_weights(grad_in_part, grad_down_part, held)
+    gain_sums, grad_qkv_share, grad_out_share, share_in, share_down = deliver_all(
+        pieces, grad_qkv_part, grad_out_part, half_way, held
+    )
     shape = (micro_count, seq_len, model_width)
     return (
         results.reshape(shape),
         grad_tokens.reshape(shape),
         grad_gates.reshape(expert_ids.shape),
         gain_sums[0],
-        grad_qkv_share.astype(single),
+        grad_qkv_share,
         gain_sums[1],
         gain_sums[2],
-        grad_out_share.astype(single),
+        grad_out_share,
         gain_sums[3],
-        share_in.astype(single),
-        share_down.astype(single),
+        share_in,
+        share_down,
     )
 
 

time: 1690 us -> 882 us (0.52)
  waiting for transfers between devices: 1080 us -> 0 us
  Pallas kernels: 0 us -> 618 us
  blocking collectives: 166 us -> 0 us
  local copies, waits for them, and re-layouts: 143 us -> 28.2 us
  other arithmetic: 63.1 us -> 35.1 us
    pallas_call x0 -> x4, Pallas kernels: none -> 618 us  [the longest x1 242 us: first_gather(): pl.pallas_call(first_gather_kernel, out_shape=(whole(wq, True), whole(wo,...]
    reduce_scatter x6 -> x0, waiting for transfers between devices: 438 us -> none  [the longest x1 246 us: local(): lax.psum_scatter(grad_qkv_part, everyone, scatter_dimension=0, tiled=True)]
    all_gather x8 -> x0, waiting for transfers between devices: 366 us -> none  [the longest x2 141 us: gather_alike(): lax.all_gather(column, 'expert', axis=1, axis_index_groups=core_groups())]
    unnamed x24 -> x0, waiting for transfers between devices: 187 us -> none
    all_gather x3 -> x0, blocking collectives: 166 us -> none  [the longest x1 144 us: local(): gains = lax.all_gather(gain_rows, everyone, axis=1, tiled=True)]
    all_to_all x2 -> x0, waiting for transfers between devices: 91 us -> none  [the longest x1 91 us: return_weights(): turned = lax.all_to_all(own, 'dp', split_axis=0, concat_axis=0)]
    reshape x4 -> x0, local copies, waits for them, and re-layouts: 50.9 us -> none  [the longest x2 28.9 us: fetch_weights(): both.transpose(2, 3, 0, 1, 4).reshape(depth * rows, 4 * held * part)]
    unnamed x116 -> x98, local copies, waits for them, and re-layouts: 32.4 us -> 9.29 us
  transfers between devices with their start and end apart: 21 -> 0, of which waited for: 16 -> 0; matrix products, arithmetic and copies ran while one was open for 18% -> 0% of each run, Pallas kernels for 0% -> 0%
where the time goes in v2:
time: 882 us; the launch traced here: 873 us
  Pallas kernels  618 us (70%)
  matrix products  191 us (22%)
  other arithmetic  35.1 us (4%)
  local copies, waits for them, and re-layouts  28.2 us (3%)
    pallas_call x1, Pallas kernels, first_gather(): pl.pallas_call(first_gather_kernel, out_shape=(whole(wq, True), whole(wo,...  242 us
    pallas_call x1, Pallas kernels, last_sum(): pl.pallas_call(last_sum_kernel, out_shape=(jax.ShapeDtypeStruct((rows, co...  158 us
    pallas_call x1, Pallas kernels, row_sum(): pl.pallas_call(row_sum_kernel, out_shape=(jax.ShapeDtypeStruct((rows, col...  145 us
    pallas_call x1, Pallas kernels, row_gather(): pl.pallas_call(row_gather_kernel, out_shape=jax.ShapeDtypeStruct((DEPTH,...  73 us
    dot_general x4, matrix products, contract_last(): lax.dot_general(left, right, (((1,), (1,)), ((), ())), preferred_element_...  68.2 us
    dot_general x4, matrix products, contract_rows(): lax.dot_general(left, right, (((0,), (0,)), ((), ())), preferred_element_...  55.5 us
    dot_general x1, matrix products, expert_round(): gate_up = jnp.dot(mid_rows, weight_in, preferred_element_type=single)  24.6 us

profile of v2, /device:TPU:0, one launch (start us, length us, event | category | flops | bytes accessed | tf_op | source)
XLA Modules:
  0.0 873.5 jit_solution(8252016448527331692)
XLA Ops:
  3.6 242.1 %bring.1 = (bf16[4,4,2,64,6144]{4,3,2,1,0:T(8,128)(2,1)}, bf16[4,4,2,64,2048]{4,3,2,1,0:T(8,128)(2,1)}, bf16[4,4,128,2048]{3,2,1,0:T(8,128)(2,1)}, f32[4,4,2,24,...) custom-call(bf16[64,6144]{1,0:T(8,128)(2,1)} %wq.1, bf16[64,2048]{1,0:T(8,128)(2,1)} %wo.1, ...), custom_call_target="tpu_custom_call" | custom-call | tf_op jit(solution)/shard_map/bring/pallas_call | solution.py:516
  247.7 10.0 %fusion.60 = f32[128,6144]{1,0:T(8,128)S(1)} fusion(bf16[128,2048]{1,0:T(8,128)(2,1)S(1)} %bitcast.194, bf16[2048,6144]{1,0:T(8,128)(2,1)} %bitcast.178), kind=kOutput, calls=%fused_computation.161 | convolution fusion | flops 3221225472 | bytes 28835840 | tf_op jit(solution)/shard_map/dot_general | solution.py:1103
  258.6 1.6 fusion.58
  260.4 1.6 fusion.57
  264.1 4.9 subtract_convert_fusion.1
  269.1 3.3 fusion.59
  272.5 3.3 convolution_convert_fusion.2
  275.8 4.9 multiply_reduce_fusion.7
  281.9 73.0 %spread.1 = bf16[4,4,128,2048]{3,2,1,0:T(8,128)(2,1)} custom-call(bf16[128,2048]{1,0:T(8,128)(2,1)} %multiply_convert_fusion.6.rows), custom_call_target="tpu_custom_call" | custom-call | tf_op jit(solution)/shard_map/spread/pallas_call | solution.py:541
  354.9 24.6 %fusion.61 = f32[2048,2048]{0,1:T(8,128)} fusion(bf16[2048,2048]{1,0:T(8,128)(2,1)} %bitcast.183, bf16[2048,2048]{1,0:T(8,128)(2,1)} %get-tuple-element.29), kind=kOutput, calls=%fused_computation.162 | convolution fusion | flops 17179869184 | bytes 33554432 | tf_op jit(solution)/shard_map/dot_general | solution.py:122
  379.5 23.5 %multiply_convert_fusion.1 = (bf16[2048,1024]{0,1:T(8,128)(2,1)}, bf16[2048,1024]{0,1:T(8,128)(2,1)}, bf16[2048,1024]{0,1:T(8,128)(2,1)}, f32[2048,1024]{0,1:T(8,128)}) fusion(f32[2048,2048]{0,1:T(8,128)} %fusion.61, f32[2048,4]{0,1:T(4,128)S(1)} %bitcast.205, bf16[2048,2048]{1,0:T(8,128)(2,1)} %bitcast.186, bf16[1024,2048]{1,0:T(8,128)(2,1)} %bitcast.192), kind=kOutput, calls=%fused_computation.7 | convolution fusion | flops 8625586176 | bytes 50364416 | tf_op jit(solution)/shard_map/dot_general | solution.py:65
  403.1 14.4 %fusion.63.gdown = bf16[1024,2048]{1,0:T(8,128)(2,1)} fusion(bf16[2048,1024]{0,1:T(8,128)(2,1)} %get-tuple-element.83, bf16[2048,2048]{1,0:T(8,128)(2,1)} %bitcast.187), kind=kOutput, calls=%fused_computation.164 | convolution fusion | flops 8589934592 | bytes 16777216 | tf_op jit(solution)/shard_map/dot_general | solution.py:61
  417.5 22.6 %fusion.3.gin = bf16[2048,2048]{1,0:T(8,128)(2,1)} fusion(bf16[2048,2048]{1,0:T(8,128)(2,1)} %bitcast.184, bf16[2048,1024]{0,1:T(8,128)(2,1)} %get-tuple-element.82, bf16[2048,1024]{0,1:T(8,128)(2,1)S(1)} %copy-done.9), kind=kOutput, calls=%fused_computation.11 | convolution fusion | flops 17196646400 | bytes 25165824 | tf_op jit(solution)/shard_map/dot_general | solution.py:61
  440.1 7.4 bitcast_reduce_fusion
  447.5 22.8 %fusion.4 = bf16[2048,2048]{1,0:T(8,128)(2,1)} fusion(bf16[2048,2048]{1,0:T(8,128)(2,1)} %get-tuple-element.29, bf16[2048,1024]{0,1:T(8,128)(2,1)} %get-tuple-element.82, bf16[2048,1024]{0,1:T(8,128)(2,1)S(1)} %copy-done.9), kind=kOutput, calls=%fused_computation.12 | convolution fusion | flops 17196646400 | bytes 25165824 | tf_op jit(solution)/shard_map/dot_general | solution.py:65
  470.4 6.4 copy.111
  476.8 13.9 %fusion.62.out = bf16[4,4,128,2048]{3,2,1,0:T(8,128)(2,1)} fusion(bf16[4,4,128,1024]{3,2,1,0:T(8,128)(2,1)} %bitcast.191, bf16[1024,2048,1,1]{1,0,3,2:T(8,128)(2,1)} %bitcast.193), kind=kOutput, calls=%fused_computation.163 | convolution fusion | flops 8589934592 | bytes 16777216 | tf_op jit(solution)/shard_map/dot_general | solution.py:131
  490.7 145.0 %collect.1 = (f32[128,2048]{1,0:T(8,128)}, f32[128,2048]{1,0:T(8,128)}, f32[16,128]{1,0:T(8,128)}, bf16[2,512,1024]{2,1,0:T(8,128)(2,1)}, bf16[2048,512]{1,0:T(8,128)(2,1)}, /*index=5*/f32[512,2048]{1,0:T(8,128)}) custom-call(bf16[4,4,128,2048]{3,2,1,0:T(8,128)(2,1)} %fusion.62.out, bf16[4,4,128,2048]{3,2,1,0:T(8,128)(2,1)} %bitcast.182, ...), custom_call_target="tpu_custom_call" | custom-call | tf_op jit(solution)/shard_map/collect/pallas_call | solution.py:911
  635.7 1.6 multiply_reduce_fusion
  637.3 3.3 multiply_add_fusion.3
  641.6 7.1 convolution_convert_fusion
  648.7 2.1 copy.117
  650.7 1.8 multiply_reduce_fusion.5
  654.0 1.7 fusion.10
  658.2 1.9 multiply_convert_fusion.4
  660.1 2.8 convolution_convert_fusion.1
  663.3 14.8 %multiply_reduce_fusion.1 = (f32[2048]{0:T(1024)S(1)}, f32[128]{0:T(128)S(1)}, bf16[128,2048]{1,0:T(8,128)(2,1)}, f32[128,2048]{1,0:T(8,128)}) fusion(bf16[2,64,2048]{2,1,0:T(8,128)(2,1)} %param.13, f32[128]{0:T(128)S(1)} %rsqrt.40, f32[2048]{0:T(1024)S(1)} %copy-done.27, bf16[2048,6144]{1,0:T(8,128)(2,1)} %bitcast.179, bf16[128,2048]{1,0:T(8,128)(2,1)S(1)} %copy.112, ...), kind=kOutput, calls=%fused_computation.41 | convolution fusion | flops 3228301312 | bytes 28853248 | tf_op jit(solution)/shard_map/dot_general | solution.py:65
  679.1 5.7 fusion.20.go
  686.2 12.8 %fusion.6.gq = bf16[4,4,2,64,6144]{4,3,2,1,0:T(8,128)(2,1)} fusion(bf16[4,4,2,64,128]{4,3,2,1,0:T(8,128)(2,1)S(1)} %bitcast.196, bf16[128,2048]{1,0:T(8,128)(2,1)S(1)} %copy.112, bf16[128,2048]{1,0:T(8,128)(2,1)} %get-tuple-element.85, bf16[128,2048]{1,0:T(8,128)(2,1)S(1)} %copy-done.13), kind=kOutput, calls=%fused_computation.18 | convolution fusion | flops 3225944064 | bytes 27262976 | tf_op jit(solution)/shard_map/dot_general | solution.py:61
  699.0 157.8 %deliver.1 = (f32[64,8192]{1,0:T(8,128)}, f32[8,128]{1,0:T(8,128)}, bf16[2,512,1024]{2,1,0:T(8,128)(2,1)}) custom-call(bf16[4,4,2,64,6144]{4,3,2,1,0:T(8,128)(2,1)} %fusion.6.gq, bf16[4,4,2,64,2048]{4,3,2,1,0:T(8,128)(2,1)} %fusion.20.go, f32[4,4,2,8,128]{4,3,2,1,0:T(8,128)} %bitcast.198, bf16[2048,512]{1,0:T(8,128)(2,1)} %get-tuple-element.35.up_half), custom_call_target="tpu_custom_call" | custom-call | tf_op jit(solution)/shard_map/deliver/pallas_call | solution.py:959
  856.9 6.8 maximum_convert_fusion
  868.3 4.7 copy.149
  (156 shorter events, 21.6 us)
Async XLA Ops:
  0.6 246.3 %copy-start.6 = (bf16[2,64,2048]{2,1,0:T(8,128)(2,1)S(1)}, bf16[2,64,2048]{2,1,0:T(8,128)(2,1)}, u32[]{:S(2)}) copy-start(bf16[2,64,2048]{2,1,0:T(8,128)(2,1)} %param.13) | copy-start | bytes 1572868
  1.5 245.3 %copy-start.28 = (s32[128,8]{0,1:T(8,128)}, s32[128,8]{0,1:T(8,128)S(1)}, u32[]{:S(2)}) copy-start(s32[128,8]{0,1:T(8,128)S(1)} %eq.32) | copy-start | bytes 12292
  257.7 14.8 %copy-start = (f32[128,6144]{1,0:T(8,128)}, f32[128,6144]{1,0:T(8,128)S(1)}, u32[]{:S(2)}) copy-start(f32[128,6144]{1,0:T(8,128)S(1)} %fusion.60) | copy-start | bytes 9437188
  269.1 11.6 %copy-start.30 = (pred[128,128]{0,1:T(8,128)(4,1)}, pred[128,128]{0,1:T(8,128)(4,1)S(1)}, u32[]{:S(2)}) copy-start(pred[128,128]{0,1:T(8,128)(4,1)S(1)} %fusion.28) | copy-start | bytes 49156
  272.5 8.3 copy-start.31
  280.8 98.7 %copy-start.4 = (f32[128,2048]{1,0:T(8,128)}, f32[128,2048]{1,0:T(8,128)S(1)}, u32[]{:S(2)}) copy-start(f32[128,2048]{1,0:T(8,128)S(1)} %get-tuple-element.117) | copy-start | bytes 3145732
  280.8 74.1 %copy-start.38 = (f32[128]{0:T(128)}, f32[128]{0:T(128)S(1)}, u32[]{:S(2)}) copy-start(f32[128]{0:T(128)S(1)} %add_rsqrt_fusion.1) | copy-start | bytes 1540
  280.9 74.0 %copy-start.20 = (f32[2048]{0:T(1024)}, f32[2048]{0:T(1024)S(1)}, u32[]{:S(2)}) copy-start(f32[2048]{0:T(1024)S(1)} %mul.463) | copy-start | bytes 24580
  354.9 24.6 %copy-start.19 = (f32[4,4,2,24,128]{4,3,2,1,0:T(8,128)S(1)}, f32[4,4,2,24,128]{4,3,2,1,0:T(8,128)}, u32[]{:S(2)}) copy-start(f32[4,4,2,24,128]{4,3,2,1,0:T(8,128)} %get-tuple-element.26) | copy-start | bytes 1179652
  403.1 14.4 %copy-start.9 = (bf16[2048,1024]{0,1:T(8,128)(2,1)S(1)}, bf16[2048,1024]{0,1:T(8,128)(2,1)}, u32[]{:S(2)}) copy-start(bf16[2048,1024]{0,1:T(8,128)(2,1)} %get-tuple-element.81) | copy-start | bytes 12582916
  403.1 37.0 %slice-start = ((s8[8388608]{0:T(1024)(128)(4,1)}), s8[4194304]{0:T(1024)(128)(4,1)S(1)}, s32[]{:S(2)}) async-start(s8[8388608]{0:T(1024)(128)(4,1)} %bitcast.176), calls=%async_computation | async-start | bytes 8388608
  417.5 22.6 %slice-start.1 = ((s8[8388608]{0:T(1024)(128)(4,1)}), s8[4194304]{0:T(1024)(128)(4,1)S(1)}, s32[]{:S(2)}) async-start(s8[8388608]{0:T(1024)(128)(4,1)} %bitcast.176), calls=%async_computation.1 | async-start | bytes 8388608
  447.5 22.8 %copy-start.17 = (f32[4,4,16,128]{3,2,1,0:T(8,128)}, f32[4,4,16,128]{3,2,1,0:T(8,128)S(1)}, u32[]{:S(2)}) copy-start(f32[4,4,16,128]{3,2,1,0:T(8,128)S(1)} %constant_dynamic-update-slice_fusion.gate) | copy-start | bytes 393220
  490.7 145.0 %copy-start.5 = (f32[128,2048]{1,0:T(8,128)S(1)}, f32[128,2048]{1,0:T(8,128)}, u32[]{:S(2)}) copy-start(f32[128,2048]{1,0:T(8,128)} %copy-done.4) | copy-start | bytes 3145732
  490.7 145.0 %copy-start.21 = (f32[2048]{0:T(1024)S(1)}, f32[2048]{0:T(1024)}, u32[]{:S(2)}) copy-start(f32[2048]{0:T(1024)} %copy-done.20) | copy-start | bytes 24580
  490.7 145.0 %copy-start.39 = (f32[128]{0:T(128)S(1)}, f32[128]{0:T(128)}, u32[]{:S(2)}) copy-start(f32[128]{0:T(128)} %copy-done.38) | copy-start | bytes 1540
  637.3 13.5 %copy-start.1 = (f32[128,6144]{1,0:T(8,128)S(1)}, f32[128,6144]{1,0:T(8,128)}, u32[]{:S(2)}) copy-start(f32[128,6144]{1,0:T(8,128)} %copy-done) | copy-start | bytes 9437188
  637.3 13.5 %copy-start.32 = (f32[16,128]{1,0:T(8,128)S(1)}, f32[16,128]{1,0:T(8,128)}, u32[]{:S(2)}) copy-start(f32[16,128]{1,0:T(8,128)} %copy-done.31) | copy-start | bytes 24580
  648.7 7.6 copy-start.16
  648.7 7.6 copy-start.18
  650.7 5.0 copy-start.10
  650.7 5.0 copy-start.11
  658.2 5.0 copy-start.27
  663.3 15.9 %copy-start.3 = (f32[128,2048]{1,0:T(8,128)S(1)}, f32[128,2048]{1,0:T(8,128)}, u32[]{:S(2)}) copy-start(f32[128,2048]{1,0:T(8,128)} %copy-done.2) | copy-start | bytes 3145732
  663.3 15.9 %copy-start.8 = (bf16[16,128,128]{2,1,0:T(8,128)(2,1)S(1)}, bf16[16,128,128]{2,1,0:T(8,128)(2,1)}, u32[]{:S(2)}) copy-start(bf16[16,128,128]{2,1,0:T(8,128)(2,1)} %convolution_convert_fusion.2) | copy-start | bytes 1572868
  678.0 8.1 copy-start.13
  856.8 6.8 copy-start.12
  856.8 8.9 %copy-start.43 = (f32[8,128]{1,0:T(8,128)S(1)}, f32[8,128]{1,0:T(8,128)}, u32[]{:S(2)}) copy-start(f32[8,128]{1,0:T(8,128)} %get-tuple-element.36) | copy-start | bytes 12292
  856.9 9.4 %copy-start.7 = (bf16[2,64,2048]{2,1,0:T(8,128)(2,1)S(1)}, bf16[2,64,2048]{2,1,0:T(8,128)(2,1)}, u32[]{:S(2)}) copy-start(bf16[2,64,2048]{2,1,0:T(8,128)(2,1)} %param.13) | copy-start | bytes 1572868
  856.9 9.4 %copy-start.14 = (f32[128,2048]{1,0:T(8,128)S(1)}, f32[128,2048]{1,0:T(8,128)}, u32[]{:S(2)}) copy-start(f32[128,2048]{1,0:T(8,128)} %get-tuple-element.121) | copy-start | bytes 3145732
  856.9 10.7 %copy-start.29 = (s32[128,8]{0,1:T(8,128)S(1)}, s32[128,8]{0,1:T(8,128)}, u32[]{:S(2)}) copy-start(s32[128,8]{0,1:T(8,128)} %copy-done.28) | copy-start | bytes 12292
  856.9 10.7 %copy-start.37 = (f32[16,128]{1,0:T(8,128)S(1)}, f32[16,128]{1,0:T(8,128)}, u32[]{:S(2)}) copy-start(f32[16,128]{1,0:T(8,128)} %get-tuple-element.34) | copy-start | bytes 24580
  (14 other events, 46.8 us)

commit v3 on v2

--- a/solution.py
+++ b/solution.py
@@ -286,98 +286,98 @@
         copy.start()
 
 
-def run_gather(here, items, between=()):
-    places = [(0, 0)] + [(step, way) for step in range(1, DEPTH) for way in (0, 1)]
-
-    def when(step, way, body):
-        z = here.z - step if way == 0 else here.z + step
-        if step == 0:
-            body(z)
-        else:
-            pl.when(z >= 0 if way == 0 else z < DEPTH)(lambda: body(z))
-
-    def depart(step, way, item):
+def gather_third(item, z):
+    for way in (0, 1):
+        copy = item.onward(z, way, False)
+        if copy is not None:
+            copy.wait_recv()
+
+
+class Rounds:
+    def __init__(self, here, items):
+        self.here, self.items = here, items
+        for item in items:
+            item.keep().start()
+            for way in (0, 1):
+                self.depart(0, way, item)
+            for way in (0, 1):
+                item.round(here.z, way, True).start()
+
+    def depart(self, step, way, item):
+        here = self.here
         ahead = here.z + 1 < DEPTH if way == 0 else here.z >= 1
         pl.when(ahead)(lambda: item.along(step + 1, way, step == 0).start())
 
-    for item in items:
-        item.keep().start()
-        for way in (0, 1):
-            depart(0, way, item)
-        for way in (0, 1):
-            item.round(here.z, way, True).start()
-
-    def second(z):
-        for item in items:
-            for way in (0, 1):
-                item.heard(z, way).wait_recv()
-                start(item.onward(z, way, True))
-
-    def third(z):
-        for item in items:
-            for way in (0, 1):
-                copy = item.onward(z, way, False)
-                if copy is not None:
-                    copy.wait_recv()
-            if item.shared:
-                item.swap(z, True).start()
-
-    for step in range(1, DEPTH):
-        for way in (0, 1):
-
-            def first(z, step=step, way=way):
-                for item in items:
-                    block = item.block(z, 0)
-                    remote(
-                        block, block, item.line.at[0, way, step - 1], item.line.at[1, way, step - 1], here.above(1)
-                    ).wait_recv()
-                    if step + 1 < DEPTH:
-                        depart(step, way, item)
-                    for side in (0, 1):
-                        item.round(z, side).start()
-
-            when(step, way, first)
-        if step == 1:
+    def places(self, step, body):
+        here = self.here
+        if step == 0:
+            body(here.z, 0)
+            return
+        pl.when(here.z >= step)(lambda: body(here.z - step, 0))
+        pl.when(here.z + step < DEPTH)(lambda: body(here.z + step, 1))
+
+    def service(self, step):
+        items, here = self.items, self.here
+
+        def first(z, way):
+            for item in items:
+                block = item.block(z, 0)
+                remote(
+                    block, block, item.line.at[0, way, step], item.line.at[1, way, step], here.above(1)
+                ).wait_recv()
+                if step + 2 < DEPTH:
+                    self.depart(step + 1, way, item)
+                for side in (0, 1):
+                    item.round(z, side).start()
+
+        def second(z, way):
+            for item in items:
+                for side in (0, 1):
+                    item.heard(z, side).wait_recv()
+                    start(item.onward(z, side, True))
+
+        if step + 1 < DEPTH:
+            self.places(step + 1, first)
+        if step == 0:
             for item in items:
                 item.keep().wait()
-        if step <= len(between):
-            between[step - 1]()
-        for before, way in places:
-            if before == step - 1:
-                when(before, way, second)
-        for before, way in places:
-            if before == step - 2:
-                when(before, way, third)
-    for before, way in places:
-        if before == DEPTH - 1:
-            when(before, way, second)
-    for late in (DEPTH - 2, DEPTH - 1):
-        for before, way in places:
-            if before == late:
-                when(before, way, third)
-
-    def settle(z):
-        for item in items:
-            for way in (0, 1):
-                item.round(z, way).wait_send()
-                copy = item.onward(z, way, True)
-                if copy is not None:
-                    copy.wait_send()
-            if item.shared:
-                item.swap(z, True).wait_send()
-                item.swap(z, False).wait_recv()
-
-    for step, way in places:
-        when(step, way, settle)
-    for item in items:
-        for step in range(DEPTH - 1):
-            for way in (0, 1):
-
-                def sent(z, step=step, way=way, item=item):
-                    ahead = here.z + 1 < DEPTH if way == 0 else here.z >= 1
-                    pl.when(ahead)(lambda: item.along(step + 1, way, step == 0).wait_send())
-
-                when(step, way, sent)
+        self.places(step, second)
+
+    def third(self, step):
+        def body(z, way):
+            for item in self.items:
+                gather_third(item, z)
+                if item.shared:
+                    item.swap(z, True).start()
+
+        self.places(step, body)
+
+    def finish(self):
+        def settle(z, way):
+            for item in self.items:
+                for side in (0, 1):
+                    item.round(z, side).wait_send()
+                    copy = item.onward(z, side, True)
+                    if copy is not None:
+                        copy.wait_send()
+                if item.shared:
+                    item.swap(z, True).wait_send()
+                    item.swap(z, False).wait_recv()
+
+        for step in range(DEPTH):
+            self.places(step, settle)
+        here = self.here
+        for item in self.items:
+            for step in range(DEPTH - 1):
+                for way in (0, 1):
+
+                    def sent(z, side, step=step, way=way, item=item):
+                        if step and side != way:
+                            return
+                        ahead = here.z + 1 < DEPTH if way == 0 else here.z >= 1
+                        pl.when(ahead)(lambda: item.along(step + 1, way, step == 0).wait_send())
+
+                    self.places(step, sent)
 
 
 class Recut:
@@ -502,8 +502,16 @@
     ):
         items.append(Gather(here, source, whole, halves, shared, sems[4 * number : 4 * number + 4]))
     recut = Recut(here, ein, eout, win, wout, sems[16:20])
-    run_gather(here, items, (recut.begin,))
+    rounds = Rounds(here, items)
+    for step in range(DEPTH):
+        rounds.service(step)
+        if step == 0:
+            recut.begin()
+        else:
+            rounds.third(step - 1)
+    rounds.third(DEPTH - 1)
     recut.relay()
+    rounds.finish()
     recut.end()
 
 
@@ -530,25 +538,6 @@
         name="bring",
     )(wq, wo, up, small, ein, eout)
 
-
-def row_gather_kernel(rows, whole, *sems):
-    here = Here()
-    here.meet()
-    run_gather(here, [Gather(here, rows, whole, halves_of(rows.shape[0]), False, sems)])
-
-
-def row_gather(rows):
-    return pl.pallas_call(
-        row_gather_kernel,
-        out_shape=jax.ShapeDtypeStruct((DEPTH, RING) + rows.shape, rows.dtype),
-        in_specs=[HBM],
-        out_specs=HBM,
-        scratch_shapes=GATHER_SEMS,
-        compiler_params=pltpu.CompilerParams(collective_id=2, has_side_effects=True),
-        name="spread",
-    )(rows)
-
-
 def add_up(target, terms, rows, columns):
     high = 16 if rows % 16 == 0 else 8
     wide = min(columns, 1024)
@@ -575,18 +564,18 @@
 ]
 
 
-def sum_scratch(rows, columns, kind, halves, paired):
+def sum_scratch(rows, columns, kind, halves, paired=False, made=False):
     high = max(size for _, size in filter(None, halves))
-    kept = RING if paired else RING - 1
-    made = [
+    kept = RING if paired or made else RING - 1
+    scratch = [
         pltpu.VMEM((DEPTH, kept, rows, columns), kind),
         pltpu.VMEM((DEPTH, 2, high, columns), kind),
         pltpu.VMEM((DEPTH, 2, rows, columns), kind),
-        pltpu.VMEM((2, DEPTH, rows, columns), kind),
+        pltpu.VMEM((DEPTH + 1, rows, columns), kind),
     ] + SUM_SEMS
     if paired:
-        made += [pltpu.VMEM((DEPTH, RING, rows, columns), kind), pltpu.SemaphoreType.DMA((2, DEPTH, 2))]
-    return made
+        scratch += [pltpu.VMEM((DEPTH, RING, rows, columns), kind), pltpu.SemaphoreType.DMA((2, DEPTH, 2))]
+    return scratch
 
 
 class Sum:
@@ -599,6 +588,8 @@
         self.rows, self.columns = self.mine.shape[2:]
 
     def kept(self, z, turn):
+        if self.sources is None:
+            return self.mine.at[z, self.here.chip_at(turn)]
         return self.mine.at[z, turn if self.paired else {0: 0, 1: 1, 3: 2}[turn]]
 
     def raw(self, part, z, turn):
@@ -606,11 +597,11 @@
         return part.at[z, chip, self.here.core] if self.paired else part.at[z, chip]
 
     def spots(self):
-        at, made = 0, []
-        for part in self.sources:
-            made.append((part, pl.ds(at, part.shape[-1])))
+        at, spots = 0, []
+        for part in self.sources or []:
+            spots.append((part, pl.ds(at, part.shape[-1])))
             at += part.shape[-1]
-        return made
+        return spots
 
     def loads(self, z, turn):
         return [
@@ -636,7 +627,8 @@
         if self.halves[way] is None:
             return None
         rows = pl.ds(*self.halves[way])
-        source = (self.kept(z, 2) if self.paired else self.raw(self.sources[0], z, 2)).at[rows]
+        loaded = self.sources is not None and not self.paired
+        source = (self.raw(self.sources[0], z, 2) if loaded else self.kept(z, 2)).at[rows]
         return remote(
             source,
             self.half.at[z, way, pl.ds(0, self.halves[way][1])],
@@ -654,10 +646,13 @@
             self.here.beside(1 if way == 0 else -1),
         )
 
-    def climb(self, z, way, up):
+    def climb(self, z, way, up, slot=None):
+        if slot is None:
+            down_to_owner = way * (z == self.here.z - 1).astype(jnp.int32)
+            slot = z + down_to_owner * (DEPTH - z)
         return remote(
             self.kept(z, 0),
-            self.column.at[way, z],
+            self.column.at[slot],
             self.line_sem.at[0, way, z],
             self.line_sem.at[1, way, z],
             self.here.above(2 * up - 1),
@@ -712,22 +707,22 @@
         kept = self.kept(z, 0)
         terms = [kept, self.full.at[z, 0], self.full.at[z, 1]]
         if last:
-            below, above = self.column.at[0, z], self.column.at[1, z]
+            below, above = self.column.at[z], self.column.at[DEPTH]
 
             @pl.when(here.z == 0)
             def _():
-                self.climb(z, 1, 0).wait_recv()
+                self.climb(z, 1, 0, DEPTH).wait_recv()
                 add_up(self.target, terms + [above], self.rows, self.columns)
 
             @pl.when(here.z == DEPTH - 1)
             def _():
-                self.climb(z, 0, 0).wait_recv()
+                self.climb(z, 0, 0, z).wait_recv()
                 add_up(self.target, terms + [below], self.rows, self.columns)
 
             @pl.when((here.z > 0) & (here.z < DEPTH - 1))
             def _():
-                for way in (0, 1):
-                    self.climb(z, way, 0).wait_recv()
+                self.climb(z, 0, 0, z).wait_recv()
+                self.climb(z, 1, 0, DEPTH).wait_recv()
                 add_up(self.target, terms + [below, above], self.rows, self.columns)
 
             return
@@ -737,8 +732,8 @@
 
         @pl.when(follows > 0)
         def _():
-            self.climb(z, way, up).wait_recv()
-            add_up(kept, terms + [self.column.at[way, z]], self.rows, self.columns)
+            self.climb(z, way, up, z).wait_recv()
+            add_up(kept, terms + [self.column.at[z]], self.rows, self.columns)
 
         @pl.when(follows == 0)
         def _():
@@ -839,17 +834,12 @@
 
 
 def row_sum_kernel(
-    out, mid, gate, gin, gdown, out_sum, mid_sum, gate_sum, gate_half, up_half, down_sum, *scratch
+    out, gin, gdown, out_sum, gate_half, up_half, down_sum, *scratch
 ):
     here = Here()
     here.meet()
-    rows, slots = out.shape[2], gate.shape[2]
-    items = [
-        Sum(here, [mid], mid_sum, halves_of(rows), False, scratch[0:8]),
-        Sum(here, [out], out_sum, halves_of(rows), False, scratch[8:16]),
-        Sum(here, [gate], gate_sum, halves_of(slots, False), False, scratch[16:24]),
-    ]
-    other_in, other_down, own_in, own_down, sems, loads, share_sems = scratch[24:31]
+    items = [Sum(here, [out], out_sum, halves_of(out.shape[2]), False, scratch[0:8])]
+    other_in, other_down, own_in, own_down, sems, loads, share_sems = scratch[8:15]
     width = own_in.shape[2]
     tall = own_down.shape[0]
     swaps, kept = [], []
@@ -901,9 +891,8 @@
         copy.wait_send()
 
 
-def row_sum(out, mid, gate, gin, gdown, held):
+def row_sum(out, gin, gdown, held):
     rows, columns = out.shape[2:]
-    slots = gate.shape[2]
     deep, wide = gin.shape
     width = wide // 4
     tall = gdown.shape[0] // 2
@@ -912,16 +901,13 @@
         row_sum_kernel,
         out_shape=(
             jax.ShapeDtypeStruct((rows, columns), single),
-            jax.ShapeDtypeStruct((rows, columns), single),
-            jax.ShapeDtypeStruct(gate.shape[2:], single),
             jax.ShapeDtypeStruct((held, deep // DEPTH, wide // 2), narrow),
             jax.ShapeDtypeStruct((deep, width), narrow),
             jax.ShapeDtypeStruct((tall, columns), single),
         ),
-        in_specs=[HBM] * 5,
-        out_specs=(vmem, vmem, vmem, HBM, vmem, vmem),
-        scratch_shapes=sum_scratch(rows, columns, narrow, halves_of(rows), False) * 2
-        + sum_scratch(slots, gate.shape[3], single, halves_of(slots, False), False)
+        in_specs=[HBM] * 3,
+        out_specs=(vmem, HBM, vmem, vmem),
+        scratch_shapes=sum_scratch(rows, columns, narrow, halves_of(rows))
         + [
             pltpu.VMEM((2, deep, width), narrow),
             pltpu.VMEM((tall, columns), narrow),
@@ -935,7 +921,7 @@
             collective_id=3, has_side_effects=True, vmem_limit_bytes=62 * 2**20
         ),
         name="collect",
-    )(out, mid, gate, gin, gdown)
+    )(out, gin, gdown)
 
 
 def last_sum_kernel(gq, go, small, up_half, q_sum, small_sum, up_share, *scratch):
@@ -974,6 +960,247 @@
         name="deliver",
     )(gq, go, small, up_half)
 
+def near_first(here, number):
+    high = lax.div(here.z, 2)
+    inner = lax.rem(lax.div(here.z + 1, 2), 2)
+    low = number + inner * (1, -1, 0, 0)[number]
+    return low + high * (DEPTH - 1 - 2 * low)
+
+
+TILE = 256
+
+
+class Tiles:
+    def __init__(self, stage, sems):
+        self.stage, self.sems = stage, sems
+
+    def run(self, first, last, count, target, make):
+        def store(number):
+            slot = lax.rem(number, 2)
+            rows = pl.ds(pl.multiple_of(number * TILE, TILE), TILE)
+            return pltpu.make_async_copy(self.stage.at[slot], target.at[rows], self.sems.at[slot])
+
+        def body(number, carry):
+            pl.when(number >= 2)(lambda: store(number - 2).wait())
+            make(number, self.stage.at[lax.rem(number, 2)])
+            store(number).start()
+            return carry
+
+        lax.fori_loop(first, last, body, 0)
+        if last == count:
+            for number in (count - 2, count - 1):
+                store(number).wait()
+
+
+def experts_kernel(
+    rows, ups, gates, win, wout, mid_sum, gate_sum, out, gin, gdown, rows_all, *scratch
+):
+    here = Here()
+    here.meet()
+    (
+        w_in, w_out, grads, scaled, row_plane, up_plane, gate_plane, served, strip, stage, loads, strip_sems, stage_sems
+    ) = scratch[:13]
+    gather = Gather(here, rows, rows_all, halves_of(rows.shape[0]), False, scratch[13:17])
+    mids = Sum(here, None, mid_sum, halves_of(rows.shape[0]), False, scratch[17:25])
+    tables = Sum(here, None, gate_sum, halves_of(gate_sum.shape[0], False), False, scratch[25:33])
+    block, width = rows.shape
+    plane = RING * block
+    hidden = w_out.shape[0]
+    chunk = hidden // 4
+    column = lax.broadcasted_iota(jnp.int32, (plane, 128), 1)
+    fetch_in = pltpu.make_async_copy(win, w_in, loads.at[0])
+    fetch_out = pltpu.make_async_copy(wout, w_out, loads.at[1])
+    fetch_in.start()
+    fetch_out.start()
+
+    def fetch_plane(number):
+        z = near_first(here, number)
+        return (
+            pltpu.make_async_copy(ups.at[z], up_plane.at[number % 2], loads.at[2 + number % 2]),
+            pltpu.make_async_copy(gates.at[z], gate_plane.at[number % 2], loads.at[4 + number % 2]),
+        )
+
+    def fetch_rows(number):
+        return pltpu.make_async_copy(rows_all.at[near_first(here, number)], row_plane, loads.at[6])
+
+    def hidden_units(number):
+        z = near_first(here, number)
+        fetch_rows(number).start()
+        for copy in fetch_plane(number):
+            copy.wait()
+        if number == 0:
+            fetch_in.wait()
+            fetch_out.wait()
+        fetch_rows(number).wait()
+        served[...] = jnp.zeros_like(served)
+        at = pl.ds(pl.multiple_of(z * plane, plane), plane)
+
+        def one(expert, carry):
+            mid = row_plane[...].reshape(plane, width)
+            up_rows = up_plane[number % 2]
+            spot = pl.ds(pl.multiple_of(expert * chunk, chunk), chunk)
+            spot_up = pl.ds(pl.multiple_of(hidden + expert * chunk, chunk), chunk)
+            gate = jnp.sum(jnp.where(column == expert, gate_plane[number % 2], 0.0), axis=1, keepdims=True)
+            gate_part = jnp.dot(mid, w_in[:, spot], preferred_element_type=single)
+            up_part = jnp.dot(mid, w_in[:, spot_up], preferred_element_type=single)
+            back = contract_last(up_rows, w_out[spot])
+            sigmoid = 1.0 / (1.0 + jnp.exp(-gate_part))
+            activated = gate_part * sigmoid
+            units = activated * up_part
+            scaled[at, spot] = (gate * units).astype(narrow)
+            total = jnp.sum(units * back, axis=1, keepdims=True)
+            served[...] += jnp.where(column == here.chip * 4 + expert, total, 0.0)
+            grad = gate * back
+            grads[at, spot] = (grad * up_part * (sigmoid * (1.0 + gate_part * (1.0 - sigmoid)))).astype(narrow)
+            grads[at, spot_up] = (grad * activated).astype(narrow)
+            return carry
+
+        lax.fori_loop(0, 4, one, 0)
+        for chip in range(RING):
+            turned = jnp.transpose(served[chip * block : (chip + 1) * block])
+            tables.mine[z, chip] = turned[: tables.rows]
+
+    def row_grads(z):
+        at = pl.ds(pl.multiple_of(z * plane, plane), plane)
+
+        def one(number, carry):
+            spot = pl.ds(pl.multiple_of(number * TILE, TILE), TILE)
+            made = contract_last(grads[at], w_in[spot]).astype(narrow)
+            for chip in range(RING):
+                mids.mine[z, chip, :, spot] = made[chip * block : (chip + 1) * block]
+            return carry
+
+        lax.fori_loop(0, width // TILE, one, 0)
+
+    for copy in fetch_plane(0):
+        copy.start()
+    rounds = Rounds(here, [gather])
+    for number in range(DEPTH):
+        rounds.service(number)
+        gather_third(gather, near_first(here, number))
+        if number + 1 < DEPTH:
+            for copy in fetch_plane(number + 1):
+                copy.start()
+        hidden_units(number)
+
+    tiles = Tiles(stage, stage_sems)
+    strips = width // TILE
+
+    def fetch_strip(number):
+        spot = pl.ds(pl.multiple_of(number * TILE, TILE), TILE)
+        slot = lax.rem(number, 2)
+        return pltpu.make_async_copy(rows_all.at[:, :, :, spot], strip.at[slot], strip_sems.at[slot])
+
+    def columns_of(result, stage, step=512):
+        for begin in range(0, width, step):
+            stage[:, begin : begin + step] = result(begin, step).astype(narrow)
+
+    def grad_in(number, stage):
+        slot = lax.rem(number, 2)
+        fetch_strip(number).wait()
+        pl.when(number + 1 < strips)(lambda: fetch_strip(number + 1).start())
+        left = strip[slot].reshape(DEPTH * plane, TILE)
+        columns_of(lambda begin, step: contract_rows(left, grads[:, begin : begin + step]), stage)
+
+    def outputs(number, stage):
+        at = pl.ds(pl.multiple_of(number * TILE, TILE), TILE)
+        left = scaled[at]
+        columns_of(
+            lambda begin, step: jnp.dot(left, w_out[:, begin : begin + step], preferred_element_type=single),
+            stage,
+        )
+
+    def grad_down(number, stage):
+        at = pl.ds(pl.multiple_of(number * TILE, TILE), TILE)
+        left = scaled[:, at]
+        columns_of(lambda begin, step: contract_rows(left, w_in[:, begin : begin + step]), stage)
+
+    fetch_strip(0).start()
+    order = [far_first(here, number) for number in range(DEPTH)]
+    items = [mids, tables]
+    high = DEPTH * plane // TILE
+    work = [
+        lambda: tiles.run(0, 2, strips, gin, grad_in),
+        lambda: tiles.run(2, 4, strips, gin, grad_in),
+        lambda: tiles.run(4, 6, strips, gin, grad_in),
+        lambda: tiles.run(6, strips, strips, gin, grad_in),
+    ]
+    for number, z in enumerate(order):
+        row_grads(z)
+        for item in items:
+            for way in (0, 1):
+                start(item.toss(z, way))
+        if number:
+            for item in items:
+                item.second(order[number - 1])
+        if number > 1:
+            for item in items:
+                item.third(order[number - 2], False)
+        if number + 1 < DEPTH:
+            work[number]()
+    again = [
+        pltpu.make_async_copy(ups.at[z], w_in.at[pl.ds(z * plane, plane)], loads.at[7 + z]) for z in range(DEPTH)
+    ]
+    for copy in again:
+        copy.start()
+    work[DEPTH - 1]()
+    for item in items:
+        item.second(order[DEPTH - 1])
+        item.third(order[DEPTH - 2], False)
+    tiles.run(0, high, high, out, outputs)
+    for item in items:
+        item.third(order[DEPTH - 1], True)
+    for copy in again:
+        copy.wait()
+    tiles.run(0, hidden // TILE, hidden // TILE, gdown, grad_down)
+    for number, z in enumerate(order):
+        for item in items:
+            item.end(z, number == DEPTH - 1)
+    rounds.finish()
+
+
+def experts_round(rows, ups, gates, win, wout, experts):
+    block, width = rows.shape
+    plane = RING * block
+    hidden = wout.shape[0]
+    total = DEPTH * plane
+    vmem = pl.BlockSpec(memory_space=pltpu.VMEM)
+    return pl.pallas_call(
+        experts_kernel,
+        out_shape=(
+            jax.ShapeDtypeStruct((block, width), single),
+            jax.ShapeDtypeStruct((experts, block), single),
+            jax.ShapeDtypeStruct((total, width), narrow),
+            jax.ShapeDtypeStruct((width, 2 * hidden), narrow),
+            jax.ShapeDtypeStruct((hidden, width), narrow),
+            jax.ShapeDtypeStruct((DEPTH, RING, block, width), narrow),
+        ),
+        in_specs=[HBM] * 5,
+        out_specs=(vmem, vmem) + (HBM,) * 4,
+        scratch_shapes=[
+            pltpu.VMEM((width, 2 * hidden), narrow),
+            pltpu.VMEM((hidden, width), narrow),
+            pltpu.VMEM((total, 2 * hidden), narrow),
+            pltpu.VMEM((total, hidden), narrow),
+            pltpu.VMEM((RING, block, width), narrow),
+            pltpu.VMEM((2, plane, width), narrow),
+            pltpu.VMEM((2, plane, 128), single),
+            pltpu.VMEM((plane, 128), single),
+            pltpu.VMEM((2, DEPTH, RING, block, TILE), narrow),
+            pltpu.VMEM((2, TILE, width), narrow),
+            pltpu.SemaphoreType.DMA((11,)),
+            pltpu.SemaphoreType.DMA((2,)),
+            pltpu.SemaphoreType.DMA((2,)),
+        ]
+        + GATHER_SEMS
+        + sum_scratch(block, width, narrow, halves_of(block), made=True)
+        + sum_scratch(experts, block, single, halves_of(experts, False), made=True),
+        compiler_params=pltpu.CompilerParams(
+            collective_id=2, has_side_effects=True, vmem_limit_bytes=62 * 2**20
+        ),
+        name="experts",
+    )(rows, ups, gates, win, wout)
+
 
 def by_kernels():
     return lax.axis_size("dp") == DEPTH and lax.axis_size("expert") == 2 * RING
@@ -1013,20 +1240,36 @@
     )
 
 
-def spread_rows(block):
-    every = row_gather(block) if by_kernels() else gather_alike(block)
-    return every.reshape(-1, block.shape[1])
-
-
-def collect_all(out, mid, gate, grad_in, grad_down, held):
+def experts_all(routed_in, up_rows, every_gate, weight_in, weight_down, held):
+    depth = lax.axis_size("dp")
+    owners = lax.axis_size("expert")
+    chips = owners // 2
+    experts = owners * held
+    chip_experts = 2 * held
+    rows, width = routed_in.shape
+    chip = lax.axis_index("expert") // 2
+    mine = lax.dynamic_slice_in_dim(every_gate, chip * chip_experts, chip_experts, axis=2)
+    gate = mine.transpose(0, 1, 3, 2)
     if by_kernels():
-        return row_sum(out, mid, gate, grad_in, grad_down, held)
+        gate = jnp.pad(gate.reshape(DEPTH, -1, chip_experts), ((0, 0), (0, 0), (0, 128 - chip_experts)))
+        ups = up_rows.reshape(DEPTH, -1, width)
+        grad_routed, table, out, grad_in, grad_down, _ = experts_round(
+            routed_in, ups, gate, weight_in, weight_down, experts
+        )
+        mixture, *half_way = row_sum(out.reshape(DEPTH, RING, rows, width), grad_in, grad_down, held)
+        return (mixture, grad_routed, table, half_way)
+    mid_rows = gather_alike(routed_in).reshape(-1, width)
+    out, mid, served, grad_in, grad_down = expert_rounds(
+        mid_rows, up_rows, gate.reshape(-1, chip_experts), weight_in, weight_down
+    )
+    by_gate = served.reshape(depth, chips, rows, chip_experts).transpose(0, 1, 3, 2)
+    spread = jnp.zeros((depth, chips, experts, rows), single)
+    spread = lax.dynamic_update_slice_in_dim(spread, by_gate, chip * chip_experts, axis=2)
     return (
-        scatter_alike(out).astype(single),
-        scatter_alike(mid).astype(single),
-        scatter_alike(gate),
-        grad_in,
-        grad_down,
+        scatter_alike(out.reshape(depth, chips, rows, width)).astype(single),
+        scatter_alike(mid.reshape(depth, chips, rows, width)).astype(single),
+        scatter_alike(spread),
+        (grad_in, grad_down),
     )
 
 
@@ -1081,11 +1324,8 @@
 ):
     micro_count, seq_len, model_width = tokens.shape
     rows = micro_count * seq_len
-    depth = lax.axis_size("dp")
-    owners = lax.axis_size("expert")
     held = expert_in.shape[0]
-    experts = owners * held
-    chip_experts = 2 * held
+    experts = lax.axis_size("expert") * held
     inputs = tokens.reshape(rows, model_width).astype(single)
     upstream = out_grad.reshape(rows, model_width)
     ids = expert_ids.reshape(rows, -1)
@@ -1125,28 +1365,10 @@
     normal_mid, factor_mid = normalize(middle)
     routed_in = (normal_mid * gain_ffn).astype(narrow)
 
-    chip = lax.axis_index("expert") // 2
-    mid_rows = spread_rows(routed_in)
-    mine = lax.dynamic_slice_in_dim(every_gate, chip * chip_experts, chip_experts, axis=2)
-    gate = mine.transpose(0, 1, 3, 2).reshape(-1, chip_experts)
-    piece_out, piece_mid, piece_gates, grad_in_part, grad_down_part = expert_rounds(
-        mid_rows, up_rows, gate, weight_in, weight_down
-    )
-
-    chips = owners // 2
-    by_gate = piece_gates.reshape(depth, chips, rows, chip_experts).transpose(0, 1, 3, 2)
-    spread = jnp.zeros((depth, chips, experts, rows), single)
-    spread = lax.dynamic_update_slice_in_dim(spread, by_gate, chip * chip_experts, axis=2)
-    mixture, grad_routed, gate_table, *half_way = collect_all(
-        piece_out.reshape(depth, chips, rows, model_width),
-        piece_mid.reshape(depth, chips, rows, model_width),
-        spread,
-        grad_in_part,
-        grad_down_part,
-        held,
-    )
-    gate_table = gate_table.T
-    grad_gates = jnp.sum(onehot * gate_table[:, None, :], axis=2)
+    mixture, grad_routed, gate_table, half_way = experts_all(
+        routed_in, up_rows, every_gate, weight_in, weight_down, held
+    )
+    grad_gates = jnp.sum(onehot * gate_table.T[:, None, :], axis=2)
     results = (middle + mixture).astype(narrow)
 
     grad_mid, piece_ffn = rms_back(grad_routed, normal_mid, factor_mid, gain_ffn)

time: 882 us -> 817 us (0.926)
  matrix products: 191 us -> 68.4 us
  Pallas kernels: 618 us -> 691 us
  other arithmetic: 35.1 us -> 24.7 us
    pallas_call x1, Pallas kernels: 73 us -> 212 us  [experts_round(): pl.pallas_call(experts_kernel, out_shape=(jax.ShapeDtypeStruct((block, wi...]
    pallas_call x1, Pallas kernels: 145 us -> 86.1 us  [row_sum(): pl.pallas_call(row_sum_kernel, out_shape=(jax.ShapeDtypeStruct((rows, col...]
    dot_general x4 -> x2, matrix products: 68.2 us -> 21.3 us  [contract_last(): lax.dot_general(left, right, (((1,), (1,)), ((), ())), preferred_element_...]
    dot_general x2 -> x0, matrix products: 38.5 us -> none  [the longest x1 24.6 us: expert_round(): gate_up = jnp.dot(mid_rows, weight_in, preferred_element_type=single)]
    dot_general x4 -> x2, matrix products: 55.5 us -> 18.5 us  [contract_rows(): lax.dot_general(left, right, (((0,), (0,)), ((), ())), preferred_element_...]
where the time goes in v3:
time: 817 us; the launch traced here: 806 us
  Pallas kernels  691 us (85%)
  matrix products  68.4 us (8%)
  other arithmetic  24.7 us (3%)
  local copies, waits for them, and re-layouts  21.4 us (3%)
    pallas_call x1, Pallas kernels, first_gather(): pl.pallas_call(first_gather_kernel, out_shape=(whole(wq, True), whole(wo,...  241 us
    pallas_call x1, Pallas kernels, experts_round(): pl.pallas_call(experts_kernel, out_shape=(jax.ShapeDtypeStruct((block, wi...  212 us
    pallas_call x1, Pallas kernels, last_sum(): pl.pallas_call(last_sum_kernel, out_shape=(jax.ShapeDtypeStruct((rows, co...  152 us
    pallas_call x1, Pallas kernels, row_sum(): pl.pallas_call(row_sum_kernel, out_shape=(jax.ShapeDtypeStruct((rows, col...  86.1 us
    dot_general x2, matrix products, contract_last(): lax.dot_general(left, right, (((1,), (1,)), ((), ())), preferred_element_...  21.3 us
    dot_general x2, matrix products, contract_rows(): lax.dot_general(left, right, (((0,), (0,)), ((), ())), preferred_element_...  18.5 us

profile of v3, /device:TPU:0, one launch (start us, length us, event | category | flops | bytes accessed | tf_op | source)
XLA Modules:
  0.0 806.4 jit_solution(3505104016848147110)
XLA Ops:
  2.5 1.2 multiply_reduce_fusion.10
  7.2 240.7 %bring.1 = (bf16[4,4,2,64,6144]{4,3,2,1,0:T(8,128)(2,1)}, bf16[4,4,2,64,2048]{4,3,2,1,0:T(8,128)(2,1)}, bf16[4,4,128,2048]{3,2,1,0:T(8,128)(2,1)}, f32[4,4,2,24,...) custom-call(bf16[64,6144]{1,0:T(8,128)(2,1)} %wq.1, bf16[64,2048]{1,0:T(8,128)(2,1)} %wo.1, ...), custom_call_target="tpu_custom_call" | custom-call | tf_op jit(solution)/shard_map/bring/pallas_call | solution.py:524
  250.4 1.0 multiply_convert_fusion.5
  251.7 1.0 pad.17.gates
  252.8 10.3 %fusion.53 = f32[128,6144]{1,0:T(8,128)S(1)} fusion(bf16[128,2048]{1,0:T(8,128)(2,1)} %bitcast.158, bf16[2048,6144]{1,0:T(8,128)(2,1)} %bitcast.146), kind=kOutput, calls=%fused_computation.145 | convolution fusion | flops 3221225472 | bytes 28835840 | tf_op jit(solution)/shard_map/dot_general | solution.py:1343
  264.7 2.8 subtract_convert_fusion.1
  267.5 3.3 fusion.52
  270.8 3.4 convolution_convert_fusion.2
  274.1 4.9 multiply_reduce_fusion.7
  279.1 1.0 multiply_convert_fusion.4.rows
  280.1 212.2 %experts.1 = (f32[128,2048]{1,0:T(8,128)}, f32[16,128]{1,0:T(8,128)}, bf16[2048,2048]{1,0:T(8,128)(2,1)}, bf16[2048,2048]{1,0:T(8,128)(2,1)}, bf16[1024,2048]{1,...) custom-call(bf16[128,2048]{1,0:T(8,128)(2,1)} %multiply_convert_fusion.4.rows, bf16[4,512,2048]{2,1,0:T(8,128)(2,1)} %bitcast.152, ...), custom_call_target="tpu_custom_call" | custom-call | tf_op jit(solution)/shard_map/experts/pallas_call | solution.py:1168
  493.0 86.1 %collect.1 = (f32[128,2048]{1,0:T(8,128)}, bf16[2,512,1024]{2,1,0:T(8,128)(2,1)}, bf16[2048,512]{1,0:T(8,128)(2,1)}, f32[512,2048]{1,0:T(8,128)}) custom-call(bf16[4,4,128,2048]{3,2,1,0:T(8,128)(2,1)} %bitcast.150, bf16[2048,2048]{1,0:T(8,128)(2,1)} %get-tuple-element.36.gin, bf16[1024,2048]{1,0:T(8,128)(2,1)} %get-tuple-element.37.gdown), custom_call_target="tpu_custom_call" | custom-call | tf_op jit(solution)/shard_map/collect/pallas_call | solution.py:900
  579.8 1.6 multiply_reduce_fusion
  581.3 2.7 multiply_add_fusion.3
  584.0 6.6 convolution_convert_fusion
  590.7 1.1 copy.114
  591.9 3.8 convolution_convert_fusion.1
  595.6 2.1 copy.109
  597.7 1.8 multiply_reduce_fusion.5
  601.4 1.0 multiply_subtract_fusion.1
  603.2 1.9 multiply_convert_fusion.2
  605.1 14.7 %multiply_reduce_fusion.1 = (f32[2048]{0:T(1024)S(1)}, f32[128]{0:T(128)S(1)}, bf16[128,2048]{1,0:T(8,128)(2,1)}, f32[128,2048]{1,0:T(8,128)S(1)}) fusion(bf16[2,64,2048]{2,1,0:T(8,128)(2,1)} %param.13, f32[128]{0:T(128)S(1)} %rsqrt.40, f32[2048]{0:T(1024)S(1)} %mul.395, bf16[2048,6144]{1,0:T(8,128)(2,1)} %bitcast.147, bf16[128,2048]{1,0:T(8,128)(2,1)} %copy.109, ...), kind=kOutput, calls=%fused_computation.28 | convolution fusion | flops 3228301312 | bytes 28853248 | tf_op jit(solution)/shard_map/dot_general | solution.py:65
  619.8 1.3 multiply_add_fusion
  622.2 1.3 copy.97
  623.5 5.7 fusion.15.go
  629.2 12.8 %fusion.1.gq = bf16[4,4,2,64,6144]{4,3,2,1,0:T(8,128)(2,1)} fusion(bf16[4,4,2,64,128]{4,3,2,1,0:T(8,128)(2,1)S(1)} %bitcast.160, bf16[128,2048]{1,0:T(8,128)(2,1)S(1)} %copy-done.15, bf16[128,2048]{1,0:T(8,128)(2,1)} %get-tuple-element.88, bf16[128,2048]{1,0:T(8,128)(2,1)S(1)} %copy-done.16), kind=kOutput, calls=%fused_computation.5 | convolution fusion | flops 3225944064 | bytes 27262976 | tf_op jit(solution)/shard_map/dot_general | solution.py:61
  642.0 151.8 %deliver.1 = (f32[64,8192]{1,0:T(8,128)}, f32[8,128]{1,0:T(8,128)}, bf16[2,512,1024]{2,1,0:T(8,128)(2,1)}) custom-call(bf16[4,4,2,64,6144]{4,3,2,1,0:T(8,128)(2,1)} %fusion.1.gq, bf16[4,4,2,64,2048]{4,3,2,1,0:T(8,128)(2,1)} %fusion.15.go, f32[4,4,2,8,128]{4,3,2,1,0:T(8,128)} %bitcast.162, bf16[2048,512]{1,0:T(8,128)(2,1)} %get-tuple-element.41.up_half), custom_call_target="tpu_custom_call" | custom-call | tf_op jit(solution)/shard_map/deliver/pallas_call | solution.py:945
  793.9 1.4 slice_bitcast_fusion.1
  795.2 1.9 slice.100
  797.1 2.7 slice.97
  799.8 4.4 maximum_convert_fusion
  804.2 2.0 copy.145
  (91 shorter events, 14.8 us)
Async XLA Ops:
  7.2 243.2 %copy-start.4 = (bf16[2,64,2048]{2,1,0:T(8,128)(2,1)S(1)}, bf16[2,64,2048]{2,1,0:T(8,128)(2,1)}, u32[]{:S(2)}) copy-start(bf16[2,64,2048]{2,1,0:T(8,128)(2,1)} %param.13) | copy-start | bytes 1572868
  263.1 7.7 copy-start
  493.0 88.3 %copy-start.8 = (bf16[2,64,2048]{2,1,0:T(8,128)(2,1)S(1)}, bf16[2,64,2048]{2,1,0:T(8,128)(2,1)}, u32[]{:S(2)}) copy-start(bf16[2,64,2048]{2,1,0:T(8,128)(2,1)} %param.25) | copy-start | bytes 1572868
  584.0 6.7 copy-start.2
  591.9 5.9 copy-start.1
  597.7 1.9 copy-start.17
  597.7 2.1 copy-start.11
  597.7 2.1 copy-start.12
  599.6 1.1 copy-start.9
  599.6 1.2 copy-start.10
  605.1 14.7 %copy-start.3 = (f32[128,2048]{1,0:T(8,128)S(1)}, f32[128,2048]{1,0:T(8,128)}, u32[]{:S(2)}) copy-start(f32[128,2048]{1,0:T(8,128)} %copy-done.2) | copy-start | bytes 3145732
  605.1 14.7 %copy-start.5 = (bf16[2,64,2048]{2,1,0:T(8,128)(2,1)S(1)}, bf16[2,64,2048]{2,1,0:T(8,128)(2,1)}, u32[]{:S(2)}) copy-start(bf16[2,64,2048]{2,1,0:T(8,128)(2,1)} %param.13) | copy-start | bytes 1572868
  619.8 3.7 copy-start.6
  623.5 5.8 copy-start.15
  623.5 5.7 copy-start.16
  793.8 5.9 copy-start.13
  793.9 5.9 copy-start.14
  799.8 4.4 copy-start.7

commit v4 on v3

--- a/solution.py
+++ b/solution.py
@@ -695,6 +695,7 @@
                 begin, size = self.halves[way]
                 rows = self.kept(z, turn).at[pl.ds(begin, size)]
                 add_up(rows, [rows, self.half.at[z, way, pl.ds(0, size)]], size, self.columns)
+        for way in (0, 1):
             self.pass_on(z, way).start()
 
     def third(self, z, last):
@@ -762,13 +763,11 @@
     return low + high * (DEPTH - 1 - 2 * low)
 
 
-def run_sum(here, items, before=None, between=None):
+def run_sum(here, items):
     order = [far_first(here, number) for number in range(DEPTH)]
     for z in order:
         for item in items:
             item.begin(z)
-    if before is not None:
-        before()
     for item in items:
         item.merge(order[0])
     for number, z in enumerate(order):
@@ -777,8 +776,6 @@
         if number + 1 < DEPTH:
             for item in items:
                 item.merge(order[number + 1])
-        if number == 0 and between is not None:
-            between()
         if number:
             for item in items:
                 item.third(order[number - 1], False)
@@ -789,176 +786,35 @@
             item.end(z, number == DEPTH - 1)
 
 
-class Share:
-    def __init__(self, here, source, target, sems, held):
-        self.here, self.source, self.target, self.sems, self.held = here, source, target, sems, held
-        self.rows = target.shape[1]
-        self.part = source.shape[1] // held
-
-    def pieces(self, steps, arriving):
-        here = self.here
-        origin = lax.rem(here.z + DEPTH - steps, DEPTH) if arriving else here.z
-        away = lax.rem(here.z + steps, DEPTH)
-        copies = []
-        for expert in range(self.held):
-            target = self.target.at[expert, :, pl.ds(pl.multiple_of(origin * self.part, 128), self.part)]
-            source = self.source.at[
-                pl.ds(pl.multiple_of(away * self.rows, 16), self.rows), pl.ds(expert * self.part, self.part)
-            ]
-            if steps == 0:
-                copies.append(pltpu.make_async_copy(source, target, self.sems.at[0, 0, expert]))
-            else:
-                copies.append(
-                    remote(
-                        target if arriving else source,
-                        target,
-                        self.sems.at[0, steps, expert],
-                        self.sems.at[1, steps, expert],
-                        here.above(steps),
-                    )
-                )
-        return copies
-
-    def begin(self):
-        for steps in range(DEPTH):
-            for copy in self.pieces(steps, False):
-                copy.start()
-
-    def end(self):
-        for steps in range(DEPTH):
-            for copy in self.pieces(steps, False):
-                copy.wait() if steps == 0 else copy.wait_send()
-            if steps:
-                for copy in self.pieces(steps, True):
-                    copy.wait_recv()
-
-
-def row_sum_kernel(
-    out, gin, gdown, out_sum, gate_half, up_half, down_sum, *scratch
-):
+def last_sum_kernel(gq, go, small, q_sum, small_sum, *scratch):
     here = Here()
     here.meet()
-    items = [Sum(here, [out], out_sum, halves_of(out.shape[2]), False, scratch[0:8])]
-    other_in, other_down, own_in, own_down, sems, loads, share_sems = scratch[8:15]
-    width = own_in.shape[2]
-    tall = own_down.shape[0]
-    swaps, kept = [], []
-    for side in range(2):
-        for core, into in ((1 - here.core, swaps), (here.core, kept)):
-            source = gin.at[:, pl.ds(pl.multiple_of(side * 2 * width + core * width, 128), width)]
-            into.append((source, side))
-    copies = [
-        remote(source, other_in.at[side], sems.at[0, side], sems.at[1, side], here.sibling())
-        for source, side in swaps
-    ]
-    copies.append(
-        remote(
-            gdown.at[pl.ds(pl.multiple_of((1 - here.core) * tall, 16), tall)],
-            other_down,
-            sems.at[0, 2],
-            sems.at[1, 2],
-            here.sibling(),
-        )
-    )
-    fetched = [pltpu.make_async_copy(source, own_in.at[side], loads.at[side]) for source, side in kept]
-    fetched.append(
-        pltpu.make_async_copy(
-            gdown.at[pl.ds(pl.multiple_of(here.core * tall, 16), tall)], own_down, loads.at[2]
-        )
-    )
-    held = 2
-    share = Share(here, own_in.at[0], gate_half, share_sems, held)
-
-    def before():
-        for copy in copies + fetched:
-            copy.start()
-
-    def between():
-        for side in range(2):
-            copies[side].wait_recv()
-            fetched[side].wait()
-            target = own_in.at[0] if side == 0 else up_half
-            add_up(target, [own_in.at[side], other_in.at[side]], own_in.shape[1], width)
-            if side == 0:
-                share.begin()
-        copies[2].wait_recv()
-        fetched[2].wait()
-        add_up(down_sum, [own_down, other_down], tall, own_down.shape[1])
-
-    run_sum(here, items, before, between)
-    share.end()
-    for copy in copies:
-        copy.wait_send()
-
-
-def row_sum(out, gin, gdown, held):
-    rows, columns = out.shape[2:]
-    deep, wide = gin.shape
-    width = wide // 4
-    tall = gdown.shape[0] // 2
-    vmem = pl.BlockSpec(memory_space=pltpu.VMEM)
-    return pl.pallas_call(
-        row_sum_kernel,
-        out_shape=(
-            jax.ShapeDtypeStruct((rows, columns), single),
-            jax.ShapeDtypeStruct((held, deep // DEPTH, wide // 2), narrow),
-            jax.ShapeDtypeStruct((deep, width), narrow),
-            jax.ShapeDtypeStruct((tall, columns), single),
-        ),
-        in_specs=[HBM] * 3,
-        out_specs=(vmem, HBM, vmem, vmem),
-        scratch_shapes=sum_scratch(rows, columns, narrow, halves_of(rows))
-        + [
-            pltpu.VMEM((2, deep, width), narrow),
-            pltpu.VMEM((tall, columns), narrow),
-            pltpu.VMEM((2, deep, width), narrow),
-            pltpu.VMEM((tall, columns), narrow),
-            pltpu.SemaphoreType.DMA((2, 3)),
-            pltpu.SemaphoreType.DMA((3,)),
-            pltpu.SemaphoreType.DMA((2, DEPTH, 2)),
-        ],
-        compiler_params=pltpu.CompilerParams(
-            collective_id=3, has_side_effects=True, vmem_limit_bytes=62 * 2**20
-        ),
-        name="collect",
-    )(out, gin, gdown)
-
-
-def last_sum_kernel(gq, go, small, up_half, q_sum, small_sum, up_share, *scratch):
-    here = Here()
-    here.meet()
-    rows = gq.shape[3]
     items = [
-        Sum(here, [gq, go], q_sum, halves_of(rows), True, scratch[0:10]),
+        Sum(here, [gq, go], q_sum, halves_of(gq.shape[3]), True, scratch[0:10]),
         Sum(here, [small], small_sum, halves_of(small.shape[3], False), True, scratch[10:20]),
     ]
-    share = Share(here, up_half, up_share, scratch[20], 2)
-    run_sum(here, items, share.begin)
-    share.end()
-
-
-def last_sum(gq, go, small, up_half, held):
+    run_sum(here, items)
+
+
+def last_sum(gq, go, small):
     rows = gq.shape[3]
     columns = gq.shape[4] + go.shape[4]
     vmem = pl.BlockSpec(memory_space=pltpu.VMEM)
-    deep, width = up_half.shape
     return pl.pallas_call(
         last_sum_kernel,
         out_shape=(
             jax.ShapeDtypeStruct((rows, columns), single),
             jax.ShapeDtypeStruct(small.shape[3:], single),
-            jax.ShapeDtypeStruct((held, deep // DEPTH, DEPTH * width // held), narrow),
         ),
-        in_specs=[HBM] * 4,
-        out_specs=(vmem, vmem, HBM),
-        scratch_shapes=sum_scratch(rows, columns, narrow, halves_of(rows), True)
-        + sum_scratch(small.shape[3], small.shape[4], single, halves_of(small.shape[3], False), True)
-        + [pltpu.SemaphoreType.DMA((2, DEPTH, 2))],
+        in_specs=[HBM] * 3,
+        out_specs=(vmem, vmem),
+        scratch_shapes=sum_scratch(rows, columns, narrow, halves_of(rows), paired=True)
+        + sum_scratch(small.shape[3], small.shape[4], single, halves_of(small.shape[3], False), paired=True),
         compiler_params=pltpu.CompilerParams(
             collective_id=4, has_side_effects=True, vmem_limit_bytes=62 * 2**20
         ),
         name="deliver",
-    )(gq, go, small, up_half)
+    )(gq, go, small)
 
 def near_first(here, number):
     high = lax.div(here.z, 2)
@@ -971,38 +827,61 @@
 
 
 class Tiles:
-    def __init__(self, stage, sems):
-        self.stage, self.sems = stage, sems
-
-    def run(self, first, last, count, target, make):
-        def store(number):
-            slot = lax.rem(number, 2)
-            rows = pl.ds(pl.multiple_of(number * TILE, TILE), TILE)
-            return pltpu.make_async_copy(self.stage.at[slot], target.at[rows], self.sems.at[slot])
-
+    def __init__(self, here, stage, count, sems, parts, targets):
+        self.here, self.stage, self.count = here, stage, count
+        self.kept, self.sent, self.came = sems
+        self.parts, self.targets = parts, targets
+
+    def copies(self, number, keep=True, give=True):
+        slot = lax.rem(number, 2)
+        own, other = self.targets
+        made = []
+        for piece, (mine, theirs, spot) in enumerate(self.parts(number, self.stage.at[slot])):
+            if keep:
+                made.append(pltpu.make_async_copy(mine, own.at[spot], self.kept.at[slot, piece]))
+            if give:
+                sems = (self.sent.at[slot, piece], self.came.at[number, piece])
+                made.append(remote(theirs, other.at[spot], *sems, self.here.sibling()))
+        return made
+
+    def settle(self, number):
+        for copy in self.copies(number, give=False):
+            copy.wait()
+        for copy in self.copies(number, keep=False):
+            copy.wait_send()
+
+    def run(self, first, last, make):
         def body(number, carry):
-            pl.when(number >= 2)(lambda: store(number - 2).wait())
+            pl.when(number >= 2)(lambda: self.settle(number - 2))
             make(number, self.stage.at[lax.rem(number, 2)])
-            store(number).start()
+            for copy in self.copies(number):
+                copy.start()
             return carry
 
         lax.fori_loop(first, last, body, 0)
-        if last == count:
-            for number in (count - 2, count - 1):
-                store(number).wait()
+        if last == self.count:
+            for number in (last - 2, last - 1):
+                self.settle(number)
+
+    def heard(self):
+        for number in range(self.count):
+            for copy in self.copies(number, keep=False):
+                copy.wait_recv()
 
 
 def experts_kernel(
-    rows, ups, gates, win, wout, mid_sum, gate_sum, out, gin, gdown, rows_all, *scratch
+    rows, ups, gates, win, wout, mid_sum, gate_sum, out_sum, gin, gin_other, gdown, gdown_other, rows_all, *scratch
 ):
     here = Here()
     here.meet()
     (
-        w_in, w_out, grads, scaled, row_plane, up_plane, gate_plane, served, strip, stage, loads, strip_sems, stage_sems
-    ) = scratch[:13]
-    gather = Gather(here, rows, rows_all, halves_of(rows.shape[0]), False, scratch[13:17])
-    mids = Sum(here, None, mid_sum, halves_of(rows.shape[0]), False, scratch[17:25])
-    tables = Sum(here, None, gate_sum, halves_of(gate_sum.shape[0], False), False, scratch[25:33])
+        w_in, w_out, grads, scaled, row_plane, up_plane, gate_plane, served, strip, stage, loads, strip_sems
+    ) = scratch[:12]
+    gather = Gather(here, rows, rows_all, halves_of(rows.shape[0]), False, scratch[12:16])
+    mids = Sum(here, None, mid_sum, halves_of(rows.shape[0]), False, scratch[16:24])
+    outs = Sum(here, None, out_sum, halves_of(rows.shape[0]), False, scratch[16:19] + scratch[24:29])
+    tables = Sum(here, None, gate_sum, halves_of(gate_sum.shape[0], False), False, scratch[29:37])
+    in_sems, down_sems = scratch[37:40], scratch[40:43]
     block, width = rows.shape
     plane = RING * block
     hidden = w_out.shape[0]
@@ -1072,18 +951,31 @@
 
         lax.fori_loop(0, width // TILE, one, 0)
 
+    def products(z):
+        at = pl.ds(pl.multiple_of(z * plane, plane), plane)
+
+        def one(number, carry):
+            spot = pl.ds(pl.multiple_of(number * TILE, TILE), TILE)
+            made = jnp.dot(scaled[at], w_out[:, spot], preferred_element_type=single).astype(narrow)
+            for chip in range(RING):
+                outs.mine[z, chip, :, spot] = made[chip * block : (chip + 1) * block]
+            return carry
+
+        lax.fori_loop(0, width // TILE, one, 0)
+
     for copy in fetch_plane(0):
         copy.start()
     rounds = Rounds(here, [gather])
+    rounds.service(0)
     for number in range(DEPTH):
-        rounds.service(number)
+        if number + 1 < DEPTH:
+            rounds.service(number + 1)
         gather_third(gather, near_first(here, number))
         if number + 1 < DEPTH:
             for copy in fetch_plane(number + 1):
                 copy.start()
         hidden_units(number)
 
-    tiles = Tiles(stage, stage_sems)
     strips = width // TILE
 
     def fetch_strip(number):
@@ -1102,60 +994,96 @@
         left = strip[slot].reshape(DEPTH * plane, TILE)
         columns_of(lambda begin, step: contract_rows(left, grads[:, begin : begin + step]), stage)
 
-    def outputs(number, stage):
+    def grad_in_parts(number, stage):
+        share = hidden // 2
         at = pl.ds(pl.multiple_of(number * TILE, TILE), TILE)
-        left = scaled[at]
-        columns_of(
-            lambda begin, step: jnp.dot(left, w_out[:, begin : begin + step], preferred_element_type=single),
-            stage,
-        )
+        for side in range(2):
+            mine, theirs = (
+                stage.at[:, pl.ds(pl.multiple_of(side * hidden + core * share, 128), share)]
+                for core in (here.core, 1 - here.core)
+            )
+            yield mine, theirs, (at, pl.ds(side * share, share))
 
     def grad_down(number, stage):
-        at = pl.ds(pl.multiple_of(number * TILE, TILE), TILE)
-        left = scaled[:, at]
+        half = tall // 2
+        core = here.core + (1 - lax.div(number, half)) * (1 - 2 * here.core)
+        at = core * half + lax.rem(number, half)
+        left = scaled[:, pl.ds(pl.multiple_of(at * TILE, TILE), TILE)]
         columns_of(lambda begin, step: contract_rows(left, w_in[:, begin : begin + step]), stage)
+
+    tall = hidden // TILE
+    tiles_in = Tiles(here, stage, strips, in_sems, grad_in_parts, (gin, gin_other))
+
+    def grad_down_store(number, away):
+        slot = lax.rem(number, 2)
+        rest = lax.rem(number, tall // 2)
+        spot = pl.ds(pl.multiple_of(rest * TILE, TILE), TILE)
+        kept, sent, came = down_sems
+        if away:
+            return remote(stage.at[slot], gdown_other.at[spot], sent.at[slot, 0], came.at[rest, 0], here.sibling())
+        return pltpu.make_async_copy(stage.at[slot], gdown.at[spot], kept.at[slot, 0])
+
+    def grads_down(away):
+        first = 0 if away else tall // 2
+
+        def body(number, carry):
+            grad_down(number, stage.at[lax.rem(number, 2)])
+            grad_down_store(number, away).start()
+            return carry
+
+        lax.fori_loop(first, first + tall // 2, body, 0)
+        for number in range(first, first + tall // 2):
+            copy = grad_down_store(number, away)
+            copy.wait_send() if away else copy.wait()
+
+    again = [
+        pltpu.make_async_copy(ups.at[z], w_in.at[pl.ds(z * plane, plane)], loads.at[7 + z]) for z in range(DEPTH)
+    ]
+
+    def again_wait():
+        for copy in again:
+            copy.wait()
 
     fetch_strip(0).start()
     order = [far_first(here, number) for number in range(DEPTH)]
-    items = [mids, tables]
-    high = DEPTH * plane // TILE
-    work = [
-        lambda: tiles.run(0, 2, strips, gin, grad_in),
-        lambda: tiles.run(2, 4, strips, gin, grad_in),
-        lambda: tiles.run(4, 6, strips, gin, grad_in),
-        lambda: tiles.run(6, strips, strips, gin, grad_in),
-    ]
-    for number, z in enumerate(order):
-        row_grads(z)
+    steps = [([mids, tables], z, number == DEPTH - 1) for number, z in enumerate(order)]
+    steps += [([outs], z, number == DEPTH - 1) for number, z in enumerate(order)]
+    each = strips // DEPTH
+    for number, (items, z, last) in enumerate(steps):
+        if number < DEPTH:
+            row_grads(z)
+        else:
+            mids.end(z, last)
+            products(z)
         for item in items:
             for way in (0, 1):
                 start(item.toss(z, way))
         if number:
-            for item in items:
-                item.second(order[number - 1])
+            for item in steps[number - 1][0]:
+                item.second(steps[number - 1][1])
         if number > 1:
-            for item in items:
-                item.third(order[number - 2], False)
-        if number + 1 < DEPTH:
-            work[number]()
-    again = [
-        pltpu.make_async_copy(ups.at[z], w_in.at[pl.ds(z * plane, plane)], loads.at[7 + z]) for z in range(DEPTH)
-    ]
-    for copy in again:
-        copy.start()
-    work[DEPTH - 1]()
-    for item in items:
-        item.second(order[DEPTH - 1])
-        item.third(order[DEPTH - 2], False)
-    tiles.run(0, high, high, out, outputs)
-    for item in items:
-        item.third(order[DEPTH - 1], True)
-    for copy in again:
-        copy.wait()
-    tiles.run(0, hidden // TILE, hidden // TILE, gdown, grad_down)
+            before, place, final = steps[number - 2]
+            for item in before:
+                item.third(place, final)
+        if number == DEPTH - 1:
+            for copy in again:
+                copy.start()
+        if number < DEPTH:
+            tiles_in.run(number * each, (number + 1) * each, grad_in)
+        elif number == DEPTH:
+            again_wait()
+            grads_down(True)
+        elif number == DEPTH + 1:
+            grads_down(False)
+    outs.second(order[-1])
+    outs.third(order[-2], False)
+    outs.third(order[-1], True)
     for number, z in enumerate(order):
-        for item in items:
-            item.end(z, number == DEPTH - 1)
+        outs.end(z, number == DEPTH - 1)
+        tables.end(z, number == DEPTH - 1)
+    tiles_in.heard()
+    for number in range(tall // 2):
+        grad_down_store(number, True).wait_recv()
     rounds.finish()
 
 
@@ -1170,13 +1098,15 @@
         out_shape=(
             jax.ShapeDtypeStruct((block, width), single),
             jax.ShapeDtypeStruct((experts, block), single),
-            jax.ShapeDtypeStruct((total, width), narrow),
-            jax.ShapeDtypeStruct((width, 2 * hidden), narrow),
-            jax.ShapeDtypeStruct((hidden, width), narrow),
+            jax.ShapeDtypeStruct((block, width), single),
+            jax.ShapeDtypeStruct((width, hidden), narrow),
+            jax.ShapeDtypeStruct((width, hidden), narrow),
+            jax.ShapeDtypeStruct((hidden // 2, width), narrow),
+            jax.ShapeDtypeStruct((hidden // 2, width), narrow),
             jax.ShapeDtypeStruct((DEPTH, RING, block, width), narrow),
         ),
         in_specs=[HBM] * 5,
-        out_specs=(vmem, vmem) + (HBM,) * 4,
+        out_specs=(vmem, vmem, vmem) + (HBM,) * 5,
         scratch_shapes=[
             pltpu.VMEM((width, 2 * hidden), narrow),
             pltpu.VMEM((hidden, width), narrow),
@@ -1190,11 +1120,22 @@
             pltpu.VMEM((2, TILE, width), narrow),
             pltpu.SemaphoreType.DMA((11,)),
             pltpu.SemaphoreType.DMA((2,)),
-            pltpu.SemaphoreType.DMA((2,)),
         ]
         + GATHER_SEMS
         + sum_scratch(block, width, narrow, halves_of(block), made=True)
-        + sum_scratch(experts, block, single, halves_of(experts, False), made=True),
+        + [pltpu.VMEM((DEPTH + 1, block, width), narrow)]
+        + SUM_SEMS
+        + sum_scratch(experts, block, single, halves_of(experts, False), made=True)
+        + [
+            pltpu.SemaphoreType.DMA((2, 2)),
+            pltpu.SemaphoreType.DMA((2, 2)),
+            pltpu.SemaphoreType.DMA((width // TILE, 2)),
+        ]
+        + [
+            pltpu.SemaphoreType.DMA((2, 1)),
+            pltpu.SemaphoreType.DMA((2, 1)),
+            pltpu.SemaphoreType.DMA((hidden // TILE, 1)),
+        ],
         compiler_params=pltpu.CompilerParams(
             collective_id=2, has_side_effects=True, vmem_limit_bytes=62 * 2**20
         ),
@@ -1237,6 +1178,33 @@
         lax.all_gather(gain_rows, everyone, axis=1, tiled=True),
         weight_in,
         weight_down,
+    )
+
+
+def return_halves(half_way, held):
+    grad_in, grad_in_other, grad_down, grad_down_other = half_way
+    total = (grad_in.astype(single) + grad_in_other.astype(single)).astype(narrow)
+    rows, columns = total.shape
+    cut = total.reshape(DEPTH, rows // DEPTH, columns)
+    turned = lax.all_to_all(cut, "dp", split_axis=0, concat_axis=0, tiled=True)
+    part = columns // (2 * held)
+    share = jnp.stack(
+        [
+            jnp.concatenate(
+                [
+                    turned[z, :, (side * held + expert) * part : (side * held + expert + 1) * part]
+                    for side in range(2)
+                    for z in range(DEPTH)
+                ],
+                axis=1,
+            )
+            for expert in range(held)
+        ]
+    )
+    down = grad_down.astype(single) + grad_down_other.astype(single)
+    return (
+        share.astype(single),
+        down.reshape(held, -1, down.shape[1]),
     )
 
 
@@ -1253,11 +1221,10 @@
     if by_kernels():
         gate = jnp.pad(gate.reshape(DEPTH, -1, chip_experts), ((0, 0), (0, 0), (0, 128 - chip_experts)))
         ups = up_rows.reshape(DEPTH, -1, width)
-        grad_routed, table, out, grad_in, grad_down, _ = experts_round(
+        grad_routed, table, mixture, *half_way, _ = experts_round(
             routed_in, ups, gate, weight_in, weight_down, experts
         )
-        mixture, *half_way = row_sum(out.reshape(DEPTH, RING, rows, width), grad_in, grad_down, held)
-        return (mixture, grad_routed, table, half_way)
+        return (mixture, grad_routed, table, return_halves(half_way, held))
     mid_rows = gather_alike(routed_in).reshape(-1, width)
     out, mid, served, grad_in, grad_down = expert_rounds(
         mid_rows, up_rows, gate.reshape(-1, chip_experts), weight_in, weight_down
@@ -1269,41 +1236,33 @@
         scatter_alike(out.reshape(depth, chips, rows, width)).astype(single),
         scatter_alike(mid.reshape(depth, chips, rows, width)).astype(single),
         scatter_alike(spread),
-        (grad_in, grad_down),
-    )
-
-
-def deliver_all(pieces, grad_qkv, grad_out, half_way, held):
+        [share.astype(single) for share in return_weights(grad_in, grad_down, held)],
+    )
+
+
+def deliver_all(pieces, grad_qkv, grad_out):
     owners = lax.axis_size("dp") * lax.axis_size("expert")
     share = pieces.shape[1] // owners
     if by_kernels():
-        gate_half, up_half, down = half_way
         lead = (DEPTH, RING, 2)
         small = pieces.reshape(4, owners, share).transpose(1, 0, 2)
         small = jnp.pad(small, ((0, 0), (0, 4), (0, 128 - share))).reshape(lead + (8, 128))
-        shares, gains, up_share = last_sum(
+        shares, gains = last_sum(
             grad_qkv.reshape(lead + (-1,) + grad_qkv.shape[1:]),
             grad_out.reshape(lead + (-1,) + grad_out.shape[1:]),
             small,
-            up_half,
-            held,
         )
         wide = grad_qkv.shape[1]
         return (
             gains[:4, :share],
             shares[:, :wide],
             shares[:, wide:],
-            jnp.concatenate([gate_half, up_share], axis=2).astype(single),
-            down.reshape(held, -1, down.shape[1]),
         )
     everyone = ("dp", "expert")
-    share_in, share_down = return_weights(*half_way, held)
     return (
         lax.psum_scatter(pieces, everyone, scatter_dimension=1, tiled=True),
         lax.psum_scatter(grad_qkv, everyone, scatter_dimension=0, tiled=True).astype(single),
         lax.psum_scatter(grad_out, everyone, scatter_dimension=0, tiled=True).astype(single),
-        share_in.astype(single),
-        share_down.astype(single),
     )
 
 
@@ -1365,7 +1324,7 @@
     normal_mid, factor_mid = normalize(middle)
     routed_in = (normal_mid * gain_ffn).astype(narrow)
 
-    mixture, grad_routed, gate_table, half_way = experts_all(
+    mixture, grad_routed, gate_table, (share_in, share_down) = experts_all(
         routed_in, up_rows, every_gate, weight_in, weight_down, held
     )
     grad_gates = jnp.sum(onehot * gate_table.T[:, None, :], axis=2)
@@ -1401,9 +1360,7 @@
     grad_tokens = grad_middle + grad_input
 
     pieces = jnp.stack([piece_attn, piece_query, piece_key, piece_ffn])
-    gain_sums, grad_qkv_share, grad_out_share, share_in, share_down = deliver_all(
-        pieces, grad_qkv_part, grad_out_part, half_way, held
-    )
+    gain_sums, grad_qkv_share, grad_out_share = deliver_all(pieces, grad_qkv_part, grad_out_part)
     shape = (micro_count, seq_len, model_width)
     return (
         results.reshape(shape),

time: 817 us -> 792 us (0.969)
  Pallas kernels: 691 us -> 633 us
  starting transfers between devices: 0 us -> 14 us
  other arithmetic: 24.7 us -> 36.3 us
    pallas_call x1 -> x0, Pallas kernels: 86.1 us -> none  [row_sum(): pl.pallas_call(row_sum_kernel, out_shape=(jax.ShapeDtypeStruct((rows, col...]
    pallas_call x1, Pallas kernels: 212 us -> 240 us  [experts_round(): pl.pallas_call(experts_kernel, out_shape=(jax.ShapeDtypeStruct((block, wi...]
    all_to_all x0 -> x1, starting transfers between devices: none -> 14 us  [return_halves(): turned = lax.all_to_all(cut, 'dp', split_axis=0, concat_axis=0, tiled=True)]
  transfers between devices with their start and end apart: 0 -> 1, of which waited for: 0 -> 0; matrix products, arithmetic and copies ran while one was open for 0% -> 9% of each run, Pallas kernels for 0% -> 19%
where the time goes in v4:
time: 792 us; the launch traced here: 783 us
  Pallas kernels  633 us (80%)
  matrix products  70.2 us (9%)
  other arithmetic  36.3 us (5%)
  local copies, waits for them, and re-layouts  27.7 us (3%)
  starting transfers between devices  14 us (2%)
    pallas_call x1, Pallas kernels, first_gather(): pl.pallas_call(first_gather_kernel, out_shape=(whole(wq, True), whole(wo,...  241 us
    pallas_call x1, Pallas kernels, experts_round(): pl.pallas_call(experts_kernel, out_shape=(jax.ShapeDtypeStruct((block, wi...  240 us
    pallas_call x1, Pallas kernels, last_sum(): pl.pallas_call(last_sum_kernel, out_shape=(jax.ShapeDtypeStruct((rows, co...  153 us
    dot_general x2, matrix products, contract_last(): lax.dot_general(left, right, (((1,), (1,)), ((), ())), preferred_element_...  21 us
    dot_general x2, matrix products, contract_rows(): lax.dot_general(left, right, (((0,), (0,)), ((), ())), preferred_element_...  18.7 us
  transfers between devices with their start and end apart: 1, of which 0 were waited for; matrix products, arithmetic and copies ran while one was open for 9% of the time, Pallas kernels for 19%

profile of v4, /device:TPU:0, one launch (start us, length us, event | category | flops | bytes accessed | tf_op | source)
XLA Modules:
  0.0 782.8 jit_solution(1377771947946576418)
XLA Ops:
  2.6 1.2 multiply_reduce_fusion.10
  6.8 240.7 %bring.1 = (bf16[4,4,2,64,6144]{4,3,2,1,0:T(8,128)(2,1)}, bf16[4,4,2,64,2048]{4,3,2,1,0:T(8,128)(2,1)}, bf16[4,4,128,2048]{3,2,1,0:T(8,128)(2,1)}, f32[4,4,2,24,...) custom-call(bf16[64,6144]{1,0:T(8,128)(2,1)} %wq.1, bf16[64,2048]{1,0:T(8,128)(2,1)} %wo.1, ...), custom_call_target="tpu_custom_call" | custom-call | tf_op jit(solution)/shard_map/bring/pallas_call | solution.py:524
  249.9 1.3 copy.83
  251.5 10.2 %fusion.69 = f32[128,6144]{1,0:T(8,128)S(1)} fusion(bf16[128,2048]{1,0:T(8,128)(2,1)S(1)} %bitcast.226, bf16[2048,6144]{1,0:T(8,128)(2,1)} %bitcast.212), kind=kOutput, calls=%fused_computation.179 | convolution fusion | flops 3221225472 | bytes 28835840 | tf_op jit(solution)/shard_map/dot_general | solution.py:1302
  263.6 2.8 subtract_convert_fusion.1
  266.4 3.3 fusion.68
  269.7 3.4 convolution_convert_fusion.2
  273.0 5.0 multiply_reduce_fusion.7
  280.1 239.8 %experts.1 = (f32[128,2048]{1,0:T(8,128)}, f32[16,128]{1,0:T(8,128)}, f32[128,2048]{1,0:T(8,128)}, bf16[2048,1024]{1,0:T(8,128)(2,1)}, bf16[2048,1024]{1,0:T(8,1...) custom-call(bf16[128,2048]{1,0:T(8,128)(2,1)} %multiply_convert_fusion.4.rows, ...), custom_call_target="tpu_custom_call" | custom-call | tf_op jit(solution)/shard_map/experts/pallas_call | solution.py:1096
  519.9 7.6 add_convert_fusion
  527.5 14.0 %all-to-all-start = ((bf16[4,512,1024]{2,1,0:T(8,128)(2,1)}), bf16[4,512,1024]{2,1,0:T(8,128)(2,1)}, u32[]{:S(2)}, u32[]{:S(2)}) async-start(bf16[4,512,1024]{2,1,0:T(8,128)(2,1)} %bitcast.214), calls=%async_computation | async-start | bytes 8388608 | tf_op jit(solution)/shard_map/all_to_all | solution.py:1189
  542.0 2.4 multiply_add_fusion.3
  545.4 6.3 convolution_convert_fusion
  552.7 3.8 convolution_convert_fusion.1
  556.5 1.8 multiply_reduce_fusion.5
  558.6 1.4 fusion.5
  560.0 1.5 fusion.6
  561.6 2.0 copy.109
  563.7 3.0 multiply_subtract_fusion.1
  567.6 1.9 multiply_convert_fusion.2
  569.4 14.8 %multiply_reduce_fusion.1 = (f32[2048]{0:T(1024)S(1)}, f32[128]{0:T(128)S(1)}, bf16[128,2048]{1,0:T(8,128)(2,1)S(1)}, f32[128,2048]{1,0:T(8,128)}) fusion(bf16[2,64,2048]{2,1,0:T(8,128)(2,1)} %param.13, f32[128]{0:T(128)S(1)} %rsqrt.40, f32[2048]{0:T(1024)S(1)} %mul.395, bf16[2048,6144]{1,0:T(8,128)(2,1)} %bitcast.213, bf16[128,2048]{1,0:T(8,128)(2,1)} %copy.109, ...), kind=kOutput, calls=%fused_computation.30 | convolution fusion | flops 3228301312 | bytes 28853248 | tf_op jit(solution)/shard_map/dot_general | solution.py:65
  585.5 5.7 fusion.15.go
  591.2 12.9 %fusion.1.gq = bf16[4,4,2,64,6144]{4,3,2,1,0:T(8,128)(2,1)} fusion(bf16[4,4,2,64,128]{4,3,2,1,0:T(8,128)(2,1)S(1)} %bitcast.228, bf16[128,2048]{1,0:T(8,128)(2,1)S(1)} %copy-done.15, bf16[128,2048]{1,0:T(8,128)(2,1)} %get-tuple-element.98, bf16[128,2048]{1,0:T(8,128)(2,1)} %get-tuple-element.97), kind=kOutput, calls=%fused_computation.7 | convolution fusion | flops 3225944064 | bytes 27262976 | tf_op jit(solution)/shard_map/dot_general | solution.py:61
  604.2 152.6 %deliver.1 = (f32[64,8192]{1,0:T(8,128)}, f32[8,128]{1,0:T(8,128)}) custom-call(bf16[4,4,2,64,6144]{4,3,2,1,0:T(8,128)(2,1)} %fusion.1.gq, bf16[4,4,2,64,2048]{4,3,2,1,0:T(8,128)(2,1)} %fusion.15.go, f32[4,4,2,8,128]{4,3,2,1,0:T(8,128)} %bitcast.230), custom_call_target="tpu_custom_call" | custom-call | tf_op jit(solution)/shard_map/deliver/pallas_call | solution.py:803
  756.8 1.9 slice.148
  758.7 2.7 slice.145
  762.7 2.6 multiply_add_fusion
  765.2 4.4 convert_add_fusion
  770.7 1.1 fusion.33
  771.8 1.1 fusion.32
  772.9 1.1 fusion.31
  778.4 3.9 maximum_convert_fusion
  (103 shorter events, 23.0 us)
Async XLA Ops:
  6.8 244.5 %copy-start.4 = (bf16[2,64,2048]{2,1,0:T(8,128)(2,1)S(1)}, bf16[2,64,2048]{2,1,0:T(8,128)(2,1)}, u32[]{:S(2)}) copy-start(bf16[2,64,2048]{2,1,0:T(8,128)(2,1)} %param.13) | copy-start | bytes 1572868
  261.7 8.0 %copy-start = (f32[128,6144]{1,0:T(8,128)}, f32[128,6144]{1,0:T(8,128)S(1)}, u32[]{:S(2)}) copy-start(f32[128,6144]{1,0:T(8,128)S(1)} %fusion.69) | copy-start | bytes 9437188
  273.0 5.0 copy-start.7
  527.5 14.1 %copy-start.8 = (f32[128,2048]{1,0:T(8,128)S(1)}, f32[128,2048]{1,0:T(8,128)}, u32[]{:S(2)}) copy-start(f32[128,2048]{1,0:T(8,128)} %get-tuple-element.33) | copy-start | bytes 3145732
  527.5 14.4 %copy-start.9 = (bf16[2,64,2048]{2,1,0:T(8,128)(2,1)S(1)}, bf16[2,64,2048]{2,1,0:T(8,128)(2,1)}, u32[]{:S(2)}) copy-start(bf16[2,64,2048]{2,1,0:T(8,128)(2,1)} %param.25) | copy-start | bytes 1572868
  527.5 242.0 %all-to-all-start = ((bf16[4,512,1024]{2,1,0:T(8,128)(2,1)}), bf16[4,512,1024]{2,1,0:T(8,128)(2,1)}, u32[]{:S(2)}, u32[]{:S(2)}) async-start(bf16[4,512,1024]{2,1,0:T(8,128)(2,1)} %bitcast.214), calls=%async_computation | async-start | bytes 8388608 | tf_op jit(solution)/shard_map/all_to_all | solution.py:1189
  544.4 1.0 copy-start.2
  552.7 3.8 copy-start.1
  556.5 1.9 copy-start.16
  556.5 2.1 copy-start.12
  556.5 2.1 copy-start.13
  558.3 1.7 copy-start.10
  558.3 1.7 copy-start.11
  569.4 16.0 %copy-start.3 = (f32[128,2048]{1,0:T(8,128)S(1)}, f32[128,2048]{1,0:T(8,128)}, u32[]{:S(2)}) copy-start(f32[128,2048]{1,0:T(8,128)} %copy-done.2) | copy-start | bytes 3145732
  569.4 16.1 %copy-start.6 = (bf16[16,128,128]{2,1,0:T(8,128)(2,1)S(1)}, bf16[16,128,128]{2,1,0:T(8,128)(2,1)}, u32[]{:S(2)}) copy-start(bf16[16,128,128]{2,1,0:T(8,128)(2,1)} %convolution_convert_fusion.2) | copy-start | bytes 1572868
  585.5 5.7 copy-start.15
  756.8 4.6 copy-start.17
  756.8 5.3 copy-start.18
  756.8 5.8 copy-start.5
  761.5 3.7 copy-start.14

commit v5 on v4

--- a/solution.py
+++ b/solution.py
@@ -580,7 +580,8 @@
 
 class Sum:
     def __init__(self, here, sources, target, halves, paired, scratch):
-        self.here, self.sources, self.target, self.halves, self.paired = here, sources, target, halves, paired
+        self.here, self.sources, self.halves, self.paired = here, sources, halves, paired
+        self.target = target if isinstance(target, list) else [(target, 0, target.shape[0])]
         self.mine, self.half, self.full, self.column = scratch[:4]
         self.half_sem, self.full_sem, self.line_sem, self.load_sem = scratch[4:8]
         if paired:
@@ -708,24 +709,7 @@
         kept = self.kept(z, 0)
         terms = [kept, self.full.at[z, 0], self.full.at[z, 1]]
         if last:
-            below, above = self.column.at[z], self.column.at[DEPTH]
-
-            @pl.when(here.z == 0)
-            def _():
-                self.climb(z, 1, 0, DEPTH).wait_recv()
-                add_up(self.target, terms + [above], self.rows, self.columns)
-
-            @pl.when(here.z == DEPTH - 1)
-            def _():
-                self.climb(z, 0, 0, z).wait_recv()
-                add_up(self.target, terms + [below], self.rows, self.columns)
-
-            @pl.when((here.z > 0) & (here.z < DEPTH - 1))
-            def _():
-                self.climb(z, 0, 0, z).wait_recv()
-                self.climb(z, 1, 0, DEPTH).wait_recv()
-                add_up(self.target, terms + [below, above], self.rows, self.columns)
-
+            self.arrive(z, terms)
             return
         up = (z > here.z).astype(jnp.int32)
         way = 1 - up
@@ -741,6 +725,40 @@
             add_up(kept, terms, self.rows, self.columns)
 
         self.climb(z, way, up).start()
+
+    def own_part(self, z):
+        for way in (0, 1):
+            self.pass_on(z, way).wait_recv()
+        [(target, _, rows)] = self.target
+        add_up(target, [self.kept(z, 0), self.full.at[z, 0], self.full.at[z, 1]], rows, self.columns)
+
+    def own_rest(self, z):
+        self.arrive(z, [self.target[0][0]])
+
+    def arrive(self, z, terms):
+        here = self.here
+        below, above = self.column.at[z], self.column.at[DEPTH]
+
+        def total(more):
+            for target, row, rows in self.target:
+                part = [term.at[pl.ds(row, rows)] for term in terms + more]
+                add_up(target, part, rows, self.columns)
+
+        @pl.when(here.z == 0)
+        def _():
+            self.climb(z, 1, 0, DEPTH).wait_recv()
+            total([above])
+
+        @pl.when(here.z == DEPTH - 1)
+        def _():
+            self.climb(z, 0, 0, z).wait_recv()
+            total([below])
+
+        @pl.when((here.z > 0) & (here.z < DEPTH - 1))
+        def _():
+            self.climb(z, 0, 0, z).wait_recv()
+            self.climb(z, 1, 0, DEPTH).wait_recv()
+            total([below, above])
 
     def end(self, z, last):
         if self.paired:
@@ -763,58 +781,124 @@
     return low + high * (DEPTH - 1 - 2 * low)
 
 
-def run_sum(here, items):
+def last_sum_kernel(
+    normed, grad, attended, branch, small, q_sum, o_sum, small_sum, left, left_out, right, sems, *scratch
+):
+    here = Here()
+    here.meet()
+    block, width = normed.shape
+    share = q_sum.shape[0]
+    wide = grad.shape[1]
+    sides = wide // width
+    moved = [
+        (normed, left, None),
+        (grad, right, pl.ds(0, wide)),
+        (attended, left_out, None),
+        (branch, right, pl.ds(wide, width)),
+    ]
+    copies = []
+    for number, (source, target, spot) in enumerate(moved):
+        own, other = (target.at[core] if spot is None else target.at[core, :, spot] for core in (0, 1))
+        copies.append(
+            (
+                pltpu.make_async_copy(source, own, sems.at[number]),
+                remote(source, other, sems.at[4 + number], sems.at[8 + number], here.sibling()),
+            )
+        )
+    for kept, sent in copies:
+        sent.start()
+        kept.start()
+    targets = [(q_sum.at[:, pl.ds(side * width, width)], side * share, share) for side in range(sides)]
+    targets.append((o_sum, sides * share, share))
+    big = Sum(here, None, targets, halves_of((sides + 1) * share), False, scratch[0:8])
+    few = Sum(here, [small], small_sum, halves_of(small.shape[3], False), True, scratch[8:18])
     order = [far_first(here, number) for number in range(DEPTH)]
     for z in order:
-        for item in items:
-            item.begin(z)
-    for item in items:
-        item.merge(order[0])
+        few.begin(z)
+    for kept, sent in copies:
+        kept.wait()
+        sent.wait_recv()
+    step = 512
+    each = width // step
+    rows = RING * 2 * share
+
+    def make(z):
+        at = pl.ds(pl.multiple_of(z * rows, rows), rows)
+
+        def piece(number, source):
+            spot = pl.ds(pl.multiple_of(number * step, step), step)
+            turned = source[:, :, at].reshape(2 * block, rows)
+            made = contract_rows(turned, right[:, :, spot].reshape(2 * block, step))
+            made = made.reshape(RING, 2, share, step)
+            mine = jnp.where(here.core == 0, made[:, 0], made[:, 1]).astype(narrow)
+            row = pl.multiple_of(lax.div(number, each) * share, share)
+            column = pl.multiple_of(lax.rem(number, each) * step, step)
+            for chip in range(RING):
+                big.mine[z, chip, pl.ds(row, share), pl.ds(column, step)] = mine[chip]
+
+        def qkv(number, carry):
+            piece(number, left)
+            return carry
+
+        def out(number, carry):
+            piece(number, left_out)
+            return carry
+
+        lax.fori_loop(0, sides * each, qkv, 0)
+        lax.fori_loop(sides * each, (sides + 1) * each, out, 0)
+
+    items = [big, few]
     for number, z in enumerate(order):
-        for item in items:
-            item.second(z)
-        if number + 1 < DEPTH:
-            for item in items:
-                item.merge(order[number + 1])
+        make(z)
+        for way in (0, 1):
+            start(big.toss(z, way))
+        few.merge(z)
         if number:
             for item in items:
-                item.third(order[number - 1], False)
+                item.second(order[number - 1])
+        if number > 1:
+            for item in items:
+                item.third(order[number - 2], False)
+    for item in items:
+        item.second(order[-1])
+    for item in items:
+        item.third(order[-2], False)
     for item in items:
         item.third(order[-1], True)
     for number, z in enumerate(order):
         for item in items:
             item.end(z, number == DEPTH - 1)
-
-
-def last_sum_kernel(gq, go, small, q_sum, small_sum, *scratch):
-    here = Here()
-    here.meet()
-    items = [
-        Sum(here, [gq, go], q_sum, halves_of(gq.shape[3]), True, scratch[0:10]),
-        Sum(here, [small], small_sum, halves_of(small.shape[3], False), True, scratch[10:20]),
-    ]
-    run_sum(here, items)
-
-
-def last_sum(gq, go, small):
-    rows = gq.shape[3]
-    columns = gq.shape[4] + go.shape[4]
+    for kept, sent in copies:
+        sent.wait_send()
+
+
+def last_sum(normed, grad, attended, branch, small, share):
+    block, width = normed.shape
+    wide = grad.shape[1]
+    rows = (wide // width + 1) * share
     vmem = pl.BlockSpec(memory_space=pltpu.VMEM)
     return pl.pallas_call(
         last_sum_kernel,
         out_shape=(
-            jax.ShapeDtypeStruct((rows, columns), single),
+            jax.ShapeDtypeStruct((share, wide), single),
+            jax.ShapeDtypeStruct((share, width), single),
             jax.ShapeDtypeStruct(small.shape[3:], single),
         ),
-        in_specs=[HBM] * 3,
-        out_specs=(vmem, vmem),
-        scratch_shapes=sum_scratch(rows, columns, narrow, halves_of(rows), paired=True)
+        in_specs=[HBM] * 5,
+        out_specs=(vmem, vmem, vmem),
+        scratch_shapes=[
+            pltpu.VMEM((2, block, width), narrow),
+            pltpu.VMEM((2, block, width), narrow),
+            pltpu.VMEM((2, block, wide + width), narrow),
+            pltpu.SemaphoreType.DMA((12,)),
+        ]
+        + sum_scratch(rows, width, narrow, halves_of(rows), made=True)
         + sum_scratch(small.shape[3], small.shape[4], single, halves_of(small.shape[3], False), paired=True),
         compiler_params=pltpu.CompilerParams(
             collective_id=4, has_side_effects=True, vmem_limit_bytes=62 * 2**20
         ),
         name="deliver",
-    )(gq, go, small)
+    )(normed, grad, attended, branch, small)
 
 def near_first(here, number):
     high = lax.div(here.z, 2)
@@ -963,19 +1047,6 @@
 
         lax.fori_loop(0, width // TILE, one, 0)
 
-    for copy in fetch_plane(0):
-        copy.start()
-    rounds = Rounds(here, [gather])
-    rounds.service(0)
-    for number in range(DEPTH):
-        if number + 1 < DEPTH:
-            rounds.service(number + 1)
-        gather_third(gather, near_first(here, number))
-        if number + 1 < DEPTH:
-            for copy in fetch_plane(number + 1):
-                copy.start()
-        hidden_units(number)
-
     strips = width // TILE
 
     def fetch_strip(number):
@@ -1044,12 +1115,13 @@
         for copy in again:
             copy.wait()
 
-    fetch_strip(0).start()
     order = [far_first(here, number) for number in range(DEPTH)]
-    steps = [([mids, tables], z, number == DEPTH - 1) for number, z in enumerate(order)]
+    first = [mids, tables]
+    steps = [(first, z, False) for z in [here.z] + order[:-1]]
     steps += [([outs], z, number == DEPTH - 1) for number, z in enumerate(order)]
-    each = strips // DEPTH
-    for number, (items, z, last) in enumerate(steps):
+
+    def begin(number):
+        items, z, last = steps[number]
         if number < DEPTH:
             row_grads(z)
         else:
@@ -1058,23 +1130,52 @@
         for item in items:
             for way in (0, 1):
                 start(item.toss(z, way))
-        if number:
-            for item in steps[number - 1][0]:
-                item.second(steps[number - 1][1])
+
+    def second(number):
+        for item in steps[number][0]:
+            item.second(steps[number][1])
+
+    def third(number):
+        items, z, last = steps[number]
+        for item in items:
+            item.own_part(z) if number == 0 else item.third(z, last)
+
+    for copy in fetch_plane(0):
+        copy.start()
+    rounds = Rounds(here, [gather])
+    rounds.service(0)
+    for number in range(DEPTH):
+        if number + 1 < DEPTH:
+            rounds.service(number + 1)
+        if number == DEPTH - 1:
+            second(0)
+        gather_third(gather, near_first(here, number))
+        if number + 1 < DEPTH:
+            for copy in fetch_plane(number + 1):
+                copy.start()
+        hidden_units(number)
+        if number == 1:
+            begin(0)
+    fetch_strip(0).start()
+    ends = [0] + [strips * (number + 1) // (DEPTH - 1) for number in range(DEPTH - 1)]
+    for number in range(1, 2 * DEPTH):
+        begin(number)
         if number > 1:
-            before, place, final = steps[number - 2]
-            for item in before:
-                item.third(place, final)
+            second(number - 1)
+            third(number - 2)
         if number == DEPTH - 1:
             for copy in again:
                 copy.start()
         if number < DEPTH:
-            tiles_in.run(number * each, (number + 1) * each, grad_in)
+            tiles_in.run(ends[number - 1], ends[number], grad_in)
         elif number == DEPTH:
             again_wait()
             grads_down(True)
         elif number == DEPTH + 1:
             grads_down(False)
+        elif number == DEPTH + 2:
+            for item in first:
+                item.own_rest(here.z)
     outs.second(order[-1])
     outs.third(order[-2], False)
     outs.third(order[-1], True)
@@ -1142,6 +1243,23 @@
         name="experts",
     )(rows, ups, gates, win, wout)
 
+def turn_kernel(source, target):
+    target[...] = source[...].astype(target.dtype)
+
+
+def turn_back(turned, held):
+    planes, rows, columns = turned.shape
+    part = columns // (2 * held)
+    return pl.pallas_call(
+        turn_kernel,
+        out_shape=jax.ShapeDtypeStruct((held, rows, 2 * planes * part), single),
+        grid=(held, 2, planes),
+        in_specs=[pl.BlockSpec((1, rows, part), lambda expert, side, z: (z, 0, side * held + expert))],
+        out_specs=pl.BlockSpec((1, rows, part), lambda expert, side, z: (expert, 0, side * planes + z)),
+        cost_estimate=pl.CostEstimate(flops=0, bytes_accessed=6 * turned.size, transcendentals=0),
+        name="turn",
+    )(turned)
+
 
 def by_kernels():
     return lax.axis_size("dp") == DEPTH and lax.axis_size("expert") == 2 * RING
@@ -1187,23 +1305,9 @@
     rows, columns = total.shape
     cut = total.reshape(DEPTH, rows // DEPTH, columns)
     turned = lax.all_to_all(cut, "dp", split_axis=0, concat_axis=0, tiled=True)
-    part = columns // (2 * held)
-    share = jnp.stack(
-        [
-            jnp.concatenate(
-                [
-                    turned[z, :, (side * held + expert) * part : (side * held + expert + 1) * part]
-                    for side in range(2)
-                    for z in range(DEPTH)
-                ],
-                axis=1,
-            )
-            for expert in range(held)
-        ]
-    )
     down = grad_down.astype(single) + grad_down_other.astype(single)
     return (
-        share.astype(single),
+        turn_back(turned, held),
         down.reshape(held, -1, down.shape[1]),
     )
 
@@ -1240,29 +1344,23 @@
     )
 
 
-def deliver_all(pieces, grad_qkv, grad_out):
+def deliver_all(pieces, normed, grad_qkv, attended, branch):
     owners = lax.axis_size("dp") * lax.axis_size("expert")
     share = pieces.shape[1] // owners
     if by_kernels():
-        lead = (DEPTH, RING, 2)
         small = pieces.reshape(4, owners, share).transpose(1, 0, 2)
-        small = jnp.pad(small, ((0, 0), (0, 4), (0, 128 - share))).reshape(lead + (8, 128))
-        shares, gains = last_sum(
-            grad_qkv.reshape(lead + (-1,) + grad_qkv.shape[1:]),
-            grad_out.reshape(lead + (-1,) + grad_out.shape[1:]),
-            small,
-        )
-        wide = grad_qkv.shape[1]
-        return (
-            gains[:4, :share],
-            shares[:, :wide],
-            shares[:, wide:],
-        )
+        small = jnp.pad(small, ((0, 0), (0, 4), (0, 128 - share))).reshape(DEPTH, RING, 2, 8, 128)
+        share_qkv, share_out, gains = last_sum(normed, grad_qkv, attended, branch, small, share)
+        return (gains[:4, :share], share_qkv, share_out)
     everyone = ("dp", "expert")
     return (
         lax.psum_scatter(pieces, everyone, scatter_dimension=1, tiled=True),
-        lax.psum_scatter(grad_qkv, everyone, scatter_dimension=0, tiled=True).astype(single),
-        lax.psum_scatter(grad_out, everyone, scatter_dimension=0, tiled=True).astype(single),
+        *(
+            lax.psum_scatter(
+                contract_rows(left, right, narrow), everyone, scatter_dimension=0, tiled=True
+            ).astype(single)
+            for left, right in ((normed, grad_qkv), (attended, branch))
+        ),
     )
 
 
@@ -1333,7 +1431,6 @@
     grad_mid, piece_ffn = rms_back(grad_routed, normal_mid, factor_mid, gain_ffn)
     grad_middle = upstream.astype(single) + grad_mid
     grad_branch = grad_middle.astype(narrow)
-    grad_out_part = contract_rows(attended, grad_branch, narrow)
     grad_attended = contract_last(grad_branch, weight_out).astype(narrow).reshape(rows, -1, HEAD)
     grad_probs = jnp.einsum("qhd,khd->hqk", grad_attended, value_rows, preferred_element_type=single)
     inner = jnp.sum(grad_probs * probs, axis=-1, keepdims=True)
@@ -1354,13 +1451,14 @@
     grad_qkv = jnp.concatenate(
         [grad_q_raw, grad_k_raw, grad_value.reshape(rows, model_width)], axis=1
     ).astype(narrow)
-    grad_qkv_part = contract_rows(normed_in, grad_qkv, narrow)
     grad_normed = contract_last(grad_qkv, weight_qkv)
     grad_input, piece_attn = rms_back(grad_normed, normal_in, factor_in, gain_attn)
     grad_tokens = grad_middle + grad_input
 
     pieces = jnp.stack([piece_attn, piece_query, piece_key, piece_ffn])
-    gain_sums, grad_qkv_share, grad_out_share = deliver_all(pieces, grad_qkv_part, grad_out_part)
+    gain_sums, grad_qkv_share, grad_out_share = deliver_all(
+        pieces, normed_in, grad_qkv, attended, grad_branch
+    )
     shape = (micro_count, seq_len, model_width)
     return (
         results.reshape(shape),

time: 792 us -> 759 us (0.958)
  matrix products: 70.2 us -> 51.6 us
  local copies, waits for them, and re-layouts: 27.7 us -> 19 us
  Pallas kernels: 633 us -> 625 us
    dot_general x2 -> x0, matrix products: 18.7 us -> none  [contract_rows(): lax.dot_general(left, right, (((0,), (0,)), ((), ())), preferred_element_...]
    pallas_call x1, Pallas kernels: 240 us -> 223 us  [experts_round(): pl.pallas_call(experts_kernel, out_shape=(jax.ShapeDtypeStruct((block, wi...]
    pallas_call x1 -> x2, Pallas kernels: 153 us -> 162 us  [the longest x1 151 us: last_sum(): pl.pallas_call(last_sum_kernel, out_shape=(jax.ShapeDtypeStruct((share, w...]
  transfers between devices with their start and end apart: 1 -> 1, of which waited for: 0 -> 0; matrix products, arithmetic and copies ran while one was open for 9% -> 7% of each run, Pallas kernels for 19% -> 20%
where the time goes in v5:
time: 759 us; the launch traced here: 749 us
  Pallas kernels  625 us (82%)
  matrix products  51.6 us (7%)
  other arithmetic  32.3 us (4%)
  starting transfers between devices  19.7 us (3%)
  local copies, waits for them, and re-layouts  19 us (3%)
    pallas_call x1, Pallas kernels, first_gather(): pl.pallas_call(first_gather_kernel, out_shape=(whole(wq, True), whole(wo,...  241 us
    pallas_call x1, Pallas kernels, experts_round(): pl.pallas_call(experts_kernel, out_shape=(jax.ShapeDtypeStruct((block, wi...  223 us
    pallas_call x1, Pallas kernels, last_sum(): pl.pallas_call(last_sum_kernel, out_shape=(jax.ShapeDtypeStruct((share, w...  151 us
    dot_general x2, matrix products, contract_last(): lax.dot_general(left, right, (((1,), (1,)), ((), ())), preferred_element_...  20.9 us
    all_to_all x1, starting transfers between devices, return_halves(): turned = lax.all_to_all(cut, 'dp', split_axis=0, concat_axis=0, tiled=True)  19.7 us
  transfers between devices with their start and end apart: 1, of which 0 were waited for; matrix products, arithmetic and copies ran while one was open for 7% of the time, Pallas kernels for 20%

profile of v5, /device:TPU:0, one launch (start us, length us, event | category | flops | bytes accessed | tf_op | source)
XLA Modules:
  0.0 749.4 jit_solution(6214185157046647661)
XLA Ops:
  2.6 1.2 multiply_reduce_fusion.10
  6.8 240.7 %bring.1 = (bf16[4,4,2,64,6144]{4,3,2,1,0:T(8,128)(2,1)}, bf16[4,4,2,64,2048]{4,3,2,1,0:T(8,128)(2,1)}, bf16[4,4,128,2048]{3,2,1,0:T(8,128)(2,1)}, f32[4,4,2,24,...) custom-call(bf16[64,6144]{1,0:T(8,128)(2,1)} %wq.1, bf16[64,2048]{1,0:T(8,128)(2,1)} %wo.1, ...), custom_call_target="tpu_custom_call" | custom-call | tf_op jit(solution)/shard_map/bring/pallas_call | solution.py:524
  248.4 1.0 dynamic-slice_bitcast_fusion
  249.9 1.3 copy.84
  251.5 10.3 %fusion.46 = f32[128,6144]{1,0:T(8,128)S(1)} fusion(bf16[128,2048]{1,0:T(8,128)(2,1)S(1)} %bitcast.146, bf16[2048,6144]{1,0:T(8,128)(2,1)} %bitcast.133), kind=kOutput, calls=%fused_computation.139 | convolution fusion | flops 3221225472 | bytes 28835840 | tf_op jit(solution)/shard_map/dot_general | solution.py:1400
  263.7 2.8 subtract_convert_fusion.1
  266.4 3.3 fusion.45
  269.8 3.4 convolution_convert_fusion.2
  273.2 5.0 multiply_reduce_fusion.7
  278.2 1.1 pad.17.gates
  279.4 0.9 multiply_convert_fusion.4.rows
  280.3 223.2 %experts.1 = (f32[128,2048]{1,0:T(8,128)}, f32[16,128]{1,0:T(8,128)}, f32[128,2048]{1,0:T(8,128)}, bf16[2048,1024]{1,0:T(8,128)(2,1)}, bf16[2048,1024]{1,0:T(8,1...) custom-call(bf16[128,2048]{1,0:T(8,128)(2,1)} %multiply_convert_fusion.4.rows, ...), custom_call_target="tpu_custom_call" | custom-call | tf_op jit(solution)/shard_map/experts/pallas_call | solution.py:1197
  503.5 7.6 %add_convert_fusion = bf16[2048,1024]{1,0:T(8,128)(2,1)} fusion(bf16[2048,1024]{1,0:T(8,128)(2,1)} %get-tuple-element.40, bf16[2048,1024]{1,0:T(8,128)(2,1)} %get-tuple-element.39), kind=kLoop, calls=%fused_computation.1 | loop fusion | flops 8388608 | bytes 12582912 | tf_op jit(solution)/shard_map/convert_element_type | solution.py:1304
  511.1 19.7 %all-to-all-start = ((bf16[4,512,1024]{2,1,0:T(8,128)(2,1)}), bf16[4,512,1024]{2,1,0:T(8,128)(2,1)}, u32[]{:S(2)}, u32[]{:S(2)}) async-start(bf16[4,512,1024]{2,1,0:T(8,128)(2,1)} %bitcast.135), calls=%async_computation | async-start | bytes 8388608 | tf_op jit(solution)/shard_map/all_to_all | solution.py:1307
  530.9 2.1 copy.107.attended
  534.6 6.3 convolution_convert_fusion
  540.9 1.0 copy.113
  541.9 3.8 convolution_convert_fusion.1
  545.7 1.8 multiply_reduce_fusion.5
  547.8 1.4 fusion.3
  549.2 1.5 fusion.4
  551.5 2.0 copy.108
  553.6 2.9 multiply_subtract_fusion.1
  557.4 1.9 multiply_convert_fusion.2
  559.3 14.6 %multiply_reduce_fusion.1 = (f32[2048]{0:T(1024)S(1)}, f32[128]{0:T(128)S(1)}, bf16[128,2048]{1,0:T(8,128)(2,1)}, f32[128,2048]{1,0:T(8,128)}) fusion(bf16[2,64,2048]{2,1,0:T(8,128)(2,1)} %param.13, f32[128]{0:T(128)S(1)} %rsqrt.40, f32[2048]{0:T(1024)S(1)} %mul.395, bf16[2048,6144]{1,0:T(8,128)(2,1)} %bitcast.134, bf16[128,2048]{1,0:T(8,128)(2,1)} %copy.108, ...), kind=kOutput, calls=%fused_computation.27 | convolution fusion | flops 3228301312 | bytes 28853248 | tf_op jit(solution)/shard_map/dot_general | solution.py:65
  574.9 2.4 pad_maximum_fusion.grad
  577.4 150.7 %deliver.1 = (f32[64,6144]{1,0:T(8,128)}, f32[64,2048]{1,0:T(8,128)}, f32[8,128]{1,0:T(8,128)}) custom-call(bf16[128,2048]{1,0:T(8,128)(2,1)} %get-tuple-element.101.normed, bf16[128,6144]{1,0:T(8,128)(2,1)} %pad_maximum_fusion.grad, bf16[128,2048]{1,0:T(8,128)(2,1)} %copy.107.attended, bf16[128,2048]{1,0:T(8,128)(2,1)} %copy-done.8, ...), custom_call_target="tpu_custom_call" | custom-call | tf_op jit(solution)/shard_map/deliver/pallas_call | solution.py:880
  728.0 1.4 slice_bitcast_fusion.1
  729.4 3.8 multiply_add_fusion
  733.2 2.8 convert_add_fusion
  736.0 10.9 %turn.1 = f32[2,512,2048]{2,1,0:T(8,128)} custom-call(bf16[4,512,1024]{2,1,0:T(8,128)(2,1)} %all-to-all-done.source), custom_call_target="tpu_custom_call" | custom-call | bytes 12582912 | tf_op jit(solution)/shard_map/turn/pallas_call | solution.py:1253
  747.0 1.1 copy.145
  (100 shorter events, 13.9 us)
Async XLA Ops:
  6.8 244.5 %copy-start.5 = (bf16[2,64,2048]{2,1,0:T(8,128)(2,1)S(1)}, bf16[2,64,2048]{2,1,0:T(8,128)(2,1)}, u32[]{:S(2)}) copy-start(bf16[2,64,2048]{2,1,0:T(8,128)(2,1)} %param.13) | copy-start | bytes 1572868
  261.8 8.0 %copy-start = (f32[128,6144]{1,0:T(8,128)}, f32[128,6144]{1,0:T(8,128)S(1)}, u32[]{:S(2)}) copy-start(f32[128,6144]{1,0:T(8,128)S(1)} %fusion.46) | copy-start | bytes 9437188
  273.2 5.0 copy-start.9
  278.2 255.2 %copy-start.2 = (f32[128,2048]{1,0:T(8,128)}, f32[128,2048]{1,0:T(8,128)S(1)}, u32[]{:S(2)}) copy-start(f32[128,2048]{1,0:T(8,128)S(1)} %get-tuple-element.116) | copy-start | bytes 3145732
  511.1 22.0 %copy-start.4 = (f32[128,2048]{1,0:T(8,128)S(1)}, f32[128,2048]{1,0:T(8,128)}, u32[]{:S(2)}) copy-start(f32[128,2048]{1,0:T(8,128)} %get-tuple-element.34) | copy-start | bytes 3145732
  511.1 224.9 %all-to-all-start = ((bf16[4,512,1024]{2,1,0:T(8,128)(2,1)}), bf16[4,512,1024]{2,1,0:T(8,128)(2,1)}, u32[]{:S(2)}, u32[]{:S(2)}) async-start(bf16[4,512,1024]{2,1,0:T(8,128)(2,1)} %bitcast.135), calls=%async_computation | async-start | bytes 8388608 | tf_op jit(solution)/shard_map/all_to_all | solution.py:1307
  530.8 2.6 copy-start.7
  533.8 0.8 copy-start.8
  541.9 3.8 copy-start.1
  545.7 1.9 copy-start.19
  545.7 2.1 copy-start.12
  545.7 2.1 copy-start.13
  547.5 1.7 copy-start.10
  547.5 1.7 copy-start.11
  547.8 3.0 copy-start.21
  559.3 15.6 %copy-start.14 = (bf16[128,2048]{1,0:T(8,128)(2,1)S(1)}, bf16[128,2048]{1,0:T(8,128)(2,1)}, u32[]{:S(2)}) copy-start(bf16[128,2048]{1,0:T(8,128)(2,1)} %copy.108) | copy-start | bytes 1572868
  559.3 15.6 %copy-start.17 = (bf16[128,2048]{1,0:T(8,128)(2,1)S(1)}, bf16[128,2048]{1,0:T(8,128)(2,1)}, u32[]{:S(2)}) copy-start(bf16[128,2048]{1,0:T(8,128)(2,1)} %get-tuple-element.83) | copy-start | bytes 1572868
  574.9 154.5 %copy-start.3 = (f32[128,2048]{1,0:T(8,128)S(1)}, f32[128,2048]{1,0:T(8,128)}, u32[]{:S(2)}) copy-start(f32[128,2048]{1,0:T(8,128)} %copy-done.2) | copy-start | bytes 3145732
  574.9 154.5 %copy-start.6 = (bf16[2,64,2048]{2,1,0:T(8,128)(2,1)S(1)}, bf16[2,64,2048]{2,1,0:T(8,128)(2,1)}, u32[]{:S(2)}) copy-start(bf16[2,64,2048]{2,1,0:T(8,128)(2,1)} %param.13) | copy-start | bytes 1572868
  729.4 3.8 copy-start.15
  729.4 3.8 copy-start.16
  736.0 10.9 %copy-start.18 = (f32[64,6144]{1,0:T(8,128)S(1)}, f32[64,6144]{1,0:T(8,128)}, u32[]{:S(2)}) copy-start(f32[64,6144]{1,0:T(8,128)} %get-tuple-element.139) | copy-start | bytes 4718596
  746.9 1.4 copy-start.20

commit v6 on v5

--- a/solution.py
+++ b/solution.py
@@ -316,7 +316,7 @@
         pl.when(here.z >= step)(lambda: body(here.z - step, 0))
         pl.when(here.z + step < DEPTH)(lambda: body(here.z + step, 1))
 
-    def service(self, step):
+    def service(self, step, between=None):
         items, here = self.items, self.here
 
         def first(z, way):
@@ -338,6 +338,8 @@
 
         if step + 1 < DEPTH:
             self.places(step + 1, first)
+        if between is not None:
+            between()
         if step == 0:
             for item in items:
                 item.keep().wait()
@@ -504,10 +506,8 @@
     recut = Recut(here, ein, eout, win, wout, sems[16:20])
     rounds = Rounds(here, items)
     for step in range(DEPTH):
-        rounds.service(step)
-        if step == 0:
-            recut.begin()
-        else:
+        rounds.service(step, recut.begin if step == 1 else None)
+        if step:
             rounds.third(step - 1)
     rounds.third(DEPTH - 1)
     recut.relay()
@@ -538,6 +538,9 @@
         name="bring",
     )(wq, wo, up, small, ein, eout)
 
+TILE = 256
+
+
 def add_up(target, terms, rows, columns):
     high = 16 if rows % 16 == 0 else 8
     wide = min(columns, 1024)
@@ -781,8 +784,74 @@
     return low + high * (DEPTH - 1 - 2 * low)
 
 
+class Share:
+    def __init__(self, here, source, target, sems):
+        self.here, self.source, self.target, self.sems = here, source, target, sems
+        self.held, self.rows, columns = target.shape
+        self.part = columns // (2 * DEPTH)
+
+    def pieces(self, steps, arriving):
+        here = self.here
+        origin = lax.rem(here.z + DEPTH - steps, DEPTH) if arriving else here.z
+        away = lax.rem(here.z + steps, DEPTH)
+        copies = []
+        for number in range(2 * self.held):
+            side, expert = divmod(number, self.held)
+            column = (side * DEPTH + origin) * self.part
+            target = self.target.at[expert, :, pl.ds(pl.multiple_of(column, 128), self.part)]
+            source = self.source.at[
+                pl.ds(pl.multiple_of(away * self.rows, 16), self.rows), pl.ds(number * self.part, self.part)
+            ]
+            if steps == 0:
+                copies.append(pltpu.make_async_copy(source, target, self.sems.at[0, 0, number]))
+            else:
+                sems = (self.sems.at[0, steps, number], self.sems.at[1, steps, number])
+                copies.append(remote(target if arriving else source, target, *sems, here.above(steps)))
+        return copies
+
+    def begin(self):
+        for steps in range(DEPTH):
+            for copy in self.pieces(steps, False):
+                copy.start()
+
+    def end(self):
+        for steps in range(DEPTH):
+            for copy in self.pieces(steps, False):
+                copy.wait() if steps == 0 else copy.wait_send()
+            if steps:
+                for copy in self.pieces(steps, True):
+                    copy.wait_recv()
+
+
 def last_sum_kernel(
-    normed, grad, attended, branch, small, q_sum, o_sum, small_sum, left, left_out, right, sems, *scratch
+    normed,
+    grad,
+    attended,
+    branch,
+    gin_sum,
+    weight,
+    tokens,
+    grad_middle,
+    gain,
+    pieces,
+    q_sum,
+    o_sum,
+    gains,
+    grad_tokens,
+    share_in,
+    left,
+    left_out,
+    right,
+    sems,
+    panel,
+    panel_sems,
+    back,
+    piece,
+    few_sum,
+    few_other,
+    pair_sems,
+    share_sems,
+    *scratch,
 ):
     here = Here()
     here.meet()
@@ -808,13 +877,21 @@
     for kept, sent in copies:
         sent.start()
         kept.start()
+    back_share = Share(here, gin_sum, share_in, share_sems)
+    back_share.begin()
     targets = [(q_sum.at[:, pl.ds(side * width, width)], side * share, share) for side in range(sides)]
     targets.append((o_sum, sides * share, share))
     big = Sum(here, None, targets, halves_of((sides + 1) * share), False, scratch[0:8])
-    few = Sum(here, [small], small_sum, halves_of(small.shape[3], False), True, scratch[8:18])
+    few = Sum(here, None, few_sum, halves_of(few_sum.shape[0], False), False, scratch[8:16])
     order = [far_first(here, number) for number in range(DEPTH)]
-    for z in order:
-        few.begin(z)
+
+    def fetch_panel(number):
+        slot = lax.rem(number, 2)
+        rows = pl.ds(pl.multiple_of(number * TILE, TILE), TILE)
+        return pltpu.make_async_copy(weight.at[rows], panel.at[slot], panel_sems.at[slot])
+
+    panels = width // TILE
+    fetch_panel(0).start()
     for kept, sent in copies:
         kept.wait()
         sent.wait_recv()
@@ -825,7 +902,7 @@
     def make(z):
         at = pl.ds(pl.multiple_of(z * rows, rows), rows)
 
-        def piece(number, source):
+        def one(number, source):
             spot = pl.ds(pl.multiple_of(number * step, step), step)
             turned = source[:, :, at].reshape(2 * block, rows)
             made = contract_rows(turned, right[:, :, spot].reshape(2 * block, step))
@@ -837,77 +914,127 @@
                 big.mine[z, chip, pl.ds(row, share), pl.ds(column, step)] = mine[chip]
 
         def qkv(number, carry):
-            piece(number, left)
+            one(number, left)
             return carry
 
         def out(number, carry):
-            piece(number, left_out)
+            one(number, left_out)
             return carry
 
         lax.fori_loop(0, sides * each, qkv, 0)
         lax.fori_loop(sides * each, (sides + 1) * each, out, 0)
 
-    items = [big, few]
+    def through(first, last):
+        def body(number, carry):
+            fetch_panel(number).wait()
+            pl.when(number + 1 < panels)(lambda: fetch_panel(number + 1).start())
+            spot = pl.ds(pl.multiple_of(number * TILE, TILE), TILE)
+            back[:, spot] = contract_last(right[0, :, 0:wide], panel[lax.rem(number, 2)])
+            return carry
+
+        lax.fori_loop(first, last, body, 0)
+
+    def norm_back():
+        piece[...] = pieces[...]
+        high = 16
+
+        def body(number, carry):
+            at = pl.ds(pl.multiple_of(number * high, high), high)
+            values = tokens[at].astype(single)
+            factor = lax.rsqrt(jnp.mean(values * values, axis=-1, keepdims=True) + epsilon)
+            normal = values * factor
+            upstream = back[at]
+            weighted = upstream * gain[...]
+            inner = jnp.mean(weighted * normal, axis=-1, keepdims=True)
+            grad_tokens[at] = grad_middle[at] + factor * (weighted - normal * inner)
+            piece[0:1] += jnp.sum(upstream * normal, axis=0, keepdims=True)
+            return carry
+
+        lax.fori_loop(0, block // high, body, 0)
+        for z in range(DEPTH):
+            for chip in range(RING):
+                begin = (z * RING + chip) * 2 * share
+                few.mine[z, chip] = piece[:, begin : begin + 2 * share]
+
     for number, z in enumerate(order):
         make(z)
         for way in (0, 1):
             start(big.toss(z, way))
-        few.merge(z)
         if number:
-            for item in items:
-                item.second(order[number - 1])
+            big.second(order[number - 1])
         if number > 1:
-            for item in items:
-                item.third(order[number - 2], False)
-    for item in items:
-        item.second(order[-1])
-    for item in items:
-        item.third(order[-2], False)
-    for item in items:
-        item.third(order[-1], True)
+            big.third(order[number - 2], False)
+        if number < 2:
+            through(number * panels // 2, (number + 1) * panels // 2)
+        if number == 2:
+            norm_back()
+            for place in order:
+                start(few.toss(place, 0))
+    big.second(order[-1])
+    for z in order:
+        few.second(z)
+    big.third(order[-2], False)
+    for z in order[:-1]:
+        few.third(z, False)
+    big.third(order[-1], True)
+    few.third(order[-1], True)
+    swap = remote(few_sum, few_other, pair_sems.at[0], pair_sems.at[1], here.sibling())
+    swap.start()
+    swap.wait_recv()
+    gains[...] = few_sum[...] + few_other[...]
+    swap.wait_send()
     for number, z in enumerate(order):
-        for item in items:
+        for item in (big, few):
             item.end(z, number == DEPTH - 1)
     for kept, sent in copies:
         sent.wait_send()
-
-
-def last_sum(normed, grad, attended, branch, small, share):
+    back_share.end()
+
+
+def last_sum(normed, grad, attended, branch, gin_sum, weight, tokens, grad_middle, gain, pieces, share, held):
     block, width = normed.shape
     wide = grad.shape[1]
     rows = (wide // width + 1) * share
     vmem = pl.BlockSpec(memory_space=pltpu.VMEM)
+    few = (pieces.shape[0], 2 * share)
     return pl.pallas_call(
         last_sum_kernel,
         out_shape=(
             jax.ShapeDtypeStruct((share, wide), single),
             jax.ShapeDtypeStruct((share, width), single),
-            jax.ShapeDtypeStruct(small.shape[3:], single),
+            jax.ShapeDtypeStruct(few, single),
+            jax.ShapeDtypeStruct((block, width), single),
+            jax.ShapeDtypeStruct((held, gin_sum.shape[0] // DEPTH, DEPTH * gin_sum.shape[1] // held), narrow),
         ),
-        in_specs=[HBM] * 5,
-        out_specs=(vmem, vmem, vmem),
+        in_specs=[HBM] * 6 + [vmem] * 4,
+        out_specs=(vmem, vmem, vmem, vmem, HBM),
         scratch_shapes=[
             pltpu.VMEM((2, block, width), narrow),
             pltpu.VMEM((2, block, width), narrow),
             pltpu.VMEM((2, block, wide + width), narrow),
             pltpu.SemaphoreType.DMA((12,)),
+            pltpu.VMEM((2, TILE, wide), narrow),
+            pltpu.SemaphoreType.DMA((2,)),
+            pltpu.VMEM((block, width), single),
+            pltpu.VMEM(pieces.shape, single),
+            pltpu.VMEM(few, single),
+            pltpu.VMEM(few, single),
+            pltpu.SemaphoreType.DMA((2,)),
+            pltpu.SemaphoreType.DMA((2, DEPTH, 2 * held)),
         ]
         + sum_scratch(rows, width, narrow, halves_of(rows), made=True)
-        + sum_scratch(small.shape[3], small.shape[4], single, halves_of(small.shape[3], False), paired=True),
+        + sum_scratch(few[0], few[1], single, halves_of(few[0], False), made=True),
         compiler_params=pltpu.CompilerParams(
             collective_id=4, has_side_effects=True, vmem_limit_bytes=62 * 2**20
         ),
         name="deliver",
-    )(normed, grad, attended, branch, small)
+    )(normed, grad, attended, branch, gin_sum, weight, tokens, grad_middle, gain, pieces)
 
 def near_first(here, number):
     high = lax.div(here.z, 2)
     inner = lax.rem(lax.div(here.z + 1, 2), 2)
     low = number + inner * (1, -1, 0, 0)[number]
     return low + high * (DEPTH - 1 - 2 * low)
-
-
-TILE = 256
 
 
 class Tiles:
@@ -954,7 +1081,7 @@
 
 
 def experts_kernel(
-    rows, ups, gates, win, wout, mid_sum, gate_sum, out_sum, gin, gin_other, gdown, gdown_other, rows_all, *scratch
+    rows, ups, gates, win, wout, mid_sum, gate_sum, out_sum, gin_sum, gdown, gdown_other, gin, gin_other, rows_all, *scratch
 ):
     here = Here()
     here.meet()
@@ -1106,6 +1233,44 @@
         for number in range(first, first + tall // 2):
             copy = grad_down_store(number, away)
             copy.wait_send() if away else copy.wait()
+
+    def add_cores():
+        half = hidden
+        adds, puts = scratch[43], scratch[44]
+
+        def fetch(number):
+            slot = lax.rem(number, 2)
+            at = pl.ds(pl.multiple_of(number * TILE, TILE), TILE)
+            return [
+                pltpu.make_async_copy(
+                    source.at[at], stage.at[slot, :, pl.ds(side * half, half)], adds.at[slot, side]
+                )
+                for side, source in enumerate((gin, gin_other))
+            ]
+
+        def put(number):
+            slot = lax.rem(number, 2)
+            at = pl.ds(pl.multiple_of(number * TILE, TILE), TILE)
+            return pltpu.make_async_copy(stage.at[slot, :, pl.ds(0, half)], gin_sum.at[at], puts.at[slot])
+
+        def start_fetch(number):
+            for copy in fetch(number):
+                copy.start()
+
+        def body(number, carry):
+            for copy in fetch(number):
+                copy.wait()
+            pl.when(number >= 1)(lambda: put(number - 1).wait())
+            pl.when(number + 1 < strips)(lambda: start_fetch(number + 1))
+            slot = lax.rem(number, 2)
+            own = stage.at[slot, :, pl.ds(0, half)]
+            add_up(own, [own, stage.at[slot, :, pl.ds(half, half)]], TILE, half)
+            put(number).start()
+            return carry
+
+        start_fetch(0)
+        lax.fori_loop(0, strips, body, 0)
+        put(strips - 1).wait()
 
     again = [
         pltpu.make_async_copy(ups.at[z], w_in.at[pl.ds(z * plane, plane)], loads.at[7 + z]) for z in range(DEPTH)
@@ -1176,13 +1341,14 @@
         elif number == DEPTH + 2:
             for item in first:
                 item.own_rest(here.z)
+            tiles_in.heard()
+            add_cores()
     outs.second(order[-1])
     outs.third(order[-2], False)
     outs.third(order[-1], True)
     for number, z in enumerate(order):
         outs.end(z, number == DEPTH - 1)
         tables.end(z, number == DEPTH - 1)
-    tiles_in.heard()
     for number in range(tall // 2):
         grad_down_store(number, True).wait_recv()
     rounds.finish()
@@ -1201,13 +1367,14 @@
             jax.ShapeDtypeStruct((experts, block), single),
             jax.ShapeDtypeStruct((block, width), single),
             jax.ShapeDtypeStruct((width, hidden), narrow),
-            jax.ShapeDtypeStruct((width, hidden), narrow),
             jax.ShapeDtypeStruct((hidden // 2, width), narrow),
             jax.ShapeDtypeStruct((hidden // 2, width), narrow),
+            jax.ShapeDtypeStruct((width, hidden), narrow),
+            jax.ShapeDtypeStruct((width, hidden), narrow),
             jax.ShapeDtypeStruct((DEPTH, RING, block, width), narrow),
         ),
         in_specs=[HBM] * 5,
-        out_specs=(vmem, vmem, vmem) + (HBM,) * 5,
+        out_specs=(vmem, vmem, vmem) + (HBM,) * 6,
         scratch_shapes=[
             pltpu.VMEM((width, 2 * hidden), narrow),
             pltpu.VMEM((hidden, width), narrow),
@@ -1236,29 +1403,13 @@
             pltpu.SemaphoreType.DMA((2, 1)),
             pltpu.SemaphoreType.DMA((2, 1)),
             pltpu.SemaphoreType.DMA((hidden // TILE, 1)),
-        ],
+        ]
+        + [pltpu.SemaphoreType.DMA((2, 2)), pltpu.SemaphoreType.DMA((2,))],
         compiler_params=pltpu.CompilerParams(
             collective_id=2, has_side_effects=True, vmem_limit_bytes=62 * 2**20
         ),
         name="experts",
     )(rows, ups, gates, win, wout)
-
-def turn_kernel(source, target):
-    target[...] = source[...].astype(target.dtype)
-
-
-def turn_back(turned, held):
-    planes, rows, columns = turned.shape
-    part = columns // (2 * held)
-    return pl.pallas_call(
-        turn_kernel,
-        out_shape=jax.ShapeDtypeStruct((held, rows, 2 * planes * part), single),
-        grid=(held, 2, planes),
-        in_specs=[pl.BlockSpec((1, rows, part), lambda expert, side, z: (z, 0, side * held + expert))],
-        out_specs=pl.BlockSpec((1, rows, part), lambda expert, side, z: (expert, 0, side * planes + z)),
-        cost_estimate=pl.CostEstimate(flops=0, bytes_accessed=6 * turned.size, transcendentals=0),
-        name="turn",
-    )(turned)
 
 
 def by_kernels():
@@ -1299,19 +1450,6 @@
     )
 
 
-def return_halves(half_way, held):
-    grad_in, grad_in_other, grad_down, grad_down_other = half_way
-    total = (grad_in.astype(single) + grad_in_other.astype(single)).astype(narrow)
-    rows, columns = total.shape
-    cut = total.reshape(DEPTH, rows // DEPTH, columns)
-    turned = lax.all_to_all(cut, "dp", split_axis=0, concat_axis=0, tiled=True)
-    down = grad_down.astype(single) + grad_down_other.astype(single)
-    return (
-        turn_back(turned, held),
-        down.reshape(held, -1, down.shape[1]),
-    )
-
-
 def experts_all(routed_in, up_rows, every_gate, weight_in, weight_down, held):
     depth = lax.axis_size("dp")
     owners = lax.axis_size("expert")
@@ -1325,10 +1463,11 @@
     if by_kernels():
         gate = jnp.pad(gate.reshape(DEPTH, -1, chip_experts), ((0, 0), (0, 0), (0, 128 - chip_experts)))
         ups = up_rows.reshape(DEPTH, -1, width)
-        grad_routed, table, mixture, *half_way, _ = experts_round(
+        grad_routed, table, mixture, grad_in, grad_down, grad_down_other = experts_round(
             routed_in, ups, gate, weight_in, weight_down, experts
-        )
-        return (mixture, grad_routed, table, return_halves(half_way, held))
+        )[:6]
+        down = grad_down.astype(single) + grad_down_other.astype(single)
+        return (mixture, grad_routed, table, (grad_in, down.reshape(held, -1, width)))
     mid_rows = gather_alike(routed_in).reshape(-1, width)
     out, mid, served, grad_in, grad_down = expert_rounds(
         mid_rows, up_rows, gate.reshape(-1, chip_experts), weight_in, weight_down
@@ -1340,27 +1479,34 @@
         scatter_alike(out.reshape(depth, chips, rows, width)).astype(single),
         scatter_alike(mid.reshape(depth, chips, rows, width)).astype(single),
         scatter_alike(spread),
-        [share.astype(single) for share in return_weights(grad_in, grad_down, held)],
+        return_weights(grad_in, grad_down, held),
     )
 
 
-def deliver_all(pieces, normed, grad_qkv, attended, branch):
+def deliver_all(tokens, gain, grad_middle, pieces, normed, grad_qkv, weight_qkv, attended, branch, share_in, held):
     owners = lax.axis_size("dp") * lax.axis_size("expert")
-    share = pieces.shape[1] // owners
+    share = gain.shape[0] // owners
     if by_kernels():
-        small = pieces.reshape(4, owners, share).transpose(1, 0, 2)
-        small = jnp.pad(small, ((0, 0), (0, 4), (0, 128 - share))).reshape(DEPTH, RING, 2, 8, 128)
-        share_qkv, share_out, gains = last_sum(normed, grad_qkv, attended, branch, small, share)
-        return (gains[:4, :share], share_qkv, share_out)
+        rows = jnp.stack([jnp.zeros_like(gain), *pieces] + [jnp.zeros_like(gain)] * (7 - len(pieces)))
+        share_qkv, share_out, gains, grad_tokens, share_in = last_sum(
+            normed, grad_qkv, attended, branch, share_in, weight_qkv, tokens, grad_middle, gain[None], rows, share, held
+        )
+        core = lax.rem(lax.axis_index("expert"), 2)
+        gains = lax.dynamic_slice_in_dim(gains, core * share, share, axis=1)
+        return (grad_tokens, gains, share_qkv, share_out, share_in.astype(single))
     everyone = ("dp", "expert")
+    normal, factor = normalize(tokens.astype(single))
+    grad_input, piece = rms_back(contract_last(grad_qkv, weight_qkv), normal, factor, gain)
     return (
-        lax.psum_scatter(pieces, everyone, scatter_dimension=1, tiled=True),
+        grad_middle + grad_input,
+        lax.psum_scatter(jnp.stack([piece, *pieces]), everyone, scatter_dimension=1, tiled=True),
         *(
             lax.psum_scatter(
                 contract_rows(left, right, narrow), everyone, scatter_dimension=0, tiled=True
             ).astype(single)
             for left, right in ((normed, grad_qkv), (attended, branch))
         ),
+        share_in.astype(single),
     )
 
 
@@ -1451,13 +1597,18 @@
     grad_qkv = jnp.concatenate(
         [grad_q_raw, grad_k_raw, grad_value.reshape(rows, model_width)], axis=1
     ).astype(narrow)
-    grad_normed = contract_last(grad_qkv, weight_qkv)
-    grad_input, piece_attn = rms_back(grad_normed, normal_in, factor_in, gain_attn)
-    grad_tokens = grad_middle + grad_input
-
-    pieces = jnp.stack([piece_attn, piece_query, piece_key, piece_ffn])
-    gain_sums, grad_qkv_share, grad_out_share = deliver_all(
-        pieces, normed_in, grad_qkv, attended, grad_branch
+    grad_tokens, gain_sums, grad_qkv_share, grad_out_share, share_in = deliver_all(
+        tokens.reshape(rows, model_width),
+        gain_attn,
+        grad_middle,
+        (piece_query, piece_key, piece_ffn),
+        normed_in,
+        grad_qkv,
+        weight_qkv,
+        attended,
+        grad_branch,
+        share_in,
+        held,
     )
     shape = (micro_count, seq_len, model_width)
     return (
@@ -1471,7 +1622,7 @@
         grad_out_share,
         gain_sums[3],
         share_in,
-        share_down,
+        share_down.astype(single),
     )
 
 

time: 759 us -> 718 us (0.946)
  starting transfers between devices: 19.7 us -> 0 us
  matrix products: 51.6 us -> 34.9 us
    pallas_call x1, Pallas kernels: 151 us -> 182 us  [last_sum(): pl.pallas_call(last_sum_kernel, out_shape=(jax.ShapeDtypeStruct((share, w...]
    all_to_all x1 -> x0, starting transfers between devices: 19.7 us -> none  [return_halves(): turned = lax.all_to_all(cut, 'dp', split_axis=0, concat_axis=0, tiled=True)]
    pallas_call x1, Pallas kernels: 241 us -> 221 us  [first_gather(): pl.pallas_call(first_gather_kernel, out_shape=(whole(wq, True), whole(wo,...]
    dot_general x2 -> x1, matrix products: 20.9 us -> 7.24 us  [contract_last(): lax.dot_general(left, right, (((1,), (1,)), ((), ())), preferred_element_...]
    pallas_call x1 -> x0, Pallas kernels: 10.9 us -> none  [turn_back(): pl.pallas_call(turn_kernel, out_shape=jax.ShapeDtypeStruct((held, rows, 2...]
  transfers between devices with their start and end apart: 1 -> 0, of which waited for: 0 -> 0; matrix products, arithmetic and copies ran while one was open for 7% -> 0% of each run, Pallas kernels for 20% -> 0%
where the time goes in v6:
time: 718 us; the launch traced here: 714 us
  Pallas kernels  627 us (87%)
  matrix products  34.9 us (5%)
  other arithmetic  31 us (4%)
  local copies, waits for them, and re-layouts  19.7 us (3%)
    pallas_call x1, Pallas kernels, experts_round(): pl.pallas_call(experts_kernel, out_shape=(jax.ShapeDtypeStruct((block, wi...  224 us
    pallas_call x1, Pallas kernels, first_gather(): pl.pallas_call(first_gather_kernel, out_shape=(whole(wq, True), whole(wo,...  221 us
    pallas_call x1, Pallas kernels, last_sum(): pl.pallas_call(last_sum_kernel, out_shape=(jax.ShapeDtypeStruct((share, w...  182 us

profile of v6, /device:TPU:0, one launch (start us, length us, event | category | flops | bytes accessed | tf_op | source)
XLA Modules:
  0.0 714.1 jit_solution(2170650292023563791)
XLA Ops:
  0.6 0.7 copy.74
  2.2 0.7 fusion.33
  3.6 221.2 %bring.1 = (bf16[4,4,2,64,6144]{4,3,2,1,0:T(8,128)(2,1)}, bf16[4,4,2,64,2048]{4,3,2,1,0:T(8,128)(2,1)}, bf16[4,4,128,2048]{3,2,1,0:T(8,128)(2,1)}, f32[4,4,2,24,...) custom-call(bf16[64,6144]{1,0:T(8,128)(2,1)} %wq.1, bf16[64,2048]{1,0:T(8,128)(2,1)} %wo.1, ...), custom_call_target="tpu_custom_call" | custom-call | tf_op jit(solution)/shard_map/bring/pallas_call | solution.py:524
  224.8 0.9 slice_bitcast_fusion
  226.4 10.2 %fusion.50 = f32[128,6144]{1,0:T(8,128)S(1)} fusion(bf16[128,2048]{1,0:T(8,128)(2,1)S(1)} %bitcast.132, bf16[2048,6144]{1,0:T(8,128)(2,1)} %bitcast.118), kind=kOutput, calls=%fused_computation.137 | convolution fusion | flops 3221225472 | bytes 28835840 | tf_op jit(solution)/shard_map/dot_general | solution.py:1546
  237.5 1.7 fusion.48
  239.3 1.6 fusion.47
  241.7 4.8 subtract_convert_fusion.1
  246.7 3.3 fusion.49
  250.1 3.4 convolution_convert_fusion.2
  253.5 5.0 multiply_reduce_fusion.5
  258.5 1.0 multiply_convert_fusion.3.rows
  259.9 1.0 pad.13.gates
  261.0 223.9 %experts.1 = (f32[128,2048]{1,0:T(8,128)}, f32[16,128]{1,0:T(8,128)}, f32[128,2048]{1,0:T(8,128)}, bf16[2048,1024]{1,0:T(8,128)(2,1)}, bf16[512,2048]{1,0:T(8,12...) custom-call(bf16[128,2048]{1,0:T(8,128)(2,1)} %multiply_convert_fusi, ...), custom_call_target="tpu_custom_call" | custom-call | tf_op jit(solution)/shard_map/experts/pallas_call | solution.py:1363
  484.9 5.2 convert_add_fusion
  490.5 1.5 fusion.46
  492.0 0.8 copy-done.8
  492.8 7.2 %convolution_convert_fusion = bf16[128,2048]{1,0:T(8,128)(2,1)} fusion(bf16[128,2048]{1,0:T(8,128)(2,1)S(1)} %get-tuple-element.83.branch, bf16[2048,2048]{1,0:T(8,128)(2,1)} %bitcast.121), kind=kOutput, calls=%fused_computation.3 | convolution fusion | flops 1074003968 | bytes 9437184 | tf_op jit(solution)/shard_map/dot_general | solution.py:65
  500.0 2.0 copy.113
  502.1 1.8 multiply_reduce_fusion.3
  505.7 1.0 multiply_subtract_fusion.1
  506.7 0.9 fusion.11
  509.4 4.1 multiply_convert_fusion.1
  513.5 2.9 convolution_convert_fusion.1
  516.7 1.3 pad_maximum_fusion.grad
  517.9 1.0 copy.107.attended
  519.0 1.0 fusion.7.normed
  520.7 182.2 %deliver.1 = (f32[64,6144]{1,0:T(8,128)}, f32[64,2048]{1,0:T(8,128)}, f32[8,128]{1,0:T(8,128)}, f32[128,2048]{1,0:T(8,128)}, bf16[2,512,2048]{2,1,0:T(8,128)(2,1)}) custom-call(bf16[128,2048]{1,0:T(8,128)(2,1)} %fusion.7.normed, bf16[128,6144]{1,0:T(8,128)(2,1)} %pad_maximum_fusion.grad, bf16[128,2048]{1,0:T(8,128)(2,1)} %copy.107.attended, ...), custom_call_target="tpu_custom_call" | custom-call | tf_op jit(solution)/shard_map/deliver/pallas_call | solution.py:1000
  702.9 6.7 convert_element_type.94
  711.0 1.0 copy.146
  712.0 1.1 copy.147
  713.1 0.8 copy.148
  (105 shorter events, 10.8 us)
Async XLA Ops:
  3.6 222.5 %copy-start.2 = (bf16[2,64,2048]{2,1,0:T(8,128)(2,1)S(1)}, bf16[2,64,2048]{2,1,0:T(8,128)(2,1)}, u32[]{:S(2)}) copy-start(bf16[2,64,2048]{2,1,0:T(8,128)(2,1)} %param.13) | copy-start | bytes 1572868
  236.6 13.4 %copy-start = (f32[128,6144]{1,0:T(8,128)}, f32[128,6144]{1,0:T(8,128)S(1)}, u32[]{:S(2)}) copy-start(f32[128,6144]{1,0:T(8,128)S(1)} %fusion.50) | copy-start | bytes 9437188
  239.2 1.8 copy-start.25
  253.4 6.0 copy-start.23
  484.9 5.2 copy-start.9
  484.9 5.6 copy-start.11
  484.9 5.6 copy-start.19
  492.0 0.8 copy-start.8
  492.8 9.3 %copy-start.1 = (f32[128,6144]{1,0:T(8,128)S(1)}, f32[128,6144]{1,0:T(8,128)}, u32[]{:S(2)}) copy-start(f32[128,6144]{1,0:T(8,128)} %copy-done) | copy-start | bytes 9437188
  502.1 1.9 copy-start.20
  502.1 2.1 copy-start.12
  502.1 2.1 copy-start.13
  503.9 1.1 copy-start.14
  503.9 1.2 copy-start.15
  506.7 1.1 copy-start.4
  506.7 1.3 copy-start.5
  506.7 1.6 copy-start.6
  506.7 2.0 copy-start.7
  513.5 3.2 copy-start.16
  513.5 3.2 copy-start.17
  516.4 1.5 copy-start.10
  516.4 2.6 copy-start.3
  702.9 6.8 copy-start.26
  702.9 7.4 %copy-start.24 = (f32[16,128]{1,0:T(8,128)S(1)}, f32[16,128]{1,0:T(8,128)}, u32[]{:S(2)}) copy-start(f32[16,128]{1,0:T(8,128)} %get-tuple-element.38) | copy-start | bytes 24580
  702.9 8.1 %copy-start.21 = (f32[128,2048]{1,0:T(8,128)S(1)}, f32[128,2048]{1,0:T(8,128)}, u32[]{:S(2)}) copy-start(f32[128,2048]{1,0:T(8,128)} %get-tuple-element.37) | copy-start | bytes 3145732
  709.7 2.3 copy-start.18
  709.7 3.4 copy-start.22

commit v7 on v6

--- a/solution.py
+++ b/solution.py
@@ -294,14 +294,15 @@
 
 
 class Rounds:
-    def __init__(self, here, items):
+    def __init__(self, here, items, ring=True):
         self.here, self.items = here, items
         for item in items:
             item.keep().start()
             for way in (0, 1):
                 self.depart(0, way, item)
-            for way in (0, 1):
-                item.round(here.z, way, True).start()
+            if ring:
+                for way in (0, 1):
+                    item.round(here.z, way, True).start()
 
     def depart(self, step, way, item):
         here = self.here
@@ -316,34 +317,50 @@
         pl.when(here.z >= step)(lambda: body(here.z - step, 0))
         pl.when(here.z + step < DEPTH)(lambda: body(here.z + step, 1))
 
-    def service(self, step, between=None):
-        items, here = self.items, self.here
-
-        def first(z, way):
-            for item in items:
+    def line(self, step, ring=True):
+        def body(z, way):
+            for item in self.items:
                 block = item.block(z, 0)
                 remote(
-                    block, block, item.line.at[0, way, step], item.line.at[1, way, step], here.above(1)
+                    block, block, item.line.at[0, way, step - 1], item.line.at[1, way, step - 1], self.here.above(1)
                 ).wait_recv()
-                if step + 2 < DEPTH:
-                    self.depart(step + 1, way, item)
+                if step + 1 < DEPTH:
+                    self.depart(step, way, item)
+                if ring:
+                    for side in (0, 1):
+                        item.round(z, side).start()
+
+        self.places(step, body)
+
+    def ring(self, step):
+        def body(z, way):
+            for item in self.items:
                 for side in (0, 1):
-                    item.round(z, side).start()
-
-        def second(z, way):
-            for item in items:
+                    item.round(z, side, step == 0).start()
+
+        self.places(step, body)
+
+    def second(self, step):
+        def body(z, way):
+            for item in self.items:
                 for side in (0, 1):
                     item.heard(z, side).wait_recv()
                     start(item.onward(z, side, True))
 
+        self.places(step, body)
+
+    def service(self, step, between=None):
         if step + 1 < DEPTH:
-            self.places(step + 1, first)
+            self.line(step + 1)
         if between is not None:
             between()
         if step == 0:
-            for item in items:
-                item.keep().wait()
-        self.places(step, second)
+            self.kept()
+        self.second(step)
+
+    def kept(self):
+        for item in self.items:
+            item.keep().wait()
 
     def third(self, step):
         def body(z, way):
@@ -453,8 +470,8 @@
             copy.start()
         self.lower_own().start()
         self.lower(True).start()
-        for steps in range(1, DEPTH):
-            for copy in self.pieces(steps, False):
+        for copies in zip(*[self.pieces(steps, False) for steps in (2, 3, 1)]):
+            for copy in copies:
                 copy.start()
 
     def relay(self):
@@ -490,37 +507,186 @@
     return ((0, rows // 2), (rows // 2, rows - rows // 2)) if split else ((0, rows), None)
 
 
-def first_gather_kernel(wq, wo, up, small, ein, eout, wq_all, wo_all, up_all, small_all, win, wout, *sems):
+PANEL = 512
+
+
+def attention_forward(
+    tokens, cosine, sine, allowed, wq, wo, gains, normed, raw, queries, keys, values, probs, attended, middle, routed,
+    panel, panel_sems, between
+):
+    block, width = tokens.shape
+    heads = width // HEAD
+    wide = wq.shape[-1]
+    high = 16
+    per = width // PANEL
+
+    def fetch(source, number):
+        slot = lax.rem(number, 2)
+        spot = pl.ds(pl.multiple_of(number * PANEL, PANEL), PANEL)
+        return pltpu.make_async_copy(source.at[:, :, :, :, spot], panel.at[slot], panel_sems.at[slot])
+
+    def slabs(body):
+        def one(number, carry):
+            body(pl.ds(pl.multiple_of(number * high, high), high))
+            return carry
+
+        lax.fori_loop(0, block // high, one, 0)
+
+    def first(at):
+        values = tokens[at].astype(single)
+        factor = lax.rsqrt(jnp.mean(values * values, axis=-1, keepdims=True) + epsilon)
+        normed[at] = (values * factor * gains[0:1]).astype(narrow)
+
+    fetch(wq, 0).start()
+    slabs(first)
+
+    def through(source, left, total, finish):
+        def one(number, carry):
+            fetch(source, number).wait()
+            pl.when(number + 1 < total)(lambda: fetch(source, number + 1).start())
+            weights = panel[lax.rem(number, 2)].reshape(width, PANEL)
+            finish(number, jnp.dot(left[...], weights, preferred_element_type=single))
+            return carry
+
+        lax.fori_loop(0, total, one, 0)
+
+    def keep(number, made):
+        side = lax.div(number, per)
+        spot = pl.ds(pl.multiple_of(lax.rem(number, per) * PANEL, PANEL), PANEL)
+
+        @pl.when(side < 2)
+        def _():
+            raw[side, :, spot] = made
+
+        @pl.when(side == 2)
+        def _():
+            values[:, spot] = made.astype(narrow)
+
+    through(wq, normed, wide // PANEL, keep)
+    fetch(wo, 0).start()
+    between(0)
+
+    factors = [
+        lax.rsqrt(jnp.mean(raw[side] * raw[side], axis=-1, keepdims=True) + epsilon) for side in range(2)
+    ]
+    turn_cos, turn_sin = cosine[...], sine[...]
+    may = allowed[...] > 0.5
+    group = 4
+
+    def some_heads(number, carry):
+        for inner in range(group):
+            head = number * group + inner
+            spot = pl.ds(pl.multiple_of(head * HEAD, HEAD), HEAD)
+            turned = []
+            for side, target in ((0, queries), (1, keys)):
+                field = raw[side, :, spot] * factors[side] * gains[side + 1 : side + 2, spot]
+                field = field * turn_cos + pltpu.roll(field, HEAD // 2, 1) * turn_sin
+                target[:, spot] = field.astype(narrow)
+                turned.append(field.astype(narrow))
+            scores = jnp.where(may, contract_last(turned[0], turned[1]) * HEAD ** (-0.5), masked_score)
+            highest = jnp.max(scores, axis=-1, keepdims=True)
+            unnormed = jnp.exp(scores - highest)
+            shares = unnormed / jnp.sum(unnormed, axis=-1, keepdims=True)
+            probs[head] = shares
+            mixed = jnp.dot(shares.astype(narrow), values[:, spot], preferred_element_type=single)
+            attended[:, spot] = mixed.astype(narrow)
+        return carry
+
+    lax.fori_loop(0, heads // group, some_heads, 0)
+    between(1)
+
+    def add(number, made):
+        spot = pl.ds(pl.multiple_of(number * PANEL, PANEL), PANEL)
+        middle[:, spot] = tokens[:, spot].astype(single) + made
+
+    through(wo, attended, per, add)
+
+    def last(at):
+        values = middle[at]
+        factor = lax.rsqrt(jnp.mean(values * values, axis=-1, keepdims=True) + epsilon)
+        routed[at] = (values * factor * gains[3:4]).astype(narrow)
+
+    slabs(last)
+    between(2)
+
+
+def first_gather_kernel(
+    wq, wo, up, small, ein, eout, tokens, cosine, sine, allowed,
+    wq_all, wo_all, up_all, small_all, win, wout, gains, normed, raw, queries, keys, values, probs, attended, middle, routed,
+    small_here, small_sem, panel, panel_sems, *sems
+):
     here = Here()
     here.meet()
-    items = []
-    for number, (source, whole, halves, shared) in enumerate(
-        (
-            (small, small_all, halves_of(small.shape[0], False), True),
-            (wq, wq_all, halves_of(wq.shape[0]), True),
-            (wo, wo_all, halves_of(wo.shape[0]), True),
-            (up, up_all, halves_of(up.shape[0]), False),
+    items = [
+        Gather(here, source, whole, halves, shared, sems[4 * number : 4 * number + 4])
+        for number, (source, whole, halves, shared) in enumerate(
+            (
+                (small, small_all, halves_of(small.shape[0], False), True),
+                (wq, wq_all, halves_of(wq.shape[0]), True),
+                (wo, wo_all, halves_of(wo.shape[0]), True),
+                (up, up_all, halves_of(up.shape[0]), False),
+            )
         )
-    ):
-        items.append(Gather(here, source, whole, halves, shared, sems[4 * number : 4 * number + 4]))
+    ]
     recut = Recut(here, ein, eout, win, wout, sems[16:20])
-    rounds = Rounds(here, items)
+    weights = Rounds(here, items[:3])
+    rows = Rounds(here, items[3:], ring=False)
+    weights.service(0, lambda: rows.line(1, ring=False))
+    weights.service(1, lambda: rows.line(2, ring=False))
+    recut.begin()
+    weights.third(0)
+    weights.service(2, lambda: rows.line(3, ring=False))
+    weights.third(1)
+    weights.service(3)
+    rows.kept()
     for step in range(DEPTH):
-        rounds.service(step, recut.begin if step == 1 else None)
-        if step:
-            rounds.third(step - 1)
-    rounds.third(DEPTH - 1)
-    recut.relay()
-    rounds.finish()
+        rows.ring(step)
+    weights.third(2)
+    weights.third(3)
+    weights.finish()
+    fetch = pltpu.make_async_copy(small_all, small_here, small_sem.at[0])
+    fetch.start()
+    fetch.wait()
+    share = wq.shape[0]
+    lanes = small.shape[1]
+    lane = lax.broadcasted_iota(jnp.int32, (8, lanes), 1)
+    skip = small.shape[0] - 8
+    for z in range(DEPTH):
+        for chip in range(RING):
+            pair = [small_here[z, chip, core, skip : skip + 8] for core in (0, 1)]
+            both = jnp.where(lane < share, pair[0], pltpu.roll(pair[1], share, 1))
+            begin = (z * RING + chip) * 2 * share
+            gains[:, begin : begin + 2 * share] = both
+
+    def between(part):
+        if part == 0:
+            rows.second(0)
+        elif part == 1:
+            for step in range(1, DEPTH):
+                rows.second(step)
+        else:
+            recut.relay()
+
+    attention_forward(
+        tokens, cosine, sine, allowed, wq_all, wo_all, gains, normed, raw, queries, keys, values, probs, attended,
+        middle, routed, panel, panel_sems, between
+    )
+    for step in range(DEPTH):
+        rows.third(step)
+    rows.finish()
     recut.end()
 
 
-def first_gather(wq, wo, up, small, ein, eout):
+def first_gather(wq, wo, up, small, ein, eout, tokens, cosine, sine, allowed):
     def whole(array, shared):
         lead = (DEPTH, RING, 2) if shared else (DEPTH, RING)
         return jax.ShapeDtypeStruct(lead + array.shape, array.dtype)
 
     held, rows, columns = ein.shape
+    block, width = tokens.shape
+    heads = width // HEAD
+    vmem = pl.BlockSpec(memory_space=pltpu.VMEM)
+    like = jax.ShapeDtypeStruct((block, width), narrow)
     return pl.pallas_call(
         first_gather_kernel,
         out_shape=(
@@ -530,13 +696,32 @@
             whole(small, True),
             jax.ShapeDtypeStruct((DEPTH * rows, columns), ein.dtype),
             jax.ShapeDtypeStruct((2 * held,) + eout.shape[1:], eout.dtype),
+            jax.ShapeDtypeStruct((8, width), single),
+            like,
+            jax.ShapeDtypeStruct((2, block, width), single),
+            like,
+            like,
+            like,
+            jax.ShapeDtypeStruct((heads, block, block), single),
+            like,
+            jax.ShapeDtypeStruct((block, width), single),
+            like,
         ),
-        in_specs=[HBM] * 6,
-        out_specs=(HBM,) * 6,
-        scratch_shapes=GATHER_SEMS * 4 + RECUT_SEMS,
-        compiler_params=pltpu.CompilerParams(collective_id=1, has_side_effects=True),
+        in_specs=[HBM] * 6 + [vmem] * 4,
+        out_specs=(HBM,) * 6 + (vmem,) * 10,
+        scratch_shapes=[
+            pltpu.VMEM((DEPTH, RING, 2) + small.shape, single),
+            pltpu.SemaphoreType.DMA((1,)),
+            pltpu.VMEM((2, DEPTH, RING, 2, wq.shape[0], PANEL), narrow),
+            pltpu.SemaphoreType.DMA((2,)),
+        ]
+        + GATHER_SEMS * 4
+        + RECUT_SEMS,
+        compiler_params=pltpu.CompilerParams(
+            collective_id=1, has_side_effects=True, vmem_limit_bytes=48 * 2**20
+        ),
         name="bring",
-    )(wq, wo, up, small, ein, eout)
+    )(wq, wo, up, small, ein, eout, tokens, cosine, sine, allowed)
 
 TILE = 256
 
@@ -1416,16 +1601,46 @@
     return lax.axis_size("dp") == DEPTH and lax.axis_size("expert") == 2 * RING
 
 
-def bring_all(w_qkv, w_out, upstream, dense, gain_rows, expert_in, expert_out):
+def forward(tokens, gains, weight_qkv, weight_out, cosine, sine, allowed):
+    rows, width = tokens.shape
+    inputs = tokens.astype(single)
+    normed_in = (normalize(inputs)[0] * gains[0]).astype(narrow)
+    projected = jnp.dot(normed_in, weight_qkv, preferred_element_type=single)
+    raw = jnp.stack([projected[:, :width], projected[:, width : 2 * width]])
+    query_rows, key_rows = (
+        rotate(normalize(raw[side])[0] * gains[side + 1], cosine, sine).astype(narrow) for side in range(2)
+    )
+    value_rows = projected[:, 2 * width :].astype(narrow)
+    by_head = (rows, -1, HEAD)
+    scores = jnp.einsum(
+        "qhd,khd->hqk", query_rows.reshape(by_head), key_rows.reshape(by_head), preferred_element_type=single
+    )
+    scores = jnp.where(allowed[None], scores * HEAD ** (-0.5), masked_score)
+    unnormed = jnp.exp(scores - jnp.max(scores, axis=-1, keepdims=True))
+    probs = unnormed / jnp.sum(unnormed, axis=-1, keepdims=True)
+    attended = jnp.einsum(
+        "hqk,khd->qhd", probs.astype(narrow), value_rows.reshape(by_head), preferred_element_type=single
+    )
+    attended = attended.reshape(rows, width).astype(narrow)
+    middle = inputs + jnp.dot(attended, weight_out, preferred_element_type=single)
+    routed_in = (normalize(middle)[0] * gains[3]).astype(narrow)
+    return (normed_in, raw, query_rows, key_rows, value_rows, probs, attended, middle, routed_in)
+
+
+def bring_all(w_qkv, w_out, upstream, dense, gain_rows, expert_in, expert_out, tokens, cosine, sine, allowed):
     width = upstream.shape[1]
     share = gain_rows.shape[1]
     if by_kernels():
         experts, rows = dense.shape[1], dense.shape[0]
         small = jnp.concatenate([dense.T, jnp.pad(gain_rows, ((0, 4), (0, rows - share)))], axis=0)
-        wq, wo, up, all_small, weight_in, weight_down = first_gather(
-            w_qkv, w_out, upstream, small, expert_in, expert_out
+        tables = (
+            jnp.concatenate([cosine[:, 0], cosine[:, 0]], axis=1),
+            jnp.concatenate([-sine[:, 0], sine[:, 0]], axis=1),
+            allowed.astype(single),
         )
-        gains = all_small[:, :, :, experts : experts + 4, :share].transpose(3, 0, 1, 2, 4).reshape(4, -1)
+        wq, wo, up, all_small, weight_in, weight_down, gains, *made = first_gather(
+            w_qkv, w_out, upstream, small, expert_in, expert_out, tokens, *tables
+        )
         core = lax.rem(lax.axis_index("expert"), 2)
         every_gate = lax.dynamic_index_in_dim(all_small, core, axis=2, keepdims=False)[:, :, :experts]
         return (
@@ -1433,20 +1648,25 @@
             wo.reshape(-1, w_out.shape[1]),
             up.reshape(-1, width),
             every_gate,
-            gains,
+            gains[:4],
             weight_in,
             weight_down.reshape(-1, width),
+            made,
         )
     everyone = ("dp", "expert")
     weight_in, weight_down = fetch_weights(expert_in, expert_out)
+    weight_qkv = lax.all_gather(w_qkv, everyone, axis=0, tiled=True)
+    weight_out = lax.all_gather(w_out, everyone, axis=0, tiled=True)
+    gains = lax.all_gather(gain_rows, everyone, axis=1, tiled=True)
     return (
-        lax.all_gather(w_qkv, everyone, axis=0, tiled=True),
-        lax.all_gather(w_out, everyone, axis=0, tiled=True),
+        weight_qkv,
+        weight_out,
         gather_alike(upstream).reshape(-1, width),
         gather_alike(dense.T),
-        lax.all_gather(gain_rows, everyone, axis=1, tiled=True),
+        gains,
         weight_in,
         weight_down,
+        forward(tokens, gains, weight_qkv, weight_out, cosine, sine, allowed),
     )
 
 
@@ -1529,44 +1749,29 @@
     rows = micro_count * seq_len
     held = expert_in.shape[0]
     experts = lax.axis_size("expert") * held
-    inputs = tokens.reshape(rows, model_width).astype(single)
+    own = tokens.reshape(rows, model_width)
     upstream = out_grad.reshape(rows, model_width)
     ids = expert_ids.reshape(rows, -1)
     gate_rows = gates.reshape(rows, -1)
     onehot = (ids[:, :, None] == jnp.arange(experts, dtype=jnp.int32)).astype(single)
     dense = jnp.sum(onehot * gate_rows[:, :, None], axis=1)
     gain_rows = jnp.stack([attn_gain, q_gain, k_gain, ffn_gain]).astype(single)
-    weight_qkv, weight_out, up_rows, every_gate, gains, weight_in, weight_down = bring_all(
-        w_qkv, w_out, upstream, dense, gain_rows, expert_in, expert_out
-    )
-    gain_attn, gain_query, gain_key, gain_ffn = gains[0], gains[1], gains[2], gains[3]
-
-    normal_in, factor_in = normalize(inputs)
-    normed_in = (normal_in * gain_attn).astype(narrow)
-    projected = jnp.dot(normed_in, weight_qkv, preferred_element_type=single)
-    normal_q, factor_q = normalize(projected[:, :model_width])
-    normal_k, factor_k = normalize(projected[:, model_width : 2 * model_width])
     document, position = layout(lengths[:, 0], seq_len)
     cosine, sine = angles(position)
-    query_rows = rotate(normal_q * gain_query, cosine, sine).astype(narrow).reshape(rows, -1, HEAD)
-    key_rows = rotate(normal_k * gain_key, cosine, sine).astype(narrow).reshape(rows, -1, HEAD)
-    value_rows = projected[:, 2 * model_width :].astype(narrow).reshape(rows, -1, HEAD)
     places = jnp.arange(rows, dtype=jnp.int32)
     allowed = (document[:, None] == document[None, :]) & (places[:, None] >= places[None, :])
-    raw = jnp.einsum("qhd,khd->hqk", query_rows, key_rows, preferred_element_type=single)
-    scores = jnp.where(allowed[None], raw * HEAD ** (-0.5), masked_score)
-    highest = jnp.max(scores, axis=-1, keepdims=True)
-    unnormed = jnp.exp(scores - highest)
-    probs = unnormed / jnp.sum(unnormed, axis=-1, keepdims=True)
+    weight_qkv, weight_out, up_rows, every_gate, gains, weight_in, weight_down, made = bring_all(
+        w_qkv, w_out, upstream, dense, gain_rows, expert_in, expert_out, own, cosine, sine, allowed
+    )
+    gain_attn, gain_query, gain_key, gain_ffn = gains[0], gains[1], gains[2], gains[3]
+    normed_in, raw, query_rows, key_rows, value_rows, probs, attended, middle, routed_in = made
+    normal_q, factor_q = normalize(raw[0])
+    normal_k, factor_k = normalize(raw[1])
+    normal_mid, factor_mid = normalize(middle)
+    query_rows, key_rows, value_rows = (
+        field.reshape(rows, -1, HEAD) for field in (query_rows, key_rows, value_rows)
+    )
     attn_probs = probs.astype(narrow)
-    attended = (
-        jnp.einsum("hqk,khd->qhd", attn_probs, value_rows, preferred_element_type=single)
-        .reshape(rows, model_width)
-        .astype(narrow)
-    )
-    middle = inputs + jnp.dot(attended, weight_out, preferred_element_type=single)
-    normal_mid, factor_mid = normalize(middle)
-    routed_in = (normal_mid * gain_ffn).astype(narrow)
 
     mixture, grad_routed, gate_table, (share_in, share_down) = experts_all(
         routed_in, up_rows, every_gate, weight_in, weight_down, held
@@ -1598,7 +1803,7 @@
         [grad_q_raw, grad_k_raw, grad_value.reshape(rows, model_width)], axis=1
     ).astype(narrow)
     grad_tokens, gain_sums, grad_qkv_share, grad_out_share, share_in = deliver_all(
-        tokens.reshape(rows, model_width),
+        own,
         gain_attn,
         grad_middle,
         (piece_query, piece_key, piece_ffn),

time: 718 us -> 707 us (0.985); the launches traced: 714 us -> 696 us
  matrix products: 34.9 us -> 8.04 us
  local copies, waits for them, and re-layouts: 19.7 us -> 29 us
    dot_general x3 -> x0, matrix products: 18.6 us -> none  [the longest x1 10.2 us: local(): projected = jnp.dot(normed_in, weight_qkv, preferred_element_type=single)]
    pallas_call x1, Pallas kernels: 221 us -> 233 us  [first_gather(): pl.pallas_call(first_gather_kernel, out_shape=(whole(wq, True), whole(wo,...]
    pallas_call x1, Pallas kernels: 182 us -> 173 us  [last_sum(): pl.pallas_call(last_sum_kernel, out_shape=(jax.ShapeDtypeStruct((share, w...]
    another operation x2 -> x1, other arithmetic: 8.94 us -> 1.74 us
    unnamed x62 -> x46, local copies, waits for them, and re-layouts: 7.76 us -> 14.5 us
where the time goes in v7:
time: 707 us; the launch traced here: 696 us
  Pallas kernels  630 us (89%)
  local copies, waits for them, and re-layouts  29 us (4%)
  other arithmetic  27.9 us (4%)
  matrix products  8.04 us (1%)
    pallas_call x1, Pallas kernels, first_gather(): pl.pallas_call(first_gather_kernel, out_shape=(whole(wq, True), whole(wo,...  233 us
    pallas_call x1, Pallas kernels, experts_round(): pl.pallas_call(experts_kernel, out_shape=(jax.ShapeDtypeStruct((block, wi...  223 us
    pallas_call x1, Pallas kernels, last_sum(): pl.pallas_call(last_sum_kernel, out_shape=(jax.ShapeDtypeStruct((share, w...  173 us
    unnamed x46, local copies, waits for them, and re-layouts  14.5 us

profile of v7, /device:TPU:0, one launch (start us, length us, event | category | flops | bytes accessed | tf_op | source)
XLA Modules:
  0.0 695.8 jit_solution(16121771004129482415)
XLA Ops:
  0.7 0.8 select_reduce_fusion.3
  5.6 1.0 copy-done
  6.7 1.0 copy-done.1
  7.7 1.1 copy-done.3
  8.8 0.9 copy-done.7
  9.8 232.9 %bring.1 = (bf16[4,4,2,64,6144]{4,3,2,1,0:T(8,128)(2,1)}, bf16[4,4,2,64,2048]{4,3,2,1,0:T(8,128)(2,1)}, bf16[4,4,128,2048]{3,2,1,0:T(8,128)(2,1)}, f32[4,4,2,24,...) custom-call(bf16[64,6144]{1,0:T(8,128)(2,1)S(1)} %copy-done.3, ...), custom_call_target="tpu_custom_call" | custom-call | tf_op jit(solution)/shard_map/bring/pallas_call | solution.py:690
  242.7 0.8 copy-done.4
  243.5 0.8 copy-done.5
  245.1 1.4 multiply_reduce_fusion.7
  246.5 1.8 fusion.7
  248.9 1.0 copy.102
  249.9 1.0 copy.105
  251.3 1.0 pad.13.gates
  252.3 223.4 %experts.1 = (f32[128,2048]{1,0:T(8,128)}, f32[16,128]{1,0:T(8,128)}, f32[128,2048]{1,0:T(8,128)}, bf16[2048,1024]{1,0:T(8,128)(2,1)}, bf16[512,2048]{1,0:T(8,12...) custom-call(bf16[128,2048]{1,0:T(8,128)(2,1)} %copy-done.6, ...), custom_call_target="tpu_custom_call" | custom-call | tf_op jit(solution)/shard_map/experts/pallas_call | solution.py:1548
  477.1 1.9 multiply_reduce_fusion
  479.0 3.4 fusion.34
  483.2 6.4 convolution_convert_fusion
  490.1 1.0 copy.108
  493.9 1.0 copy-done.10
  494.8 1.3 copy.106
  496.2 2.7 copy.107
  498.8 1.3 copy.103
  500.1 1.3 copy.104
  501.5 2.2 multiply_reduce_fusion.1
  504.4 1.7 fusion.11
  506.2 1.3 pad_maximum_fusion.grad
  507.4 173.3 %deliver.1 = (f32[64,6144]{1,0:T(8,128)}, f32[64,2048]{1,0:T(8,128)}, f32[8,128]{1,0:T(8,128)}, f32[128,2048]{1,0:T(8,128)}, bf16[2,512,2048]{2,1,0:T(8,128)(2,1)}) custom-call(bf16[128,2048]{1,0:T(8,128)(2,1)} %copy-done.4, bf16[128,6144]{1,0:T(8,128)(2,1)} %pad_maximum_fusion.grad, bf16[128,2048]{1,0:T(8,128)(2,1)} %copy-done.5, ...), custom_call_target="tpu_custom_call" | custom-call | tf_op jit(solution)/shard_map/deliver/pallas_call | solution.py:1185
  682.0 5.2 convert_add_fusion
  687.2 4.4 convert_element_type.60
  691.7 1.0 copy.120
  692.6 0.8 copy-done.17
  693.5 1.1 copy.121
  (82 shorter events, 14.1 us)
Async XLA Ops:
  5.6 1.0 copy-start
  6.7 1.0 copy-start.1
  7.7 1.1 copy-start.3
  8.8 0.9 copy-start.7
  242.7 0.8 copy-start.4
  243.5 0.8 copy-start.5
  244.3 0.8 copy-start.6
  252.3 226.7 %copy-start.2 = (bf16[2,64,2048]{2,1,0:T(8,128)(2,1)S(1)}, bf16[2,64,2048]{2,1,0:T(8,128)(2,1)}, u32[]{:S(2)}) copy-start(bf16[2,64,2048]{2,1,0:T(8,128)(2,1)} %param.25) | copy-start | bytes 1572868
  482.4 0.8 copy-start.11
  483.2 6.7 copy-start.9
  491.1 1.0 copy-start.16
  491.8 1.1 copy-start.15
  493.9 1.0 copy-start.10
  496.2 5.3 copy-start.8
  501.4 3.0 copy-start.13
  504.4 1.8 copy-start.14
  682.0 5.2 copy-start.12
  687.2 4.5 copy-start.18
  691.7 1.8 copy-start.17
  691.7 2.9 copy-start.19

commit v8 on v7

--- a/solution.py
+++ b/solution.py
@@ -970,8 +970,8 @@
 
 
 class Share:
-    def __init__(self, here, source, target, sems):
-        self.here, self.source, self.target, self.sems = here, source, target, sems
+    def __init__(self, here, source, target, side, sems):
+        self.here, self.source, self.target, self.side, self.sems = here, source, target, side, sems
         self.held, self.rows, columns = target.shape
         self.part = columns // (2 * DEPTH)
 
@@ -980,23 +980,23 @@
         origin = lax.rem(here.z + DEPTH - steps, DEPTH) if arriving else here.z
         away = lax.rem(here.z + steps, DEPTH)
         copies = []
-        for number in range(2 * self.held):
-            side, expert = divmod(number, self.held)
-            column = (side * DEPTH + origin) * self.part
+        for expert in range(self.held):
+            column = (self.side * DEPTH + origin) * self.part
             target = self.target.at[expert, :, pl.ds(pl.multiple_of(column, 128), self.part)]
             source = self.source.at[
-                pl.ds(pl.multiple_of(away * self.rows, 16), self.rows), pl.ds(number * self.part, self.part)
+                pl.ds(pl.multiple_of(away * self.rows, 16), self.rows),
+                pl.ds((self.side * self.held + expert) * self.part, self.part),
             ]
             if steps == 0:
-                copies.append(pltpu.make_async_copy(source, target, self.sems.at[0, 0, number]))
+                copies.append(pltpu.make_async_copy(source, target, self.sems.at[0, 0, expert]))
             else:
-                sems = (self.sems.at[0, steps, number], self.sems.at[1, steps, number])
+                sems = (self.sems.at[0, steps, expert], self.sems.at[1, steps, expert])
                 copies.append(remote(target if arriving else source, target, *sems, here.above(steps)))
         return copies
 
     def begin(self):
-        for steps in range(DEPTH):
-            for copy in self.pieces(steps, False):
+        for copies in zip(*[self.pieces(steps, False) for steps in (2, 3, 1, 0)]):
+            for copy in copies:
                 copy.start()
 
     def end(self):
@@ -1008,151 +1008,240 @@
                     copy.wait_recv()
 
 
+STRIP = 128
+
+
 def last_sum_kernel(
     normed,
-    grad,
     attended,
-    branch,
     gin_sum,
     weight,
+    weight_out,
     tokens,
-    grad_middle,
-    gain,
-    pieces,
+    routed,
+    upstream,
+    middle,
+    raw,
+    queries,
+    keys,
+    values,
+    probs,
+    cosine,
+    sine,
+    gains,
     q_sum,
     o_sum,
-    gains,
+    gain_sums,
     grad_tokens,
     share_in,
-    left,
-    left_out,
-    right,
-    sems,
-    panel,
-    panel_sems,
-    back,
-    piece,
-    few_sum,
-    few_other,
-    pair_sems,
-    share_sems,
     *scratch,
 ):
     here = Here()
     here.meet()
-    block, width = normed.shape
+    block, width = tokens.shape
     share = q_sum.shape[0]
-    wide = grad.shape[1]
+    wide = q_sum.shape[1]
     sides = wide // width
-    moved = [
-        (normed, left, None),
-        (grad, right, pl.ds(0, wide)),
-        (attended, left_out, None),
-        (branch, right, pl.ds(wide, width)),
-    ]
-    copies = []
-    for number, (source, target, spot) in enumerate(moved):
-        own, other = (target.at[core] if spot is None else target.at[core, :, spot] for core in (0, 1))
-        copies.append(
+    heads = width // HEAD
+    (
+        left, left_out, right, panel, x, routed_v, upstream_v, middle_v, raw_v, queries_v, keys_v, values_v, probs_v,
+        grad_middle, grad_heads, turned, piece, few_sum, few_other, sems, panel_sems, pair_sems, share_sems
+    ) = scratch[:23]
+    big = Sum(
+        here,
+        None,
+        [(q_sum.at[:, pl.ds(side * width, width)], side * share, share) for side in range(sides)],
+        halves_of(sides * share),
+        False,
+        scratch[23:31],
+    )
+    outer = Sum(here, None, o_sum, halves_of(share), False, scratch[31:39])
+    few = Sum(here, None, few_sum, halves_of(few_sum.shape[0], False), False, scratch[39:47])
+    order = [far_first(here, number) for number in range(DEPTH)]
+    loads = [
+        pltpu.make_async_copy(source, target, sems.at[number])
+        for number, (source, target) in enumerate(
             (
-                pltpu.make_async_copy(source, own, sems.at[number]),
-                remote(source, other, sems.at[4 + number], sems.at[8 + number], here.sibling()),
+                (middle, middle_v),
+                (routed, routed_v),
+                (upstream, upstream_v),
+                (attended, left_out.at[0]),
+                (values, values_v),
+                (probs, probs_v),
+                (queries, queries_v),
+                (keys, keys_v),
+                (raw, raw_v),
+                (normed, left.at[0]),
+                (tokens, x),
             )
         )
-    for kept, sent in copies:
-        sent.start()
-        kept.start()
-    back_share = Share(here, gin_sum, share_in, share_sems)
-    back_share.begin()
-    targets = [(q_sum.at[:, pl.ds(side * width, width)], side * share, share) for side in range(sides)]
-    targets.append((o_sum, sides * share, share))
-    big = Sum(here, None, targets, halves_of((sides + 1) * share), False, scratch[0:8])
-    few = Sum(here, None, few_sum, halves_of(few_sum.shape[0], False), False, scratch[8:16])
-    order = [far_first(here, number) for number in range(DEPTH)]
-
-    def fetch_panel(number):
+    ]
+
+    def fetch(source, number, columns):
         slot = lax.rem(number, 2)
-        rows = pl.ds(pl.multiple_of(number * TILE, TILE), TILE)
-        return pltpu.make_async_copy(weight.at[rows], panel.at[slot], panel_sems.at[slot])
-
-    panels = width // TILE
-    fetch_panel(0).start()
-    for kept, sent in copies:
-        kept.wait()
-        sent.wait_recv()
+        rows = pl.ds(pl.multiple_of(number * STRIP, STRIP), STRIP)
+        return pltpu.make_async_copy(source.at[rows], panel.at[slot, :, pl.ds(0, columns)], panel_sems.at[slot])
+
+    for copy in loads:
+        copy.start()
+    fetch(weight_out, 0, width).start()
+    shares_in = [Share(here, gin_sum, share_in, side, share_sems.at[side]) for side in range(2)]
+    for share_side in shares_in:
+        share_side.begin()
+
+    def swap(number, source, target):
+        base = 16 + 2 * number
+        return remote(source, target, sems.at[base], sems.at[base + 1], here.sibling())
+
+    side_out = pl.ds(wide, width)
+    side_qkv = pl.ds(0, wide)
+    swaps = [
+        swap(0, left_out.at[0], left_out.at[1]),
+        swap(1, right.at[0, :, side_out], right.at[1, :, side_out]),
+        swap(2, left.at[0], left.at[1]),
+        swap(3, right.at[0, :, side_qkv], right.at[1, :, side_qkv]),
+    ]
+    high = 16
+    panels = width // STRIP
+
+    def slabs(body):
+        def one(number, carry):
+            body(pl.ds(pl.multiple_of(number * high, high), high))
+            return carry
+
+        lax.fori_loop(0, block // high, one, 0)
+
+    def norm(values):
+        factor = lax.rsqrt(jnp.mean(values * values, axis=-1, keepdims=True) + epsilon)
+        return values * factor, factor
+
+    def norm_grad(up, values, row):
+        normal, factor = norm(values)
+        weighted = up * gains[row : row + 1]
+        inner = jnp.mean(weighted * normal, axis=-1, keepdims=True)
+        piece[row : row + 1] += jnp.sum(up * normal, axis=0, keepdims=True)
+        return factor * (weighted - normal * inner)
+
+    def first(at):
+        grad = upstream_v[at].astype(single) + norm_grad(routed_v[at], middle_v[at], 3)
+        grad_middle[at] = grad
+        right[0, at, side_out] = grad.astype(narrow)
+
+    piece[...] = jnp.zeros_like(piece)
+    for number in range(4):
+        loads[number].wait()
+    swaps[0].start()
+    slabs(first)
+    swaps[1].start()
+
+    def through(source, columns, left_rows, finish, begin=0, end=panels):
+        def one(number, carry):
+            fetch(source, number, columns).wait()
+            pl.when(number + 1 < panels)(lambda: fetch(source, number + 1, columns).start())
+            rows = panel[lax.rem(number, 2), :, 0:columns]
+            finish(pl.ds(pl.multiple_of(number * STRIP, STRIP), STRIP), contract_last(left_rows, rows))
+            return carry
+
+        lax.fori_loop(begin, end, one, 0)
+
+    def keep_heads(spot, made):
+        grad_heads[:, spot] = made.astype(narrow)
+
+    through(weight_out, width, right[0, :, side_out], keep_heads)
+    fetch(weight, 0, wide).start()
+
     step = 512
     each = width // step
     rows = RING * 2 * share
 
-    def make(z):
+    def make(z, item, source, first_chunk, last_chunk):
         at = pl.ds(pl.multiple_of(z * rows, rows), rows)
 
-        def one(number, source):
+        def one(number, carry):
             spot = pl.ds(pl.multiple_of(number * step, step), step)
-            turned = source[:, :, at].reshape(2 * block, rows)
-            made = contract_rows(turned, right[:, :, spot].reshape(2 * block, step))
+            left_rows = source[:, :, at].reshape(2 * block, rows)
+            made = contract_rows(left_rows, right[:, :, spot].reshape(2 * block, step))
             made = made.reshape(RING, 2, share, step)
             mine = jnp.where(here.core == 0, made[:, 0], made[:, 1]).astype(narrow)
-            row = pl.multiple_of(lax.div(number, each) * share, share)
+            row = pl.multiple_of(lax.div(number - first_chunk, each) * share, share)
             column = pl.multiple_of(lax.rem(number, each) * step, step)
             for chip in range(RING):
-                big.mine[z, chip, pl.ds(row, share), pl.ds(column, step)] = mine[chip]
-
-        def qkv(number, carry):
-            one(number, left)
+                item.mine[z, chip, pl.ds(row, share), pl.ds(column, step)] = mine[chip]
             return carry
 
-        def out(number, carry):
-            one(number, left_out)
-            return carry
-
-        lax.fori_loop(0, sides * each, qkv, 0)
-        lax.fori_loop(sides * each, (sides + 1) * each, out, 0)
-
-    def through(first, last):
-        def body(number, carry):
-            fetch_panel(number).wait()
-            pl.when(number + 1 < panels)(lambda: fetch_panel(number + 1).start())
-            spot = pl.ds(pl.multiple_of(number * TILE, TILE), TILE)
-            back[:, spot] = contract_last(right[0, :, 0:wide], panel[lax.rem(number, 2)])
-            return carry
-
-        lax.fori_loop(first, last, body, 0)
-
-    def norm_back():
-        piece[...] = pieces[...]
-        high = 16
-
-        def body(number, carry):
-            at = pl.ds(pl.multiple_of(number * high, high), high)
-            values = tokens[at].astype(single)
-            factor = lax.rsqrt(jnp.mean(values * values, axis=-1, keepdims=True) + epsilon)
-            normal = values * factor
-            upstream = back[at]
-            weighted = upstream * gain[...]
-            inner = jnp.mean(weighted * normal, axis=-1, keepdims=True)
-            grad_tokens[at] = grad_middle[at] + factor * (weighted - normal * inner)
-            piece[0:1] += jnp.sum(upstream * normal, axis=0, keepdims=True)
-            return carry
-
-        lax.fori_loop(0, block // high, body, 0)
-        for z in range(DEPTH):
-            for chip in range(RING):
-                begin = (z * RING + chip) * 2 * share
-                few.mine[z, chip] = piece[:, begin : begin + 2 * share]
+        lax.fori_loop(first_chunk, last_chunk, one, 0)
+
+    swaps[0].wait_recv()
+    swaps[1].wait_recv()
+    for z in order:
+        make(z, outer, left_out, sides * each, (sides + 1) * each)
+        for way in (0, 1):
+            start(outer.toss(z, way))
+    for number in range(4, len(loads)):
+        loads[number].wait()
+    swaps[2].start()
+    turn_cos, turn_sin = cosine[...], sine[...]
+    group = 4
+
+    def some_heads(number, carry):
+        for inner in range(group):
+            head = number * group + inner
+            spot = pl.ds(pl.multiple_of(head * HEAD, HEAD), HEAD)
+            grad = grad_heads[:, spot]
+            shares = probs_v[head]
+            grad_shares = contract_last(grad, values_v[:, spot])
+            along = jnp.sum(grad_shares * shares, axis=-1, keepdims=True)
+            scores = (shares * (grad_shares - along)).astype(narrow)
+            made = (
+                jnp.dot(scores, keys_v[:, spot], preferred_element_type=single),
+                contract_rows(scores, queries_v[:, spot]),
+            )
+            for side, field in enumerate(made):
+                field = field * HEAD ** (-0.5)
+                turned[side, :, spot] = field * turn_cos - pltpu.roll(field, HEAD // 2, 1) * turn_sin
+            spot_v = pl.ds(pl.multiple_of(2 * width + head * HEAD, HEAD), HEAD)
+            right[0, :, spot_v] = contract_rows(shares.astype(narrow), grad).astype(narrow)
+        return carry
+
+    lax.fori_loop(0, heads // group, some_heads, 0)
+
+    def second(at):
+        for side in range(2):
+            grad = norm_grad(turned[side, at], raw_v[side, at], side + 1)
+            right[0, at, side * width : (side + 1) * width] = grad.astype(narrow)
+
+    for z in order[:2]:
+        outer.second(z)
+    slabs(second)
+    swaps[3].start()
+    for z in order[2:]:
+        outer.second(z)
+    swaps[2].wait_recv()
+    swaps[3].wait_recv()
+
+    def keep_back(spot, made):
+        routed_v[:, spot] = made
+
+    def third(at):
+        grad_tokens[at] = grad_middle[at] + norm_grad(routed_v[at], x[at].astype(single), 0)
 
     for number, z in enumerate(order):
-        make(z)
+        make(z, big, left, 0, sides * each)
         for way in (0, 1):
             start(big.toss(z, way))
         if number:
             big.second(order[number - 1])
+        outer.third(z, number == DEPTH - 1)
         if number > 1:
             big.third(order[number - 2], False)
-        if number < 2:
-            through(number * panels // 2, (number + 1) * panels // 2)
-        if number == 2:
-            norm_back()
+        cut = panels // DEPTH
+        through(weight, wide, right[0, :, side_qkv], keep_back, number * cut, (number + 1) * cut)
+        if number == DEPTH - 1:
+            slabs(third)
+            for plane in range(DEPTH):
+                for chip in range(RING):
+                    begin = (plane * RING + chip) * 2 * share
+                    few.mine[plane, chip] = piece[:, begin : begin + 2 * share]
             for place in order:
                 start(few.toss(place, 0))
     big.second(order[-1])
@@ -1163,25 +1252,31 @@
         few.third(z, False)
     big.third(order[-1], True)
     few.third(order[-1], True)
-    swap = remote(few_sum, few_other, pair_sems.at[0], pair_sems.at[1], here.sibling())
-    swap.start()
-    swap.wait_recv()
-    gains[...] = few_sum[...] + few_other[...]
-    swap.wait_send()
+    pair = remote(few_sum, few_other, pair_sems.at[0], pair_sems.at[1], here.sibling())
+    pair.start()
+    pair.wait_recv()
+    gain_sums[...] = few_sum[...] + few_other[...]
+    pair.wait_send()
     for number, z in enumerate(order):
-        for item in (big, few):
+        for item in (big, outer, few):
             item.end(z, number == DEPTH - 1)
-    for kept, sent in copies:
-        sent.wait_send()
-    back_share.end()
-
-
-def last_sum(normed, grad, attended, branch, gin_sum, weight, tokens, grad_middle, gain, pieces, share, held):
+    for copy in swaps:
+        copy.wait_send()
+    for share_side in shares_in:
+        share_side.end()
+
+
+def last_sum(
+    normed, attended, gin_sum, weight, weight_out, tokens, routed, upstream, middle, raw, queries, keys, values, probs,
+    cosine, sine, gains, share, held
+):
     block, width = normed.shape
-    wide = grad.shape[1]
-    rows = (wide // width + 1) * share
+    wide = weight.shape[1]
+    sides = wide // width
     vmem = pl.BlockSpec(memory_space=pltpu.VMEM)
-    few = (pieces.shape[0], 2 * share)
+    few = (gains.shape[0], 2 * share)
+    like = pltpu.VMEM((block, width), narrow)
+    like_single = pltpu.VMEM((block, width), single)
     return pl.pallas_call(
         last_sum_kernel,
         out_shape=(
@@ -1191,29 +1286,44 @@
             jax.ShapeDtypeStruct((block, width), single),
             jax.ShapeDtypeStruct((held, gin_sum.shape[0] // DEPTH, DEPTH * gin_sum.shape[1] // held), narrow),
         ),
-        in_specs=[HBM] * 6 + [vmem] * 4,
+        in_specs=[HBM] * 14 + [vmem] * 3,
         out_specs=(vmem, vmem, vmem, vmem, HBM),
         scratch_shapes=[
             pltpu.VMEM((2, block, width), narrow),
             pltpu.VMEM((2, block, width), narrow),
             pltpu.VMEM((2, block, wide + width), narrow),
-            pltpu.SemaphoreType.DMA((12,)),
-            pltpu.VMEM((2, TILE, wide), narrow),
-            pltpu.SemaphoreType.DMA((2,)),
-            pltpu.VMEM((block, width), single),
-            pltpu.VMEM(pieces.shape, single),
+            pltpu.VMEM((2, STRIP, wide), narrow),
+            like,
+            like_single,
+            like,
+            like_single,
+            pltpu.VMEM(raw.shape, single),
+            like,
+            like,
+            like,
+            pltpu.VMEM(probs.shape, single),
+            like_single,
+            like,
+            pltpu.VMEM((2, block, width), single),
+            pltpu.VMEM(gains.shape, single),
             pltpu.VMEM(few, single),
             pltpu.VMEM(few, single),
+            pltpu.SemaphoreType.DMA((24,)),
             pltpu.SemaphoreType.DMA((2,)),
-            pltpu.SemaphoreType.DMA((2, DEPTH, 2 * held)),
+            pltpu.SemaphoreType.DMA((2,)),
+            pltpu.SemaphoreType.DMA((2, 2, DEPTH, held)),
         ]
-        + sum_scratch(rows, width, narrow, halves_of(rows), made=True)
+        + sum_scratch(sides * share, width, narrow, halves_of(sides * share), made=True)
+        + sum_scratch(share, width, narrow, halves_of(share), made=True)
         + sum_scratch(few[0], few[1], single, halves_of(few[0], False), made=True),
         compiler_params=pltpu.CompilerParams(
             collective_id=4, has_side_effects=True, vmem_limit_bytes=62 * 2**20
         ),
         name="deliver",
-    )(normed, grad, attended, branch, gin_sum, weight, tokens, grad_middle, gain, pieces)
+    )(
+        normed, attended, gin_sum, weight, weight_out, tokens, routed, upstream, middle, raw, queries, keys, values, probs,
+        cosine, sine, gains
+    )
 
 def near_first(here, number):
     high = lax.div(here.z, 2)
@@ -1627,17 +1737,20 @@
     return (normed_in, raw, query_rows, key_rows, value_rows, probs, attended, middle, routed_in)
 
 
+def wide_tables(cosine, sine):
+    return (
+        jnp.concatenate([cosine[:, 0], cosine[:, 0]], axis=1),
+        jnp.concatenate([-sine[:, 0], sine[:, 0]], axis=1),
+    )
+
+
 def bring_all(w_qkv, w_out, upstream, dense, gain_rows, expert_in, expert_out, tokens, cosine, sine, allowed):
     width = upstream.shape[1]
     share = gain_rows.shape[1]
     if by_kernels():
         experts, rows = dense.shape[1], dense.shape[0]
         small = jnp.concatenate([dense.T, jnp.pad(gain_rows, ((0, 4), (0, rows - share)))], axis=0)
-        tables = (
-            jnp.concatenate([cosine[:, 0], cosine[:, 0]], axis=1),
-            jnp.concatenate([-sine[:, 0], sine[:, 0]], axis=1),
-            allowed.astype(single),
-        )
+        tables = (*wide_tables(cosine, sine), allowed.astype(single))
         wq, wo, up, all_small, weight_in, weight_down, gains, *made = first_gather(
             w_qkv, w_out, upstream, small, expert_in, expert_out, tokens, *tables
         )
@@ -1648,7 +1761,7 @@
             wo.reshape(-1, w_out.shape[1]),
             up.reshape(-1, width),
             every_gate,
-            gains[:4],
+            gains,
             weight_in,
             weight_down.reshape(-1, width),
             made,
@@ -1703,28 +1816,65 @@
     )
 
 
-def deliver_all(tokens, gain, grad_middle, pieces, normed, grad_qkv, weight_qkv, attended, branch, share_in, held):
+def backward(
+    tokens, gains, grad_routed, upstream, normed, raw, queries, keys, values, probs, attended, middle, weight_qkv, weight_out,
+    cosine, sine
+):
+    rows, width = tokens.shape
+    by_head = (rows, -1, HEAD)
+    grad_mid, piece_ffn = rms_back(grad_routed, *normalize(middle), gains[3])
+    grad_middle = upstream.astype(single) + grad_mid
+    branch = grad_middle.astype(narrow)
+    grad_heads = contract_last(branch, weight_out).astype(narrow).reshape(by_head)
+    grad_probs = jnp.einsum("qhd,khd->hqk", grad_heads, values.reshape(by_head), preferred_element_type=single)
+    inner = jnp.sum(grad_probs * probs, axis=-1, keepdims=True)
+    grad_scores = (probs * (grad_probs - inner)).astype(narrow)
+    grads = (
+        jnp.einsum("hqk,khd->qhd", grad_scores, keys.reshape(by_head), preferred_element_type=single),
+        jnp.einsum("hqk,qhd->khd", grad_scores, queries.reshape(by_head), preferred_element_type=single),
+    )
+    grad_value = jnp.einsum("hqk,qhd->khd", probs.astype(narrow), grad_heads, preferred_element_type=single)
+    (grad_q, piece_query), (grad_k, piece_key) = (
+        rms_back(
+            rotate(grads[side].reshape(rows, width) * HEAD ** (-0.5), cosine, -sine),
+            *normalize(raw[side]),
+            gains[side + 1],
+        )
+        for side in range(2)
+    )
+    grad_qkv = jnp.concatenate([grad_q, grad_k, grad_value.reshape(rows, width)], axis=1).astype(narrow)
+    grad_input, piece_attn = rms_back(
+        contract_last(grad_qkv, weight_qkv), *normalize(tokens.astype(single)), gains[0]
+    )
+    pieces = jnp.stack([piece_attn, piece_query, piece_key, piece_ffn])
+    return (grad_middle + grad_input, pieces, (normed, grad_qkv), (attended, branch))
+
+
+def deliver_all(tokens, gains, grad_routed, upstream, made, weight_qkv, weight_out, cosine, sine, share_in, held):
+    normed, raw, queries, keys, values, probs, attended, middle, _ = made
     owners = lax.axis_size("dp") * lax.axis_size("expert")
-    share = gain.shape[0] // owners
+    share = gains.shape[1] // owners
     if by_kernels():
-        rows = jnp.stack([jnp.zeros_like(gain), *pieces] + [jnp.zeros_like(gain)] * (7 - len(pieces)))
-        share_qkv, share_out, gains, grad_tokens, share_in = last_sum(
-            normed, grad_qkv, attended, branch, share_in, weight_qkv, tokens, grad_middle, gain[None], rows, share, held
+        share_qkv, share_out, gain_sums, grad_tokens, share_in = last_sum(
+            normed, attended, share_in, weight_qkv, weight_out, tokens, grad_routed, upstream, middle, raw, queries, keys,
+            values, probs, *wide_tables(cosine, sine), gains, share, held
         )
         core = lax.rem(lax.axis_index("expert"), 2)
-        gains = lax.dynamic_slice_in_dim(gains, core * share, share, axis=1)
-        return (grad_tokens, gains, share_qkv, share_out, share_in.astype(single))
+        gain_sums = lax.dynamic_slice_in_dim(gain_sums, core * share, share, axis=1)
+        return (grad_tokens, gain_sums, share_qkv, share_out, share_in.astype(single))
     everyone = ("dp", "expert")
-    normal, factor = normalize(tokens.astype(single))
-    grad_input, piece = rms_back(contract_last(grad_qkv, weight_qkv), normal, factor, gain)
+    grad_tokens, pieces, *pairs = backward(
+        tokens, gains, grad_routed, upstream, normed, raw, queries, keys, values, probs, attended, middle, weight_qkv,
+        weight_out, cosine, sine
+    )
     return (
-        grad_middle + grad_input,
-        lax.psum_scatter(jnp.stack([piece, *pieces]), everyone, scatter_dimension=1, tiled=True),
+        grad_tokens,
+        lax.psum_scatter(pieces, everyone, scatter_dimension=1, tiled=True),
         *(
             lax.psum_scatter(
                 contract_rows(left, right, narrow), everyone, scatter_dimension=0, tiled=True
             ).astype(single)
-            for left, right in ((normed, grad_qkv), (attended, branch))
+            for left, right in pairs
         ),
         share_in.astype(single),
     )
@@ -1763,15 +1913,7 @@
     weight_qkv, weight_out, up_rows, every_gate, gains, weight_in, weight_down, made = bring_all(
         w_qkv, w_out, upstream, dense, gain_rows, expert_in, expert_out, own, cosine, sine, allowed
     )
-    gain_attn, gain_query, gain_key, gain_ffn = gains[0], gains[1], gains[2], gains[3]
-    normed_in, raw, query_rows, key_rows, value_rows, probs, attended, middle, routed_in = made
-    normal_q, factor_q = normalize(raw[0])
-    normal_k, factor_k = normalize(raw[1])
-    normal_mid, factor_mid = normalize(middle)
-    query_rows, key_rows, value_rows = (
-        field.reshape(rows, -1, HEAD) for field in (query_rows, key_rows, value_rows)
-    )
-    attn_probs = probs.astype(narrow)
+    middle, routed_in = made[-2:]
 
     mixture, grad_routed, gate_table, (share_in, share_down) = experts_all(
         routed_in, up_rows, every_gate, weight_in, weight_down, held
@@ -1779,41 +1921,8 @@
     grad_gates = jnp.sum(onehot * gate_table.T[:, None, :], axis=2)
     results = (middle + mixture).astype(narrow)
 
-    grad_mid, piece_ffn = rms_back(grad_routed, normal_mid, factor_mid, gain_ffn)
-    grad_middle = upstream.astype(single) + grad_mid
-    grad_branch = grad_middle.astype(narrow)
-    grad_attended = contract_last(grad_branch, weight_out).astype(narrow).reshape(rows, -1, HEAD)
-    grad_probs = jnp.einsum("qhd,khd->hqk", grad_attended, value_rows, preferred_element_type=single)
-    inner = jnp.sum(grad_probs * probs, axis=-1, keepdims=True)
-    grad_scores = (probs * (grad_probs - inner)).astype(narrow)
-    grad_query = jnp.einsum(
-        "hqk,khd->qhd", grad_scores, key_rows, preferred_element_type=single
-    ) * HEAD ** (-0.5)
-    grad_key = jnp.einsum(
-        "hqk,qhd->khd", grad_scores, query_rows, preferred_element_type=single
-    ) * HEAD ** (-0.5)
-    grad_value = jnp.einsum("hqk,qhd->khd", attn_probs, grad_attended, preferred_element_type=single)
-    grad_q_raw, piece_query = rms_back(
-        rotate(grad_query.reshape(rows, model_width), cosine, -sine), normal_q, factor_q, gain_query
-    )
-    grad_k_raw, piece_key = rms_back(
-        rotate(grad_key.reshape(rows, model_width), cosine, -sine), normal_k, factor_k, gain_key
-    )
-    grad_qkv = jnp.concatenate(
-        [grad_q_raw, grad_k_raw, grad_value.reshape(rows, model_width)], axis=1
-    ).astype(narrow)
     grad_tokens, gain_sums, grad_qkv_share, grad_out_share, share_in = deliver_all(
-        own,
-        gain_attn,
-        grad_middle,
-        (piece_query, piece_key, piece_ffn),
-        normed_in,
-        grad_qkv,
-        weight_qkv,
-        attended,
-        grad_branch,
-        share_in,
-        held,
+        own, gains, grad_routed, upstream, made, weight_qkv, weight_out, cosine, sine, share_in, held
     )
     shape = (micro_count, seq_len, model_width)
     return (

time: 707 us -> 690 us (0.976); the launches traced: 696 us -> 688 us
  Pallas kernels: 630 us -> 654 us
  other arithmetic: 27.9 us -> 15.5 us
  local copies, waits for them, and re-layouts: 29 us -> 17.6 us
  matrix products: 8.04 us -> 0 us
    pallas_call x1, Pallas kernels: 173 us -> 197 us  [last_sum(): pl.pallas_call(last_sum_kernel, out_shape=(jax.ShapeDtypeStruct((share, w...]
    dot_general x5 -> x0, matrix products: 8.04 us -> none  [the longest x1 6.38 us: contract_last(): lax.dot_general(left, right, (((1,), (1,)), ((), ())), preferred_element_...]
    reduce_sum x4 -> x0, other arithmetic: 7.26 us -> none  [the longest x2 4.12 us: rms_back(): jnp.sum(upstream * normal, axis=0)]
    unnamed x46 -> x42, local copies, waits for them, and re-layouts: 14.5 us -> 14.5 us
where the time goes in v8:
time: 690 us; the launch traced here: 688 us
  Pallas kernels  654 us (95%)
  local copies, waits for them, and re-layouts  17.6 us (3%)
  other arithmetic  15.5 us (2%)
    pallas_call x1, Pallas kernels, first_gather(): pl.pallas_call(first_gather_kernel, out_shape=(whole(wq, True), whole(wo,...  233 us
    pallas_call x1, Pallas kernels, experts_round(): pl.pallas_call(experts_kernel, out_shape=(jax.ShapeDtypeStruct((block, wi...  223 us
    pallas_call x1, Pallas kernels, last_sum(): pl.pallas_call(last_sum_kernel, out_shape=(jax.ShapeDtypeStruct((share, w...  197 us
    unnamed x42, local copies, waits for them, and re-layouts  14.5 us

profile of v8, /device:TPU:0, one launch (start us, length us, event | category | flops | bytes accessed | tf_op | source)
XLA Modules:
  0.0 687.5 jit_solution(1611032841398791091)
XLA Ops:
  0.7 0.8 select_reduce_fusion.3
  1.5 0.7 fusion.17
  2.5 0.7 fusion.13
  3.3 0.7 copy.34
  4.0 0.7 copy.35
  5.0 0.3 fusion.2
  5.5 1.0 copy-done
  6.5 1.0 copy-done.1
  7.5 1.1 copy-done.2
  8.7 0.9 copy-done.11
  9.6 232.8 %bring.1 = (bf16[4,4,2,64,6144]{4,3,2,1,0:T(8,128)(2,1)}, bf16[4,4,2,64,2048]{4,3,2,1,0:T(8,128)(2,1)}, bf16[4,4,128,2048]{3,2,1,0:T(8,128)(2,1)}, f32[4,4,2,24,...) custom-call(bf16[64,6144]{1,0:T(8,128)(2,1)S(1)} %copy-done.2, ...), custom_call_target="tpu_custom_call" | custom-call | tf_op jit(solution)/shard_map/bring/pallas_call | solution.py:690
  242.5 0.8 copy-done.5
  243.3 0.8 copy-done.6
  244.1 0.8 copy-done.7
  244.9 0.8 copy-done.8
  245.7 0.8 copy-done.9
  246.5 0.8 copy-done.10
  247.3 0.6 copy-done.12
  247.9 0.4 copy.37
  248.3 1.0 pad.13.gates
  249.3 223.3 %experts.1 = (f32[128,2048]{1,0:T(8,128)}, f32[16,128]{1,0:T(8,128)}, f32[128,2048]{1,0:T(8,128)}, bf16[2048,1024]{1,0:T(8,128)(2,1)}, bf16[512,2048]{1,0:T(8,12...) custom-call(bf16[128,2048]{1,0:T(8,128)(2,1)} %copy-done.10, ...), custom_call_target="tpu_custom_call" | custom-call | tf_op jit(solution)/shard_map/experts/pallas_call | solution.py:1658
  472.7 0.7 select_reduce_fusion
  473.4 197.4 %deliver.1 = (f32[64,6144]{1,0:T(8,128)}, f32[64,2048]{1,0:T(8,128)}, f32[8,128]{1,0:T(8,128)}, f32[128,2048]{1,0:T(8,128)}, bf16[2,512,2048]{2,1,0:T(8,128)(2,1)}) custom-call(bf16[128,2048]{1,0:T(8,128)(2,1)} %copy-done.5, bf16[128,2048]{1,0:T(8,128)(2,1)} %copy-done.9, bf16[2048,1024]{1,0:T(8,128)(2,1)} %get-tuple-element.47.gin_sum, ...), custom_call_target="tpu_custom_call" | custom-call | tf_op jit(solution)/shard_map/deliver/pallas_call | solution.py:1280
  670.9 2.1 add_convert_fusion
  673.0 0.8 constant_dynamic-slice_fusion
  673.7 0.5 slice_bitcast_fusion
  674.4 0.6 copy.38
  675.0 5.2 convert_add_fusion
  680.2 4.4 convert_element_type.39
  684.6 1.0 copy.42
  685.6 1.1 copy.43
  686.7 0.8 copy.44
  (43 shorter events, 0.9 us)
Async XLA Ops:
  5.4 237.1 %copy-start.3 = (f32[128,128]{1,0:T(8,128)}, f32[128,128]{1,0:T(8,128)S(1)}, u32[]{:S(2)}) copy-start(f32[128,128]{1,0:T(8,128)S(1)} %pad_maximum_fusion.1.sine) | copy-start | bytes 196612
  5.5 1.0 copy-start
  6.5 1.0 copy-start.1
  7.5 1.1 copy-start.2
  8.7 0.9 copy-start.11
  9.6 232.8 %copy-start.4 = (f32[128,128]{1,0:T(8,128)}, f32[128,128]{1,0:T(8,128)S(1)}, u32[]{:S(2)}) copy-start(f32[128,128]{1,0:T(8,128)S(1)} %pad_maximum_fusion.cosine) | copy-start | bytes 196612
  242.5 0.8 copy-start.5
  243.3 0.8 copy-start.6
  244.1 0.8 copy-start.7
  244.9 0.8 copy-start.8
  245.7 0.8 copy-start.9
  246.5 0.8 copy-start.10
  247.3 0.6 copy-start.12
  473.4 197.4 %copy-start.14 = (f32[128,2048]{1,0:T(8,128)S(1)}, f32[128,2048]{1,0:T(8,128)}, u32[]{:S(2)}) copy-start(f32[128,2048]{1,0:T(8,128)} %get-tuple-element.38.middle) | copy-start | bytes 3145732
  675.0 5.2 copy-start.13
  680.2 4.5 copy-start.16
  680.2 5.4 copy-start.15
  684.6 2.1 copy-start.17

commit v9 on v8

--- a/solution.py
+++ b/solution.py
@@ -612,11 +612,19 @@
 
 def first_gather_kernel(
     wq, wo, up, small, ein, eout, tokens, cosine, sine, allowed,
-    wq_all, wo_all, up_all, small_all, win, wout, gains, normed, raw, queries, keys, values, probs, attended, middle, routed,
-    small_here, small_sem, panel, panel_sems, *sems
+    wq_all, wo_all, up_all, small_all, win, wout, *rest
 ):
+    made, (tokens_v, small_here, small_sem, panel, panel_sems, put_sems), sems = rest[:10], rest[20:26], rest[26:]
+    results = rest[10:20]
+    gains, normed, raw, queries, keys, values, probs, attended, middle, routed = results
     here = Here()
     here.meet()
+    fetch_tokens = pltpu.make_async_copy(tokens, tokens_v, small_sem.at[1])
+    fetch_tokens.start()
+    puts = [
+        pltpu.make_async_copy(source, target, put_sems.at[number])
+        for number, (source, target) in enumerate(zip(results, made))
+    ]
     items = [
         Gather(here, source, whole, halves, shared, sems[4 * number : 4 * number + 4])
         for number, (source, whole, halves, shared) in enumerate(
@@ -647,6 +655,7 @@
     fetch = pltpu.make_async_copy(small_all, small_here, small_sem.at[0])
     fetch.start()
     fetch.wait()
+    fetch_tokens.wait()
     share = wq.shape[0]
     lanes = small.shape[1]
     lane = lax.broadcasted_iota(jnp.int32, (8, lanes), 1)
@@ -665,16 +674,20 @@
             for step in range(1, DEPTH):
                 rows.second(step)
         else:
+            for copy in puts:
+                copy.start()
             recut.relay()
 
     attention_forward(
-        tokens, cosine, sine, allowed, wq_all, wo_all, gains, normed, raw, queries, keys, values, probs, attended,
+        tokens_v, cosine, sine, allowed, wq_all, wo_all, gains, normed, raw, queries, keys, values, probs, attended,
         middle, routed, panel, panel_sems, between
     )
     for step in range(DEPTH):
         rows.third(step)
     rows.finish()
     recut.end()
+    for copy in puts:
+        copy.wait()
 
 
 def first_gather(wq, wo, up, small, ein, eout, tokens, cosine, sine, allowed):
@@ -686,7 +699,19 @@
     block, width = tokens.shape
     heads = width // HEAD
     vmem = pl.BlockSpec(memory_space=pltpu.VMEM)
-    like = jax.ShapeDtypeStruct((block, width), narrow)
+    like = ((block, width), narrow)
+    made = (
+        ((8, width), single),
+        like,
+        ((2, block, width), single),
+        like,
+        like,
+        like,
+        ((heads, block, block), single),
+        like,
+        ((block, width), single),
+        like,
+    )
     return pl.pallas_call(
         first_gather_kernel,
         out_shape=(
@@ -696,29 +721,23 @@
             whole(small, True),
             jax.ShapeDtypeStruct((DEPTH * rows, columns), ein.dtype),
             jax.ShapeDtypeStruct((2 * held,) + eout.shape[1:], eout.dtype),
-            jax.ShapeDtypeStruct((8, width), single),
-            like,
-            jax.ShapeDtypeStruct((2, block, width), single),
-            like,
-            like,
-            like,
-            jax.ShapeDtypeStruct((heads, block, block), single),
-            like,
-            jax.ShapeDtypeStruct((block, width), single),
-            like,
+            *(jax.ShapeDtypeStruct(*one) for one in made),
         ),
-        in_specs=[HBM] * 6 + [vmem] * 4,
-        out_specs=(HBM,) * 6 + (vmem,) * 10,
-        scratch_shapes=[
+        in_specs=[HBM] * 7 + [vmem] * 3,
+        out_specs=(HBM,) * 16,
+        scratch_shapes=[pltpu.VMEM(*one) for one in made]
+        + [
+            pltpu.VMEM((block, width), tokens.dtype),
             pltpu.VMEM((DEPTH, RING, 2) + small.shape, single),
-            pltpu.SemaphoreType.DMA((1,)),
+            pltpu.SemaphoreType.DMA((2,)),
             pltpu.VMEM((2, DEPTH, RING, 2, wq.shape[0], PANEL), narrow),
             pltpu.SemaphoreType.DMA((2,)),
+            pltpu.SemaphoreType.DMA((len(made),)),
         ]
         + GATHER_SEMS * 4
         + RECUT_SEMS,
         compiler_params=pltpu.CompilerParams(
-            collective_id=1, has_side_effects=True, vmem_limit_bytes=48 * 2**20
+            collective_id=1, has_side_effects=True, vmem_limit_bytes=62 * 2**20
         ),
         name="bring",
     )(wq, wo, up, small, ein, eout, tokens, cosine, sine, allowed)
@@ -770,6 +789,7 @@
     def __init__(self, here, sources, target, halves, paired, scratch):
         self.here, self.sources, self.halves, self.paired = here, sources, halves, paired
         self.target = target if isinstance(target, list) else [(target, 0, target.shape[0])]
+        self.extra = []
         self.mine, self.half, self.full, self.column = scratch[:4]
         self.half_sem, self.full_sem, self.line_sem, self.load_sem = scratch[4:8]
         if paired:
@@ -929,7 +949,7 @@
 
         def total(more):
             for target, row, rows in self.target:
-                part = [term.at[pl.ds(row, rows)] for term in terms + more]
+                part = [term.at[pl.ds(row, rows)] for term in terms + more + self.extra]
                 add_up(target, part, rows, self.columns)
 
         @pl.when(here.z == 0)
@@ -1147,9 +1167,6 @@
     def keep_heads(spot, made):
         grad_heads[:, spot] = made.astype(narrow)
 
-    through(weight_out, width, right[0, :, side_out], keep_heads)
-    fetch(weight, 0, wide).start()
-
     step = 512
     each = width // step
     rows = RING * 2 * share
@@ -1177,6 +1194,8 @@
         make(z, outer, left_out, sides * each, (sides + 1) * each)
         for way in (0, 1):
             start(outer.toss(z, way))
+    through(weight_out, width, right[0, :, side_out], keep_heads)
+    fetch(weight, 0, wide).start()
     for number in range(4, len(loads)):
         loads[number].wait()
     swaps[2].start()
@@ -1376,7 +1395,7 @@
 
 
 def experts_kernel(
-    rows, ups, gates, win, wout, mid_sum, gate_sum, out_sum, gin_sum, gdown, gdown_other, gin, gin_other, rows_all, *scratch
+    rows, ups, gates, win, wout, middle, mid_sum, gate_sum, out_sum, gin_sum, gdown, gdown_other, gin, gin_other, rows_all, *scratch
 ):
     here = Here()
     here.meet()
@@ -1386,6 +1405,9 @@
     gather = Gather(here, rows, rows_all, halves_of(rows.shape[0]), False, scratch[12:16])
     mids = Sum(here, None, mid_sum, halves_of(rows.shape[0]), False, scratch[16:24])
     outs = Sum(here, None, out_sum, halves_of(rows.shape[0]), False, scratch[16:19] + scratch[24:29])
+    fetch_middle = pltpu.make_async_copy(middle, scratch[45], scratch[46].at[0])
+    fetch_middle.start()
+    outs.extra = [scratch[45]]
     tables = Sum(here, None, gate_sum, halves_of(gate_sum.shape[0], False), False, scratch[29:37])
     in_sems, down_sems = scratch[37:40], scratch[40:43]
     block, width = rows.shape
@@ -1640,6 +1662,7 @@
             add_cores()
     outs.second(order[-1])
     outs.third(order[-2], False)
+    fetch_middle.wait()
     outs.third(order[-1], True)
     for number, z in enumerate(order):
         outs.end(z, number == DEPTH - 1)
@@ -1649,7 +1672,7 @@
     rounds.finish()
 
 
-def experts_round(rows, ups, gates, win, wout, experts):
+def experts_round(rows, ups, gates, win, wout, middle, experts):
     block, width = rows.shape
     plane = RING * block
     hidden = wout.shape[0]
@@ -1660,7 +1683,7 @@
         out_shape=(
             jax.ShapeDtypeStruct((block, width), single),
             jax.ShapeDtypeStruct((experts, block), single),
-            jax.ShapeDtypeStruct((block, width), single),
+            jax.ShapeDtypeStruct((block, width), narrow),
             jax.ShapeDtypeStruct((width, hidden), narrow),
             jax.ShapeDtypeStruct((hidden // 2, width), narrow),
             jax.ShapeDtypeStruct((hidden // 2, width), narrow),
@@ -1668,7 +1691,7 @@
             jax.ShapeDtypeStruct((width, hidden), narrow),
             jax.ShapeDtypeStruct((DEPTH, RING, block, width), narrow),
         ),
-        in_specs=[HBM] * 5,
+        in_specs=[HBM] * 6,
         out_specs=(vmem, vmem, vmem) + (HBM,) * 6,
         scratch_shapes=[
             pltpu.VMEM((width, 2 * hidden), narrow),
@@ -1699,12 +1722,13 @@
             pltpu.SemaphoreType.DMA((2, 1)),
             pltpu.SemaphoreType.DMA((hidden // TILE, 1)),
         ]
-        + [pltpu.SemaphoreType.DMA((2, 2)), pltpu.SemaphoreType.DMA((2,))],
+        + [pltpu.SemaphoreType.DMA((2, 2)), pltpu.SemaphoreType.DMA((2,))]
+        + [pltpu.VMEM((block, width), single), pltpu.SemaphoreType.DMA((1,))],
         compiler_params=pltpu.CompilerParams(
             collective_id=2, has_side_effects=True, vmem_limit_bytes=62 * 2**20
         ),
         name="experts",
-    )(rows, ups, gates, win, wout)
+    )(rows, ups, gates, win, wout, middle)
 
 
 def by_kernels():
@@ -1783,7 +1807,7 @@
     )
 
 
-def experts_all(routed_in, up_rows, every_gate, weight_in, weight_down, held):
+def experts_all(middle, routed_in, up_rows, every_gate, weight_in, weight_down, held):
     depth = lax.axis_size("dp")
     owners = lax.axis_size("expert")
     chips = owners // 2
@@ -1796,11 +1820,11 @@
     if by_kernels():
         gate = jnp.pad(gate.reshape(DEPTH, -1, chip_experts), ((0, 0), (0, 0), (0, 128 - chip_experts)))
         ups = up_rows.reshape(DEPTH, -1, width)
-        grad_routed, table, mixture, grad_in, grad_down, grad_down_other = experts_round(
-            routed_in, ups, gate, weight_in, weight_down, experts
+        grad_routed, table, results, grad_in, grad_down, grad_down_other = experts_round(
+            routed_in, ups, gate, weight_in, weight_down, middle, experts
         )[:6]
         down = grad_down.astype(single) + grad_down_other.astype(single)
-        return (mixture, grad_routed, table, (grad_in, down.reshape(held, -1, width)))
+        return (results, grad_routed, table, (grad_in, down.reshape(held, -1, width)))
     mid_rows = gather_alike(routed_in).reshape(-1, width)
     out, mid, served, grad_in, grad_down = expert_rounds(
         mid_rows, up_rows, gate.reshape(-1, chip_experts), weight_in, weight_down
@@ -1808,8 +1832,9 @@
     by_gate = served.reshape(depth, chips, rows, chip_experts).transpose(0, 1, 3, 2)
     spread = jnp.zeros((depth, chips, experts, rows), single)
     spread = lax.dynamic_update_slice_in_dim(spread, by_gate, chip * chip_experts, axis=2)
+    mixture = scatter_alike(out.reshape(depth, chips, rows, width)).astype(single)
     return (
-        scatter_alike(out.reshape(depth, chips, rows, width)).astype(single),
+        (middle + mixture).astype(narrow),
         scatter_alike(mid.reshape(depth, chips, rows, width)).astype(single),
         scatter_alike(spread),
         return_weights(grad_in, grad_down, held),
@@ -1915,11 +1940,10 @@
     )
     middle, routed_in = made[-2:]
 
-    mixture, grad_routed, gate_table, (share_in, share_down) = experts_all(
-        routed_in, up_rows, every_gate, weight_in, weight_down, held
+    results, grad_routed, gate_table, (share_in, share_down) = experts_all(
+        middle, routed_in, up_rows, every_gate, weight_in, weight_down, held
     )
     grad_gates = jnp.sum(onehot * gate_table.T[:, None, :], axis=2)
-    results = (middle + mixture).astype(narrow)
 
     grad_tokens, gain_sums, grad_qkv_share, grad_out_share, share_in = deliver_all(
         own, gains, grad_routed, upstream, made, weight_qkv, weight_out, cosine, sine, share_in, held

time: 690 us -> 681 us (0.987)
  local copies, waits for them, and re-layouts: 17.6 us -> 9.79 us
    unnamed x42 -> x17, local copies, waits for them, and re-layouts: 14.5 us -> 5.72 us
where the time goes in v9:
time: 681 us; the launch traced here: 679 us
  Pallas kernels  653 us (96%)
  other arithmetic  15.9 us (2%)
  local copies, waits for them, and re-layouts  9.79 us (1%)
    pallas_call x1, Pallas kernels, first_gather(): pl.pallas_call(first_gather_kernel, out_shape=(whole(wq, True), whole(wo,...  232 us
    pallas_call x1, Pallas kernels, experts_round(): pl.pallas_call(experts_kernel, out_shape=(jax.ShapeDtypeStruct((block, wi...  223 us
    pallas_call x1, Pallas kernels, last_sum(): pl.pallas_call(last_sum_kernel, out_shape=(jax.ShapeDtypeStruct((share, w...  198 us

profile of v9, /device:TPU:0, one launch (start us, length us, event | category | flops | bytes accessed | tf_op | source)
XLA Modules:
  0.0 679.1 jit_solution(489846235181683217)
XLA Ops:
  0.7 0.8 select_reduce_fusion.3
  1.5 0.7 fusion.17
  2.2 0.1 convert_reduce_fusion
  2.4 0.1 convert_element_type.32
  2.5 0.1 add.39
  2.5 0.7 fusion.13
  3.3 0.7 copy.34
  4.0 0.1 eq.28
  4.0 0.7 copy.35
  4.8 0.1 mul.57
  4.9 0.6 pad_maximum_fusion.2.small
  5.5 0.7 fusion.1.allowed
  6.2 0.3 fusion.2
  6.5 0.7 pad_maximum_fusion.1.sine
  7.2 0.7 pad_maximum_fusion.cosine
  7.9 232.3 %bring.1 = (bf16[4,4,2,64,6144]{4,3,2,1,0:T(8,128)(2,1)}, bf16[4,4,2,64,2048]{4,3,2,1,0:T(8,128)(2,1)}, bf16[4,4,128,2048]{3,2,1,0:T(8,128)(2,1)}, f32[4,4,2,24,...) custom-call(bf16[64,6144]{1,0:T(8,128)(2,1)} %wq.1, ...), custom_call_target="tpu_custom_call" | custom-call | tf_op jit(solution)/shard_map/bring/pallas_call | solution.py:715
  240.3 1.0 dynamic-slice_bitcast_fusion
  241.3 0.4 copy.37
  241.6 1.0 pad.13.gates
  242.7 222.9 %experts.1 = (f32[128,2048]{1,0:T(8,128)}, f32[16,128]{1,0:T(8,128)}, bf16[128,2048]{1,0:T(8,128)(2,1)}, bf16[2048,1024]{1,0:T(8,128)(2,1)}, bf16[512,2048]{1,0:...) custom-call(bf16[128,2048]{1,0:T(8,128)(2,1)} %get-tuple-element.38., ...), custom_call_target="tpu_custom_call" | custom-call | tf_op jit(solution)/shard_map/experts/pallas_call | solution.py:1681
  465.6 0.7 select_reduce_fusion
  466.3 197.5 %deliver.1 = (f32[64,6144]{1,0:T(8,128)}, f32[64,2048]{1,0:T(8,128)}, f32[8,128]{1,0:T(8,128)}, f32[128,2048]{1,0:T(8,128)}, bf16[2,512,2048]{2,1,0:T(8,128)(2,1)}) custom-call(bf16[128,2048]{1,0:T(8,128)(2,1)} %get-tuple-element.45.normed, bf16[128,2048]{1,0:T(8,128)(2,1)} %get-tuple-element.46.attended, bf16[2048,1024]{1,0:T(8,128)(2,1)} %get-tuple-element.47.gin_sum, ...), custom_call_target="tpu_custom_call" | custom-call | tf_op jit(solution)/shard_map/deliver/pallas_call | solution.py:1299
  663.8 0.8 constant_dynamic-slice_fusion
  664.5 0.5 slice_bitcast_fusion
  665.1 0.1 reshape.125
  665.2 0.6 copy.38
  665.8 5.2 convert_add_fusion
  671.0 4.4 convert_element_type.35
  675.4 0.8 copy.43
  676.2 1.0 copy.44
  677.2 1.1 copy.45
  678.3 0.8 copy.46
  (17 shorter events, 0.2 us)
Async XLA Ops:
  665.8 5.2 copy-start
  671.0 4.5 copy-start.3
  671.0 5.3 copy-start.2
  675.4 1.8 copy-start.1
  675.4 2.9 copy-start.4

commit v10 on v9

--- a/solution.py
+++ b/solution.py
@@ -399,6 +399,16 @@
                     self.places(step, sent)
 
 
+def inner_first(here, count, begin):
+    for group in (range(1, DEPTH - 1), (0, DEPTH - 1)):
+        for number in range(count):
+            for target in group:
+
+                @pl.when(here.z != target)
+                def _(target=target, number=number):
+                    begin(lax.rem(target - here.z + DEPTH, DEPTH), number)
+
+
 class Recut:
     def __init__(self, here, source_in, source_out, whole_in, whole_out, sems):
         self.here, self.source_in, self.source_out = here, source_in, source_out
@@ -408,12 +418,14 @@
         self.hidden = columns // 2
         self.part = self.hidden // DEPTH
 
-    def pieces(self, steps, arriving):
+    def pieces(self, steps, arriving, only=None):
         here, copies = self.here, []
         mine = lax.rem(here.z + DEPTH - steps, DEPTH) if arriving else here.z
         away = lax.rem(here.z + steps, DEPTH)
         for side in range(2):
             for expert in range(self.held):
+                if only not in (None, side * self.held + expert):
+                    continue
                 columns = side * self.held * 2 * self.part + (here.core * self.held + expert) * self.part
                 target = self.whole_in.at[
                     pl.ds(pl.multiple_of(mine * self.rows, 16), self.rows),
@@ -423,7 +435,7 @@
                     expert, :, pl.ds(pl.multiple_of(side * self.hidden + away * self.part, 128), self.part)
                 ]
                 spot = (steps, side * self.held + expert)
-                if steps == 0:
+                if isinstance(steps, int) and steps == 0:
                     copies.append(pltpu.make_async_copy(source, target, self.own.at[spot[1]]))
                 else:
                     copies.append(
@@ -470,9 +482,7 @@
             copy.start()
         self.lower_own().start()
         self.lower(True).start()
-        for copies in zip(*[self.pieces(steps, False) for steps in (2, 3, 1)]):
-            for copy in copies:
-                copy.start()
+        inner_first(self.here, 2 * self.held, lambda steps, number: self.pieces(steps, False, number)[0].start())
 
     def relay(self):
         for steps in range(DEPTH):
@@ -995,19 +1005,21 @@
         self.held, self.rows, columns = target.shape
         self.part = columns // (2 * DEPTH)
 
-    def pieces(self, steps, arriving):
+    def pieces(self, steps, arriving, only=None):
         here = self.here
         origin = lax.rem(here.z + DEPTH - steps, DEPTH) if arriving else here.z
         away = lax.rem(here.z + steps, DEPTH)
         copies = []
         for expert in range(self.held):
+            if only not in (None, expert):
+                continue
             column = (self.side * DEPTH + origin) * self.part
             target = self.target.at[expert, :, pl.ds(pl.multiple_of(column, 128), self.part)]
             source = self.source.at[
                 pl.ds(pl.multiple_of(away * self.rows, 16), self.rows),
                 pl.ds((self.side * self.held + expert) * self.part, self.part),
             ]
-            if steps == 0:
+            if isinstance(steps, int) and steps == 0:
                 copies.append(pltpu.make_async_copy(source, target, self.sems.at[0, 0, expert]))
             else:
                 sems = (self.sems.at[0, steps, expert], self.sems.at[1, steps, expert])
@@ -1015,9 +1027,9 @@
         return copies
 
     def begin(self):
-        for copies in zip(*[self.pieces(steps, False) for steps in (2, 3, 1, 0)]):
-            for copy in copies:
-                copy.start()
+        for copy in self.pieces(0, False):
+            copy.start()
+        inner_first(self.here, self.held, lambda steps, number: self.pieces(steps, False, number)[0].start())
 
     def end(self):
         for steps in range(DEPTH):

time: 681 us -> 668 us (0.981)
  Pallas kernels: 653 us -> 639 us
    pallas_call x1, Pallas kernels: 232 us -> 215 us  [first_gather(): pl.pallas_call(first_gather_kernel, out_shape=(whole(wq, True), whole(wo,...]
where the time goes in v10:
time: 668 us; the launch traced here: 666 us
  Pallas kernels  639 us (96%)
  other arithmetic  15.9 us (2%)
  local copies, waits for them, and re-layouts  9.79 us (1%)
    pallas_call x1, Pallas kernels, experts_round(): pl.pallas_call(experts_kernel, out_shape=(jax.ShapeDtypeStruct((block, wi...  221 us
    pallas_call x1, Pallas kernels, first_gather(): pl.pallas_call(first_gather_kernel, out_shape=(whole(wq, True), whole(wo,...  215 us
    pallas_call x1, Pallas kernels, last_sum(): pl.pallas_call(last_sum_kernel, out_shape=(jax.ShapeDtypeStruct((share, w...  203 us

profile of v10, /device:TPU:0, one launch (start us, length us, event | category | flops | bytes accessed | tf_op | source)
XLA Modules:
  0.0 665.6 jit_solution(2975901028049727432)
XLA Ops:
  0.7 0.8 select_reduce_fusion.3
  1.5 0.7 fusion.17
  2.2 0.1 convert_reduce_fusion
  2.4 0.1 convert_element_type.32
  2.5 0.1 add.39
  2.5 0.7 fusion.13
  3.3 0.7 copy.34
  4.0 0.1 eq.28
  4.0 0.7 copy.35
  4.8 0.1 mul.57
  4.9 0.6 pad_maximum_fusion.2.small
  5.5 0.7 fusion.1.allowed
  6.2 0.3 fusion.2
  6.5 0.7 pad_maximum_fusion.1.sine
  7.2 0.7 pad_maximum_fusion.cosine
  7.9 215.2 %bring.1 = (bf16[4,4,2,64,6144]{4,3,2,1,0:T(8,128)(2,1)}, bf16[4,4,2,64,2048]{4,3,2,1,0:T(8,128)(2,1)}, bf16[4,4,128,2048]{3,2,1,0:T(8,128)(2,1)}, f32[4,4,2,24,...) custom-call(bf16[64,6144]{1,0:T(8,128)(2,1)} %wq.1, ...), custom_call_target="tpu_custom_call" | custom-call | tf_op jit(solution)/shard_map/bring/pallas_call | solution.py:725
  223.1 1.0 dynamic-slice_bitcast_fusion
  224.1 0.4 copy.37
  224.5 1.0 pad.13.gates
  225.6 220.6 %experts.1 = (f32[128,2048]{1,0:T(8,128)}, f32[16,128]{1,0:T(8,128)}, bf16[128,2048]{1,0:T(8,128)(2,1)}, bf16[2048,1024]{1,0:T(8,128)(2,1)}, bf16[512,2048]{1,0:...) custom-call(bf16[128,2048]{1,0:T(8,128)(2,1)} %get-tuple-element.38., ...), custom_call_target="tpu_custom_call" | custom-call | tf_op jit(solution)/shard_map/experts/pallas_call | solution.py:1693
  446.1 0.7 select_reduce_fusion
  446.9 203.4 %deliver.1 = (f32[64,6144]{1,0:T(8,128)}, f32[64,2048]{1,0:T(8,128)}, f32[8,128]{1,0:T(8,128)}, f32[128,2048]{1,0:T(8,128)}, bf16[2,512,2048]{2,1,0:T(8,128)(2,1)}) custom-call(bf16[128,2048]{1,0:T(8,128)(2,1)} %get-tuple-element.45.normed, bf16[128,2048]{1,0:T(8,128)(2,1)} %get-tuple-element.46.attended, bf16[2048,1024]{1,0:T(8,128)(2,1)} %get-tuple-element.47.gin_sum, ...), custom_call_target="tpu_custom_call" | custom-call | tf_op jit(solution)/shard_map/deliver/pallas_call | solution.py:1311
  650.2 0.8 constant_dynamic-slice_fusion
  651.0 0.5 slice_bitcast_fusion
  651.5 0.1 reshape.125
  651.6 0.6 copy.38
  652.2 5.2 convert_add_fusion
  657.4 4.4 convert_element_type.35
  661.9 0.8 copy.43
  662.7 1.0 copy.44
  663.6 1.1 copy.45
  664.8 0.8 copy.46
  (17 shorter events, 0.2 us)
Async XLA Ops:
  652.2 5.2 copy-start
  657.4 4.5 copy-start.3
  657.4 5.3 copy-start.2
  661.9 1.8 copy-start.1
  661.9 2.9 copy-start.4

commit v11 on v10

--- a/solution.py
+++ b/solution.py
@@ -1208,6 +1208,8 @@
             start(outer.toss(z, way))
     through(weight_out, width, right[0, :, side_out], keep_heads)
     fetch(weight, 0, wide).start()
+    for z in order:
+        outer.second(z)
     for number in range(4, len(loads)):
         loads[number].wait()
     swaps[2].start()
@@ -1241,12 +1243,8 @@
             grad = norm_grad(turned[side, at], raw_v[side, at], side + 1)
             right[0, at, side * width : (side + 1) * width] = grad.astype(narrow)
 
-    for z in order[:2]:
-        outer.second(z)
     slabs(second)
     swaps[3].start()
-    for z in order[2:]:
-        outer.second(z)
     swaps[2].wait_recv()
     swaps[3].wait_recv()
 

time: 668 us -> 668 us (level)
  no operation moved by 1% of the time
where the time goes in v11:
time: 668 us; the launch traced here: 666 us
  Pallas kernels  639 us (96%)
  other arithmetic  15.9 us (2%)
  local copies, waits for them, and re-layouts  9.79 us (1%)
    pallas_call x1, Pallas kernels, experts_round(): pl.pallas_call(experts_kernel, out_shape=(jax.ShapeDtypeStruct((block, wi...  221 us
    pallas_call x1, Pallas kernels, first_gather(): pl.pallas_call(first_gather_kernel, out_shape=(whole(wq, True), whole(wo,...  215 us
    pallas_call x1, Pallas kernels, last_sum(): pl.pallas_call(last_sum_kernel, out_shape=(jax.ShapeDtypeStruct((share, w...  203 us

profile of v11, /device:TPU:0, one launch (start us, length us, event | category | flops | bytes accessed | tf_op | source)
XLA Modules:
  0.0 665.6 jit_solution(514760711888785034)
XLA Ops:
  0.7 0.8 select_reduce_fusion.3
  1.5 0.7 fusion.17
  2.2 0.1 convert_reduce_fusion
  2.4 0.1 convert_element_type.32
  2.5 0.1 add.39
  2.5 0.7 fusion.13
  3.3 0.7 copy.34
  4.0 0.1 eq.28
  4.0 0.7 copy.35
  4.8 0.1 mul.57
  4.9 0.6 pad_maximum_fusion.2.small
  5.5 0.7 fusion.1.allowed
  6.2 0.3 fusion.2
  6.5 0.7 pad_maximum_fusion.1.sine
  7.2 0.7 pad_maximum_fusion.cosine
  7.9 215.2 %bring.1 = (bf16[4,4,2,64,6144]{4,3,2,1,0:T(8,128)(2,1)}, bf16[4,4,2,64,2048]{4,3,2,1,0:T(8,128)(2,1)}, bf16[4,4,128,2048]{3,2,1,0:T(8,128)(2,1)}, f32[4,4,2,24,...) custom-call(bf16[64,6144]{1,0:T(8,128)(2,1)} %wq.1, ...), custom_call_target="tpu_custom_call" | custom-call | tf_op jit(solution)/shard_map/bring/pallas_call | solution.py:725
  223.1 1.0 dynamic-slice_bitcast_fusion
  224.1 0.4 copy.37
  224.5 1.0 pad.13.gates
  225.6 220.6 %experts.1 = (f32[128,2048]{1,0:T(8,128)}, f32[16,128]{1,0:T(8,128)}, bf16[128,2048]{1,0:T(8,128)(2,1)}, bf16[2048,1024]{1,0:T(8,128)(2,1)}, bf16[512,2048]{1,0:...) custom-call(bf16[128,2048]{1,0:T(8,128)(2,1)} %get-tuple-element.38., ...), custom_call_target="tpu_custom_call" | custom-call | tf_op jit(solution)/shard_map/experts/pallas_call | solution.py:1691
  446.1 0.7 select_reduce_fusion
  446.9 203.4 %deliver.1 = (f32[64,6144]{1,0:T(8,128)}, f32[64,2048]{1,0:T(8,128)}, f32[8,128]{1,0:T(8,128)}, f32[128,2048]{1,0:T(8,128)}, bf16[2,512,2048]{2,1,0:T(8,128)(2,1)}) custom-call(bf16[128,2048]{1,0:T(8,128)(2,1)} %get-tuple-element.45.normed, bf16[128,2048]{1,0:T(8,128)(2,1)} %get-tuple-element.46.attended, bf16[2048,1024]{1,0:T(8,128)(2,1)} %get-tuple-element.47.gin_sum, ...), custom_call_target="tpu_custom_call" | custom-call | tf_op jit(solution)/shard_map/deliver/pallas_call | solution.py:1309
  650.2 0.8 constant_dynamic-slice_fusion
  651.0 0.5 slice_bitcast_fusion
  651.5 0.1 reshape.125
  651.6 0.6 copy.38
  652.2 5.2 convert_add_fusion
  657.4 4.4 convert_element_type.35
  661.9 0.8 copy.43
  662.7 1.0 copy.44
  663.6 1.1 copy.45
  664.8 0.8 copy.46
  (17 shorter events, 0.2 us)
Async XLA Ops:
  652.2 5.2 copy-start
  657.4 4.5 copy-start.3
  657.4 5.3 copy-start.2
  661.9 1.8 copy-start.1
  661.9 2.9 copy-start.4
